TPU v7x, 256 devices: a whole 4x4x8 slice. The times are simulated.
256 devices in a mesh: lat: 4 (over y_lo, core), lon: 64 (over y_hi, x, z).
Axes of the slice: x: 4, y: 4 (y_hi: 2, y_lo: 2; y = y_hi * 2 + y_lo), z: 8, core: 2. Of those that a mesh axis runs over, the one named last changes fastest.
Arguments:
- latent: bfloat16 [64, 1024, 384], P('lat', 'lon'), may hold values from -6 to 6
- cotangent: bfloat16 [64, 1024, 384], P('lat', 'lon'), may hold values from -6 to 6
- gain_attn: float32 [384], replicated, may hold values from 0.1 to 1.9
- w_qkv: bfloat16 [384, 1152], replicated, may hold values from -0.3125 to 0.3125
- rel_bias: float32 [6, 7, 7], replicated, may hold values from -4 to 4
- w_out: bfloat16 [384, 384], replicated, may hold values from -0.3125 to 0.3125
- gain_mlp: float32 [384], replicated, may hold values from 0.1 to 1.9
- w_fc1: bfloat16 [384, 1536], replicated, may hold values from -0.3125 to 0.3125
- w_fc2: bfloat16 [1536, 384], replicated, may hold values from -0.15625 to 0.15625
Outputs:
- output: bfloat16 [64, 1024, 384], P('lat', 'lon')
- d_latent: bfloat16 [64, 1024, 384], P('lat', 'lon')
- d_qkv: float32 [384, 1152], replicated
- d_out: float32 [384, 384], replicated
- d_fc1: float32 [384, 1536], replicated
- d_fc2: float32 [1536, 384], replicated
- d_rel: float32 [6, 7, 7], replicated
- d_gain_attn: float32 [384], replicated
- d_gain_mlp: float32 [384], replicated
All inputs are finite; a program needn't handle non-finite values.
Results may differ from a plain program's by a relative error of at most 0.022.
Values may be sent and summed in bfloat16 or wider, within the bound.
No kernel may reach another device: no remote copies, remote signals or barrier semaphores. Data moves between devices by JAX's collectives and lax.ppermute only.
A program may use at most 192 MiB of HBM per device.

v0:
```python
import jax
import jax.numpy as jnp
from jax import lax
from jax.sharding import PartitionSpec as P

HEADS = 6
HEAD = 64


def shifted(value, axis, steps):
    count = lax.axis_size(axis)
    pairs = [(source, (source + steps) % count) for source in range(count)]
    return lax.ppermute(value, axis, pairs)


def layer_norm(values, gain):
    centre = jnp.mean(values, -1, keepdims=True)
    centred = values - centre
    variance = jnp.mean(centred * centred, -1, keepdims=True)
    return centred * lax.rsqrt(variance + 1e-05) * gain


def activate(values):
    return jax.nn.gelu(values, approximate=True)


def outer_sum(first_op, second_op):
    return lax.dot_general(
        first_op, second_op, (((0,), (0,)), ((), ())), preferred_element_type=jnp.float32
    )


def times_transposed(first_op, weight):
    return lax.dot_general(
        first_op, weight, (((1,), (1,)), ((), ())), preferred_element_type=jnp.float32
    )


def per_device(latent, cotangent, gain_attn, w_qkv, rel_bias, w_out, gain_mlp, w_fc1, w_fc2):
    band_rows, sector_cols, width = latent.shape
    count = band_rows * sector_cols
    bands = lax.axis_size("lat")
    band_here = lax.axis_index("lat")
    scale = HEAD ** (-0.5)
    flat = latent.reshape(count, width).astype(jnp.float32)
    normed, back_attn = jax.vjp(layer_norm, flat, gain_attn)
    normed_b = normed.astype(jnp.bfloat16)
    projected = jnp.dot(normed_b, w_qkv, preferred_element_type=jnp.float32)
    queries = projected[:, :width].astype(jnp.bfloat16)
    key_vals = projected[:, width:].astype(jnp.bfloat16)
    query_heads = queries.reshape(count, HEADS, HEAD)
    column = lax.all_gather(key_vals, "lat", axis=0, tiled=True)
    pieces = []
    for offset in range(-3, 4):
        if offset == 0:
            pieces.append(column)
        else:
            pieces.append(shifted(column, "lon", -offset))
    stacked = jnp.stack(pieces).reshape(7, bands, count, 2 * width)
    tap_keys = stacked[..., :width].reshape(7, bands, count, HEADS, HEAD)
    tap_values = stacked[..., width:].reshape(7, bands, count, HEADS, HEAD)
    scores = (
        jnp.einsum("rhd,bgrhd->bghr", query_heads, tap_keys, preferred_element_type=jnp.float32)
        * scale
    )
    bias_rows = lax.dynamic_slice_in_dim(rel_bias, 3 - band_here, bands, 1)
    scores = scores + jnp.transpose(bias_rows, (2, 1, 0))[..., None]
    weights = jnp.exp(scores)
    prob = weights / jnp.sum(weights, (0, 1), keepdims=True)
    prob_b = prob.astype(jnp.bfloat16)
    mixed = jnp.einsum("bghr,bgrhd->rhd", prob_b, tap_values, preferred_element_type=jnp.float32)
    mixed_b = mixed.reshape(count, width).astype(jnp.bfloat16)
    resid = flat + jnp.dot(mixed_b, w_out, preferred_element_type=jnp.float32)
    normed_two, back_mlp = jax.vjp(layer_norm, resid, gain_mlp)
    normed_two_b = normed_two.astype(jnp.bfloat16)
    hidden = jnp.dot(normed_two_b, w_fc1, preferred_element_type=jnp.float32)
    active, back_act = jax.vjp(activate, hidden)
    active_b = active.astype(jnp.bfloat16)
    output = (resid + jnp.dot(active_b, w_fc2, preferred_element_type=jnp.float32)).astype(
        jnp.bfloat16
    )
    grad_out = cotangent.reshape(count, width)
    d_fc2 = outer_sum(active_b, grad_out)
    d_active = times_transposed(grad_out, w_fc2)
    d_hidden = back_act(d_active)[0].astype(jnp.bfloat16)
    d_fc1 = outer_sum(normed_two_b, d_hidden)
    d_normed_two = times_transposed(d_hidden, w_fc1)
    d_resid_norm, d_gain_mlp = back_mlp(d_normed_two)
    d_resid = grad_out.astype(jnp.float32) + d_resid_norm
    d_resid_b = d_resid.astype(jnp.bfloat16)
    d_out = outer_sum(mixed_b, d_resid_b)
    d_mixed_b = times_transposed(d_resid_b, w_out).astype(jnp.bfloat16)
    d_mixed_heads = d_mixed_b.reshape(count, HEADS, HEAD)
    d_prob = jnp.einsum(
        "rhd,bgrhd->bghr", d_mixed_heads, tap_values, preferred_element_type=jnp.float32
    )
    d_score = prob * (d_prob - jnp.sum(prob * d_prob, (0, 1), keepdims=True))
    rel_part = jnp.transpose(jnp.sum(d_score, 3), (2, 1, 0))
    d_rel = lax.dynamic_update_slice(
        jnp.zeros((HEADS, 7, 7), jnp.float32), rel_part, (jnp.int32(0), 3 - band_here, jnp.int32(0))
    )
    d_score_b = (d_score * scale).astype(jnp.bfloat16)
    d_query = jnp.einsum("bghr,bgrhd->rhd", d_score_b, tap_keys, preferred_element_type=jnp.float32)
    key_terms = jnp.einsum(
        "bghr,rhd->bgrhd", d_score_b, query_heads, preferred_element_type=jnp.float32
    ).astype(jnp.bfloat16)
    value_terms = jnp.einsum(
        "bghr,rhd->bgrhd", prob_b, d_mixed_heads, preferred_element_type=jnp.float32
    ).astype(jnp.bfloat16)
    grad_terms = jnp.concatenate(
        [key_terms.reshape(7, bands, count, width), value_terms.reshape(7, bands, count, width)], -1
    )
    collected = grad_terms[3].astype(jnp.float32)
    for offset in range(-3, 4):
        if offset != 0:
            arrived = shifted(grad_terms[offset + 3], "lon", offset)
            collected = collected + arrived.astype(jnp.float32)
    owned = lax.psum_scatter(
        collected.reshape(bands * count, 2 * width), "lat", scatter_dimension=0, tiled=True
    )
    d_proj = jnp.concatenate([d_query.reshape(count, width), owned], -1).astype(jnp.bfloat16)
    d_qkv = outer_sum(normed_b, d_proj)
    d_normed = times_transposed(d_proj, w_qkv)
    d_flat_norm, d_gain_attn = back_attn(d_normed)
    d_latent = (d_resid + d_flat_norm).astype(jnp.bfloat16)
    d_qkv, d_out, d_fc1, d_fc2, d_rel, d_gain_attn, d_gain_mlp = lax.psum(
        (d_qkv, d_out, d_fc1, d_fc2, d_rel, d_gain_attn, d_gain_mlp), ("lat", "lon")
    )
    return (
        output.reshape(band_rows, sector_cols, width),
        d_latent.reshape(band_rows, sector_cols, width),
        d_qkv,
        d_out,
        d_fc1,
        d_fc2,
        d_rel,
        d_gain_attn,
        d_gain_mlp,
    )


def solution(mesh):
    return jax.shard_map(
        per_device,
        mesh=mesh,
        in_specs=(P("lat", "lon", None), P("lat", "lon", None), P(), P(), P(), P(), P(), P(), P()),
        out_specs=(P("lat", "lon", None), P("lat", "lon", None), P(), P(), P(), P(), P(), P(), P()),
        check_vma=False,
    )
```

profile of v0, /device:TPU:1, one launch (start us, length us, event | category | flops | bytes accessed | tf_op | source)
XLA Modules:
  0.0 870.0 jit_solution(16075736126402200634)
XLA Ops:
  14.4 31.7 %all-gather.2.cloned.1.call-done = bf16[1024,768]{1,0:T(8,128)(2,1)} async-done(((bf16[256,768]{1,0:T(8,128)(2,1)}), bf16[1024,768]{1,0:T(8,128)(2,1)}) %all-gather.2.cloned.1.call-update) | async-done | bytes 1572880 | tf_op jit(solution)/shard_map/all_gather | solution.py:52
  46.1 3.3 collective-permute-start
  49.3 2.6 collective-permute-start.1
  52.3 6.8 collective-permute-start.3
  59.9 96.5 %collective-permute-done = bf16[1024,768]{1,0:T(8,128)(2,1)} collective-permute-done((bf16[1024,768]{1,0:T(8,128)(2,1)}, bf16[1024,768]{1,0:T(8,128)(2,1)}, u32[]{:S(2)}, u32[]{:S(2)}) %collective-permute-start) | collective-permute-done | bytes 1572896 | tf_op jit(solution)/shard_map/ppermute | solution.py:13
  156.4 5.1 collective-permute-start.5
  162.7 3.1 fusion.44
  167.5 2.6 copy.54
  170.0 46.2 %collective-permute-done.1 = bf16[1024,768]{1,0:T(8,128)(2,1)} collective-permute-done((bf16[1024,768]{1,0:T(8,128)(2,1)}, bf16[1024,768]{1,0:T(8,128)(2,1)}, u32[]{:S(2)}, u32[]{:S(2)}) %collective-permute-start.1) | collective-permute-done | bytes 1572896 | tf_op jit(solution)/shard_map/ppermute | solution.py:13
  218.8 40.4 %collective-permute-done.2 = bf16[1024,768]{1,0:T(8,128)(2,1)} collective-permute-done((bf16[1024,768]{1,0:T(8,128)(2,1)}, bf16[1024,768]{1,0:T(8,128)(2,1)}, u32[]{:S(2)}, u32[]{:S(2)}) %collective-permute-start.2) | collective-permute-done | bytes 1572896 | tf_op jit(solution)/shard_map/ppermute | solution.py:13
  261.7 2.6 copy.58
  264.3 2.6 copy.59
  266.9 2.7 constant_dynamic-update-slice_fusion.6
  272.2 2.8 constant_dynamic-update-slice_fusion.5
  283.4 9.5 %fusion.42 = (bf16[7,4,256,384]{2,3,1,0:T(8,128)(2,1)}, bf16[7,4,256,384]{2,3,1,0:T(8,128)(2,1)}) fusion(bf16[7,4,256,768]{2,3,1,0:T(8,128)(2,1)} %constant_dynamic-update-slice_fusion), kind=kLoop, calls=%fused_computation.108 | loop fusion | bytes 22020096 | tf_op jit(solution)/shard_map/slice | solution.py:60
  292.9 4.7 multiply_reduce_fusion.3
  304.7 4.5 multiply_reduce_fusion.1
  315.6 9.0 %collective-permute-start.6 = (bf16[4,256,768]{1,2,0:T(8,128)(2,1)S(1)}, bf16[4,256,768]{1,2,0:T(8,128)(2,1)S(1)}, u32[]{:S(2)}, u32[]{:S(2)}) collective-permute-start(bf16[4,256,768]{1,2,0:T(8,128)(2,1)S(1)} %get-tuple-element.24), channel_id=1, source_target_pairs={{0,61},{1,62},{2,63},{3,0},{4,1},{5,2},{6,3},{7,4},{8,5},{9,6},{10... | collective-permute-start | bytes 4718600 | tf_op jit(solution)/shard_map/ppermute | solution.py:13
  324.6 3.5 collective-permute-start.7
  328.1 74.8 %collective-permute-done.10 = bf16[4,256,768]{1,2,0:T(8,128)(2,1)S(1)} collective-permute-done((bf16[4,256,768]{1,2,0:T(8,128)(2,1)S(1)}, bf16[4,256,768]{1,2,0:T(8,128)(2,1)S(1)}, u32[]{:S(2)}, u32[]{:S(2)}) %collective-permute-start.10) | collective-permute-done | bytes 1572896 | tf_op jit(solution)/shard_map/ppermute | solution.py:13
  402.9 83.8 %collective-permute-done.11 = bf16[4,256,768]{1,2,0:T(8,128)(2,1)S(1)} collective-permute-done((bf16[4,256,768]{1,2,0:T(8,128)(2,1)S(1)}, bf16[4,256,768]{1,2,0:T(8,128)(2,1)S(1)}, u32[]{:S(2)}, u32[]{:S(2)}) %collective-permute-start.11) | collective-permute-done | bytes 1572896 | tf_op jit(solution)/shard_map/ppermute | solution.py:13
  486.7 3.0 collective-permute-done.7
  489.7 37.5 %collective-permute-done.8 = bf16[4,256,768]{1,2,0:T(8,128)(2,1)S(1)} collective-permute-done((bf16[4,256,768]{1,2,0:T(8,128)(2,1)S(1)}, bf16[4,256,768]{1,2,0:T(8,128)(2,1)S(1)}, u32[]{:S(2)}, u32[]{:S(2)}) %collective-permute-start.8) | collective-permute-done | bytes 1572896 | tf_op jit(solution)/shard_map/ppermute | solution.py:13
  527.2 3.0 fusion.4
  530.2 3.5 copy.66
  534.7 3.8 multiply_reduce_fusion
  539.8 3.3 fusion.38
  545.2 27.0 %reduce-scatter.2.cloned.1.call-done = f32[256,768]{1,0:T(8,128)} async-done(((f32[1024,768]{1,0:T(8,128)}), f32[256,768]{1,0:T(8,128)}) %reduce-scatter.2.cloned.1.call-update) | async-done | bytes 786448 | tf_op jit(solution)/shard_map/reduce_scatter | solution.py:118
  576.4 2.9 fusion.24
  580.2 77.3 %all-reduce = (f32[6,7,7]{2,1,0:T(8,128)}, f32[384]{0:T(512)}, f32[384]{0:T(512)}) all-reduce(f32[6,7,7]{2,1,0:T(8,128)S(1)} %dynamic_update_slice.3, f32[384]{0:T(512)S(1)} %get-tuple-element.11, f32[384]{0:T(512)S(1)} %copy-done.30), channel_id=1, replica_groups=mesh['lat'=4,'lon'=64] {'lat','lon'}, use_global_device_ids=true, to_apply=%region_16.0 | all-reduce | flops 1062 | bytes 8496 | tf_op jit(solution)/shard_map/psum | solution.py:126
  658.5 197.3 %all-reduce.4.cloned.1.call-done = (f32[384,1152]{1,0:T(8,128)}, f32[384,384]{1,0:T(8,128)}, f32[384,1536]{1,0:T(8,128)}, f32[1536,384]{1,0:T(8,128)}) async-done(((f32[384,1152]{1,0:T(8,128)}, f32[384,384]{1,0:T(8,128)}, f32[384,1536]{1,0:T(8,128)}, f32[1536,384]{1,0:T(8,128)}), (f32[384,1152]{1,0:T(8,128)}, f32[384,384]{1,0:T(8,128)}, f32[384,1536]{1,0:T(8,128)}, ...) | async-done | bytes 7077904 | tf_op jit(solution)/shard_map/psum | solution.py:126
  855.8 2.9 copy.115
  (145 shorter events, 55.6 us)
Async XLA Ops:
  7.2 292.9 %copy-start = (bf16[384,1536]{1,0:T(8,128)(2,1)S(1)}, bf16[384,1536]{1,0:T(8,128)(2,1)}, u32[]{:S(2)}) copy-start(bf16[384,1536]{1,0:T(8,128)(2,1)} %param.16) | copy-start | bytes 3538948
  7.2 38.9 %all-gather.2.cloned.1.call-start = ((), (), s32[]{:S(2)}) async-start(), calls=%async_computation.1 | async-start | bytes 1966080 | tf_op jit(solution)/shard_map/all_gather | solution.py:52
  13.5 149.0 %copy-start.29 = (f32[6,7,7]{2,1,0:T(8,128)S(1)}, f32[6,7,7]{2,1,0:T(8,128)}, u32[]{:S(2)}) copy-start(f32[6,7,7]{2,1,0:T(8,128)} %param.13) | copy-start | bytes 3532
  13.5 149.1 %copy-start.10 = (bf16[16,16,384]{2,1,0:T(8,128)(2,1)S(1)}, bf16[16,16,384]{2,1,0:T(8,128)(2,1)}, u32[]{:S(2)}) copy-start(bf16[16,16,384]{2,1,0:T(8,128)(2,1)} %param.10) | copy-start | bytes 589828
  14.4 557.9 %reduce-scatter.2.cloned.1.call-start = ((), (), s32[]{:S(2)}) async-start(), calls=%async_computation.2 | async-start | bytes 3932160 | tf_op jit(solution)/shard_map/reduce_scatter | solution.py:118
  46.1 110.3 %collective-permute-start = (bf16[1024,768]{1,0:T(8,128)(2,1)}, bf16[1024,768]{1,0:T(8,128)(2,1)}, u32[]{:S(2)}, u32[]{:S(2)}) collective-permute-start(bf16[1024,768]{1,0:T(8,128)(2,1)} %all-gather.2.cloned.1.call-done), channel_id=1, source_target_pairs={{0,3},{1,4},{2,5},{3,6},{4,7},{5,8},{6,9},{7,10},{8,11},{9,12},{10... | collective-permute-start | bytes 4718600 | tf_op jit(solution)/shard_map/ppermute | solution.py:13
  49.3 166.9 %collective-permute-start.1 = (bf16[1024,768]{1,0:T(8,128)(2,1)}, bf16[1024,768]{1,0:T(8,128)(2,1)}, u32[]{:S(2)}, u32[]{:S(2)}) collective-permute-start(bf16[1024,768]{1,0:T(8,128)(2,1)} %all-gather.2.cloned.1.call-done), channel_id=1, source_target_pairs={{0,2},{1,3},{2,4},{3,5},{4,6},{5,7},{6,8},{7,9},{8,10},{9,11},{10,... | collective-permute-start | bytes 4718600 | tf_op jit(solution)/shard_map/ppermute | solution.py:13
  51.9 207.2 %collective-permute-start.2 = (bf16[1024,768]{1,0:T(8,128)(2,1)}, bf16[1024,768]{1,0:T(8,128)(2,1)}, u32[]{:S(2)}, u32[]{:S(2)}) collective-permute-start(bf16[1024,768]{1,0:T(8,128)(2,1)} %all-gather.2.cloned.1.call-done), channel_id=1, source_target_pairs={{0,1},{1,2},{2,3},{3,4},{4,5},{5,6},{6,7},{7,8},{8,9},{9,10},{10,1... | collective-permute-start | bytes 4718600 | tf_op jit(solution)/shard_map/ppermute | solution.py:13
  52.3 209.4 %collective-permute-start.3 = (bf16[1024,768]{1,0:T(8,128)(2,1)}, bf16[1024,768]{1,0:T(8,128)(2,1)}, u32[]{:S(2)}, u32[]{:S(2)}) collective-permute-start(bf16[1024,768]{1,0:T(8,128)(2,1)} %all-gather.2.cloned.1.call-done), channel_id=1, source_target_pairs={{0,63},{1,0},{2,1},{3,2},{4,3},{5,4},{6,5},{7,6},{8,7},{9,8},{10,9... | collective-permute-start | bytes 4718600 | tf_op jit(solution)/shard_map/ppermute | solution.py:13
  59.1 205.2 %collective-permute-start.4 = (bf16[1024,768]{1,0:T(8,128)(2,1)}, bf16[1024,768]{1,0:T(8,128)(2,1)}, u32[]{:S(2)}, u32[]{:S(2)}) collective-permute-start(bf16[1024,768]{1,0:T(8,128)(2,1)} %all-gather.2.cloned.1.call-done), channel_id=1, source_target_pairs={{0,62},{1,63},{2,0},{3,1},{4,2},{5,3},{6,4},{7,5},{8,6},{9,7},{10,... | collective-permute-start | bytes 4718600 | tf_op jit(solution)/shard_map/ppermute | solution.py:13
  156.4 113.2 %collective-permute-start.5 = (bf16[1024,768]{1,0:T(8,128)(2,1)}, bf16[1024,768]{1,0:T(8,128)(2,1)}, u32[]{:S(2)}, u32[]{:S(2)}) collective-permute-start(bf16[1024,768]{1,0:T(8,128)(2,1)} %all-gather.2.cloned.1.call-done), channel_id=1, source_target_pairs={{0,61},{1,62},{2,63},{3,0},{4,1},{5,2},{6,3},{7,4},{8,5},{9,6},{10... | collective-permute-start | bytes 4718600 | tf_op jit(solution)/shard_map/ppermute | solution.py:13
  272.2 2.8 copy-start.5
  283.4 9.5 %copy-start.12 = (f32[6,256,64]{1,2,0:T(8,128)S(1)}, f32[6,256,64]{1,2,0:T(8,128)}, u32[]{:S(2)}) copy-start(f32[6,256,64]{1,2,0:T(8,128)} %convert.39) | copy-start | bytes 1179652
  292.9 4.9 copy-start.2
  297.9 2.2 copy-start.11
  297.9 2.2 copy-start.28
  315.5 87.4 %collective-permute-start.10 = (bf16[4,256,768]{1,2,0:T(8,128)(2,1)S(1)}, bf16[4,256,768]{1,2,0:T(8,128)(2,1)S(1)}, u32[]{:S(2)}, u32[]{:S(2)}) collective-permute-start(bf16[4,256,768]{1,2,0:T(8,128)(2,1)S(1)} %get-tuple-element.29), channel_id=1, source_target_pairs={{0,2},{1,3},{2,4},{3,5},{4,6},{5,7},{6,8},{7,9},{8,10},{9,11},{10,... | collective-permute-start | bytes 4718600 | tf_op jit(solution)/shard_map/ppermute | solution.py:13
  315.6 171.1 %collective-permute-start.11 = (bf16[4,256,768]{1,2,0:T(8,128)(2,1)S(1)}, bf16[4,256,768]{1,2,0:T(8,128)(2,1)S(1)}, u32[]{:S(2)}, u32[]{:S(2)}) collective-permute-start(bf16[4,256,768]{1,2,0:T(8,128)(2,1)S(1)} %get-tuple-element.28), channel_id=1, source_target_pairs={{0,3},{1,4},{2,5},{3,6},{4,7},{5,8},{6,9},{7,10},{8,11},{9,12},{10... | collective-permute-start | bytes 4718600 | tf_op jit(solution)/shard_map/ppermute | solution.py:13
  315.6 171.0 %collective-permute-start.6 = (bf16[4,256,768]{1,2,0:T(8,128)(2,1)S(1)}, bf16[4,256,768]{1,2,0:T(8,128)(2,1)S(1)}, u32[]{:S(2)}, u32[]{:S(2)}) collective-permute-start(bf16[4,256,768]{1,2,0:T(8,128)(2,1)S(1)} %get-tuple-element.24), channel_id=1, source_target_pairs={{0,61},{1,62},{2,63},{3,0},{4,1},{5,2},{6,3},{7,4},{8,5},{9,6},{10... | collective-permute-start | bytes 4718600 | tf_op jit(solution)/shard_map/ppermute | solution.py:13
  324.6 165.1 %collective-permute-start.7 = (bf16[4,256,768]{1,2,0:T(8,128)(2,1)S(1)}, bf16[4,256,768]{1,2,0:T(8,128)(2,1)S(1)}, u32[]{:S(2)}, u32[]{:S(2)}) collective-permute-start(bf16[4,256,768]{1,2,0:T(8,128)(2,1)S(1)} %get-tuple-element.25), channel_id=1, source_target_pairs={{0,62},{1,63},{2,0},{3,1},{4,2},{5,3},{6,4},{7,5},{8,6},{9,7},{10,... | collective-permute-start | bytes 4718600 | tf_op jit(solution)/shard_map/ppermute | solution.py:13
  328.1 199.1 %collective-permute-start.8 = (bf16[4,256,768]{1,2,0:T(8,128)(2,1)S(1)}, bf16[4,256,768]{1,2,0:T(8,128)(2,1)S(1)}, u32[]{:S(2)}, u32[]{:S(2)}) collective-permute-start(bf16[4,256,768]{1,2,0:T(8,128)(2,1)S(1)} %get-tuple-element.26), channel_id=1, source_target_pairs={{0,63},{1,0},{2,1},{3,2},{4,3},{5,4},{6,5},{7,6},{8,7},{9,8},{10,9... | collective-permute-start | bytes 4718600 | tf_op jit(solution)/shard_map/ppermute | solution.py:13
  402.9 124.3 %collective-permute-start.9 = (bf16[4,256,768]{1,2,0:T(8,128)(2,1)S(1)}, bf16[4,256,768]{1,2,0:T(8,128)(2,1)S(1)}, u32[]{:S(2)}, u32[]{:S(2)}) collective-permute-start(bf16[4,256,768]{1,2,0:T(8,128)(2,1)S(1)} %get-tuple-element.27), channel_id=1, source_target_pairs={{0,1},{1,2},{2,3},{3,4},{4,5},{5,6},{6,7},{7,8},{8,9},{9,10},{10,1... | collective-permute-start | bytes 4718600 | tf_op jit(solution)/shard_map/ppermute | solution.py:13
  533.8 322.0 %all-reduce.4.cloned.1.call-start = ((), (), s32[]{:S(2)}) async-start(), calls=%async_computation.3 | async-start | bytes 14155776 | tf_op jit(solution)/shard_map/psum | solution.py:126
  539.8 3.3 copy-start.31
  576.4 2.9 copy-start.16
  576.4 2.9 copy-start.19
  576.4 2.9 copy-start.21
  579.3 78.3 %copy-start.25 = (f32[256]{0:T(256)S(1)}, f32[256]{0:T(256)}, u32[]{:S(2)}) copy-start(f32[256]{0:T(256)} %copy-done.24) | copy-start | bytes 3076
  855.8 3.0 copy-start.18
  855.8 3.8 copy-start.9
  859.6 2.5 copy-start.8
  859.6 3.9 copy-start.1
  (15 other events, 17.4 us)
Sparse Core Ops, SparseCore 0:
  14.5 31.5 all-gather.1
  533.9 38.3 reduce-scatter.1
  578.9 276.8 all-reduce.3
where the time goes:
time: 872 us; the launch traced here: 870 us
  waiting for transfers between devices  638 us (73%)
  blocking collectives  77.3 us (9%)
  local copies, waits for them, and re-layouts  56.7 us (7%)
  starting transfers between devices  31.7 us (4%)
  other arithmetic  31.1 us (4%)
  matrix products  20.7 us (2%)
  between operations  14.2 us (2%)
    ppermute x12, waiting for transfers between devices, shifted(): return lax.ppermute(value, axis, pairs)  382 us
    psum x1, waiting for transfers between devices, per_device(): lax.psum((d_qkv, d_out, d_fc1, d_fc2, d_rel, d_gain_attn, d_gain_mlp), ('...  197 us
    psum x1, blocking collectives, per_device(): lax.psum((d_qkv, d_out, d_fc1, d_fc2, d_rel, d_gain_attn, d_gain_mlp), ('...  77.3 us
    all_gather x1, waiting for transfers between devices, per_device(): column = lax.all_gather(key_vals, 'lat', axis=0, tiled=True)  31.7 us
    ppermute x12, starting transfers between devices, shifted(): return lax.ppermute(value, axis, pairs)  31.6 us
    reduce_scatter x1, waiting for transfers between devices, per_device(): lax.psum_scatter(collected.reshape(bands * count, 2 * width), 'lat', scat...  27 us
    unnamed x76, local copies, waits for them, and re-layouts  23.5 us
    another operation x8, local copies, waits for them, and re-layouts, per_device(): stacked = jnp.stack(pieces).reshape(7, bands, count, 2 * width)  18.5 us
  transfers between devices with their start and end apart: 15, of which 10 were waited for; matrix products, arithmetic and copies ran while one was open for 4% of the time, Pallas kernels for 0%

commit v1 on v0

v1 whole, which is shorter than its diff:
```python
import jax
import jax.numpy as jnp
from jax import lax
from jax.experimental import pallas as pl
from jax.experimental.pallas import tpu as pltpu
from jax.sharding import Mesh, PartitionSpec as P

HEADS = 6
HEAD = 64
D = 384
FF = 1536
BANDS = 4
SECTORS = 64
CELLS = BANDS * SECTORS
SCALE = HEAD ** (-0.5)
ABSENT = -1e30
AXES = ("y_lo", "core", "y_hi", "x", "z")
PLANE = ("y_lo", "y_hi", "x")

LANES = 128
HALF = 7168
PIECE = HALF // 16
PART = PIECE // 8
QKV_FIRST = 6
FC1_AT, QKV_AT, REL_AT = 0, 4608, 6912
FC2_AT, OUT_AT, QKV_REST_AT, GAIN_AT = 0, 4608, 5760, 6912

f32, bf16 = jnp.float32, jnp.bfloat16


def dot(a, b):
    return lax.dot_general(a, b, (((1,), (0,)), ((), ())), preferred_element_type=f32)


def dot_nt(a, b):
    return lax.dot_general(a, b, (((1,), (1,)), ((), ())), preferred_element_type=f32)


def dot_tn(a, b):
    return lax.dot_general(a, b, (((0,), (0,)), ((), ())), preferred_element_type=f32)


def norm(values):
    centred = values - jnp.mean(values, -1, keepdims=True)
    inverse = lax.rsqrt(jnp.mean(centred * centred, -1, keepdims=True) + 1e-05)
    return centred * inverse, inverse


def norm_back(d_normed, gain, unit, inverse):
    d_unit = d_normed * gain
    d_values = inverse * (
        d_unit
        - jnp.mean(d_unit, -1, keepdims=True)
        - unit * jnp.mean(d_unit * unit, -1, keepdims=True)
    )
    return d_values, jnp.sum(d_normed * unit, 0, keepdims=True)


def gelu_and_slope(x):
    root = 0.7978845608028654
    square = x * x
    t = jnp.tanh(root * x * (1.0 + 0.044715 * square))
    half = 0.5 * (1.0 + t)
    slope = half + (0.5 * root) * x * (1.0 - t * t) * (1.0 + 3.0 * 0.044715 * square)
    return x * half, slope


def store_columns(ref, half, at, values):
    rows, width = values.shape
    for block in range(width // LANES):
        ref[half, pl.ds(at + block * rows, rows), :] = values[:, block * LANES : (block + 1) * LANES].astype(bf16)


def block_kernel(x_ref, cot_ref, gain_attn_ref, w_qkv_ref, bias_ref, w_out_ref, gain_mlp_ref, w_fc1_ref, w_fc2_ref,
                 out_ref, d_latent_ref, grads_ref):
    x = x_ref[...].astype(f32)
    gain_attn = gain_attn_ref[...]
    unit, inverse = norm(x)
    normed = (unit * gain_attn).astype(bf16)
    projected = dot(normed, w_qkv_ref[...]).astype(bf16)

    lane = lax.broadcasted_iota(jnp.int32, (1, LANES), 1)
    low = lane < HEAD
    apart = (
        lax.broadcasted_iota(jnp.int32, (SECTORS, LANES), 1)
        - lax.broadcasted_iota(jnp.int32, (SECTORS, LANES), 0)
    ) & (SECTORS - 1)

    def one_head(pair, second):
        return jnp.where(low, jnp.bfloat16(0), pair) if second else jnp.where(low, pair, jnp.bfloat16(0))

    def pair_of(array, part, pair):
        start = part * D + pair * LANES
        return array[:, start : start + LANES]

    probs, probs_b, mixed = [], [], []
    for pair in range(HEADS // 2):
        query, key, value = (pair_of(projected, part, pair) for part in range(3))
        total = None
        for second in range(2):
            head = 2 * pair + second
            tiles = []
            for first in range(6):
                tile = jnp.full((SECTORS, LANES), ABSENT, f32)
                for step in range(7):
                    row = bias_ref[(head * 6 + first) * 7 + step : (head * 6 + first) * 7 + step + 1, :]
                    tile = jnp.where(apart == (step - 3) % SECTORS, row, tile)
                tiles.append(tile)
            bias = jnp.concatenate(
                [jnp.concatenate([tiles[2 * side - band + 3] for band in range(BANDS)], 0) for side in range(2)], 1
            )
            score = dot_nt(one_head(query, second), key) * SCALE + bias
            weight = jnp.exp(score)
            prob = weight / jnp.sum(weight, -1, keepdims=True)
            prob_b = prob.astype(bf16)
            probs.append(prob)
            probs_b.append(prob_b)
            part = dot(prob_b, one_head(value, second))
            total = part if total is None else total + part
        mixed.append(total.astype(bf16))
    mixed = jnp.concatenate(mixed, 1)

    resid = x + dot(mixed, w_out_ref[...])
    gain_mlp = gain_mlp_ref[...]
    unit_two, inverse_two = norm(resid)
    normed_two = (unit_two * gain_mlp).astype(bf16)
    hidden = dot(normed_two, w_fc1_ref[...])
    active, slope = gelu_and_slope(hidden)
    active = active.astype(bf16)
    out_ref[...] = (resid + dot(active, w_fc2_ref[...])).astype(bf16)

    cot = cot_ref[...]
    store_columns(grads_ref, 1, FC2_AT, dot_tn(active, cot))
    d_hidden = (dot_nt(cot, w_fc2_ref[...]) * slope).astype(bf16)
    store_columns(grads_ref, 0, FC1_AT, dot_tn(normed_two, d_hidden))
    d_normed_two = dot_nt(d_hidden, w_fc1_ref[...])
    d_values, d_gain_mlp = norm_back(d_normed_two, gain_mlp, unit_two, inverse_two)
    d_resid = cot.astype(f32) + d_values
    d_resid_b = d_resid.astype(bf16)
    store_columns(grads_ref, 1, OUT_AT, dot_tn(mixed, d_resid_b))
    d_mixed = dot_nt(d_resid_b, w_out_ref[...]).astype(bf16)

    d_queries, d_keys, d_values_ = [], [], []
    rel_rows = []
    for pair in range(HEADS // 2):
        query, key, value = (pair_of(projected, part, pair) for part in range(3))
        d_mixed_pair = pair_of(d_mixed, 0, pair)
        d_query = d_key = d_value = None
        for second in range(2):
            head = 2 * pair + second
            prob, prob_b = probs[head], probs_b[head]
            d_mixed_here = one_head(d_mixed_pair, second)
            d_prob = dot_nt(d_mixed_here, value)
            d_score = prob * (d_prob - jnp.sum(prob * d_prob, -1, keepdims=True))
            for first in range(6):
                tile = None
                for band in range(BANDS):
                    for side in range(2):
                        if 2 * side - band + 3 == first:
                            here = d_score[band * SECTORS : (band + 1) * SECTORS, side * LANES : (side + 1) * LANES]
                            tile = here if tile is None else tile + here
                for step in range(7):
                    rel_rows.append(jnp.sum(jnp.where(apart == (step - 3) % SECTORS, tile, 0.0), 0, keepdims=True))
            d_score_b = (d_score * SCALE).astype(bf16)
            parts = (
                dot(d_score_b, one_head(key, second)),
                dot_tn(d_score_b, one_head(query, second)),
                dot_tn(prob_b, d_mixed_here),
            )
            if d_query is None:
                d_query, d_key, d_value = parts
            else:
                d_query, d_key, d_value = d_query + parts[0], d_key + parts[1], d_value + parts[2]
        d_queries.append(d_query.astype(bf16))
        d_keys.append(d_key.astype(bf16))
        d_values_.append(d_value.astype(bf16))
    d_proj = jnp.concatenate(d_queries + d_keys + d_values_, 1)
    d_qkv = dot_tn(normed, d_proj)
    store_columns(grads_ref, 0, QKV_AT, d_qkv[:, : QKV_FIRST * LANES])
    store_columns(grads_ref, 1, QKV_REST_AT, d_qkv[:, QKV_FIRST * LANES :])
    d_normed = dot_nt(d_proj, w_qkv_ref[...])
    d_flat, d_gain_attn = norm_back(d_normed, gain_attn, unit, inverse)
    d_latent_ref[...] = (d_resid + d_flat).astype(bf16)

    rel = jnp.concatenate(rel_rows + [jnp.zeros((4, LANES), f32)], 0)
    rel_low = jnp.sum(jnp.where(low, rel, 0.0), 1, keepdims=True)
    rel_high = jnp.sum(jnp.where(low, 0.0, rel), 1, keepdims=True)
    grads_ref[0, REL_AT:HALF, :] = jnp.where(lane == 0, rel_low, jnp.where(lane == 1, rel_high, 0.0)).astype(bf16)
    gains = [g[:, k * LANES : (k + 1) * LANES] for g in (d_gain_attn, d_gain_mlp) for k in range(3)]
    grads_ref[1, GAIN_AT:HALF, :] = jnp.concatenate(gains + [jnp.zeros((HALF - GAIN_AT - 6, LANES), f32)], 0).astype(bf16)


def block(x, cot, gain_attn, w_qkv, rel_bias, w_out, gain_mlp, w_fc1, w_fc2, interpret=False):
    sides = jnp.stack([rel_bias[:, :6], rel_bias[:, 1:]], -1).reshape(HEADS * 42, 2)
    bias_rows = jnp.repeat(sides, SECTORS, 1)
    return pl.pallas_call(
        block_kernel,
        out_shape=(
            jax.ShapeDtypeStruct((CELLS, D), bf16),
            jax.ShapeDtypeStruct((CELLS, D), bf16),
            jax.ShapeDtypeStruct((2, HALF, LANES), bf16),
        ),
        compiler_params=pltpu.CompilerParams(vmem_limit_bytes=56 * 1024 * 1024),
        interpret=interpret,
    )(x, cot, gain_attn.reshape(1, D), w_qkv, bias_rows, w_out, gain_mlp.reshape(1, D), w_fc1, w_fc2)


def exchange(value, axes):
    return lax.all_to_all(value, axes, 0, 0)


def total(value):
    return jnp.sum(value.astype(f32), 0).astype(bf16)


def to_sibling(value):
    return lax.ppermute(value, "core", [(0, 1), (1, 0)])


def reduce_everywhere(grads):
    core = lax.axis_index("core")
    arrived = to_sibling(lax.dynamic_index_in_dim(grads, 1 - core, 0, False))
    kept = lax.dynamic_index_in_dim(grads, core, 0, False)
    here = (kept.astype(f32) + arrived.astype(f32)).astype(bf16)
    here = total(exchange(here.reshape(16, PIECE, LANES), PLANE))
    here = total(exchange(here.reshape(8, PART, LANES), "z"))
    here = exchange(jnp.broadcast_to(here, (8, PART, LANES)), "z").reshape(PIECE, LANES)
    here = exchange(jnp.broadcast_to(here, (16, PIECE, LANES)), PLANE).reshape(HALF, LANES)
    other = to_sibling(here)
    return jnp.where(core == 0, here, other), jnp.where(core == 0, other, here)


def beside(half, at, blocks, rows):
    taken = half[at : at + blocks * rows].reshape(blocks, rows, LANES)
    return jnp.transpose(taken, (1, 0, 2)).reshape(rows, blocks * LANES).astype(f32)


def per_device(latent, cotangent, gain_attn, w_qkv, rel_bias, w_out, gain_mlp, w_fc1, w_fc2):
    shape = latent.shape
    sent = jnp.stack([latent.reshape(CELLS, D), cotangent.reshape(CELLS, D)], 1)
    arrived = exchange(sent, AXES)
    out, d_latent, grads = block(
        arrived[:, 0], arrived[:, 1], gain_attn, w_qkv, rel_bias, w_out, gain_mlp, w_fc1, w_fc2
    )
    home = exchange(jnp.stack([out, d_latent], 1), AXES)
    first, second = reduce_everywhere(grads)
    d_qkv = jnp.concatenate(
        [beside(first, QKV_AT, QKV_FIRST, D), beside(second, QKV_REST_AT, 9 - QKV_FIRST, D)], 1
    )
    d_out = beside(second, OUT_AT, 3, D)
    d_fc1 = beside(first, FC1_AT, 12, D)
    d_fc2 = beside(second, FC2_AT, 3, FF)
    rel = first[REL_AT : REL_AT + HEADS * 42, :2].astype(f32).reshape(HEADS, 6, 7, 2)
    d_rel = jnp.pad(rel[..., 0], ((0, 0), (0, 1), (0, 0))) + jnp.pad(rel[..., 1], ((0, 0), (1, 0), (0, 0)))
    gains = second[GAIN_AT : GAIN_AT + 6].astype(f32).reshape(2, D)
    return home[:, 0].reshape(shape), home[:, 1].reshape(shape), d_qkv, d_out, d_fc1, d_fc2, d_rel, gains[0], gains[1]


def solution(mesh):
    split = Mesh(mesh.devices.reshape(2, 2, 2, 4, 8), AXES)
    cells = P(("y_lo", "core"), ("y_hi", "x", "z"), None)
    return jax.shard_map(
        per_device,
        mesh=split,
        in_specs=(cells, cells) + (P(),) * 7,
        out_specs=(cells, cells) + (P(),) * 7,
        check_vma=False,
    )
```

time: 872 us -> 197 us (0.23)
  waiting for transfers between devices: 638 us -> 37.1 us
  other arithmetic: 31.1 us -> 8.71 us
  matrix products: 20.7 us -> 0 us
  local copies, waits for them, and re-layouts: 56.7 us -> 37.3 us
  between operations: 14.2 us -> 0.87 us
  Pallas kernels: 0 us -> 12.5 us
    ppermute x12 -> x2, waiting for transfers between devices: 382 us -> 3.62 us  [to_sibling(): return lax.ppermute(value, 'core', [(0, 1), (1, 0)])]
    psum x1 -> x0, waiting for transfers between devices: 197 us -> none  [per_device(): lax.psum((d_qkv, d_out, d_fc1, d_fc2, d_rel, d_gain_attn, d_gain_mlp), ('...]
    psum x1 -> x0, blocking collectives: 77.3 us -> none  [per_device(): lax.psum((d_qkv, d_out, d_fc1, d_fc2, d_rel, d_gain_attn, d_gain_mlp), ('...]
    all_to_all x0 -> x4, blocking collectives: none -> 73.4 us  [exchange(): return lax.all_to_all(value, axes, 0, 0)]
    all_to_all x0 -> x2, waiting for transfers between devices: none -> 33.5 us  [exchange(): return lax.all_to_all(value, axes, 0, 0)]
    all_gather x1 -> x0, waiting for transfers between devices: 31.7 us -> none  [per_device(): column = lax.all_gather(key_vals, 'lat', axis=0, tiled=True)]
    reduce_scatter x1 -> x0, waiting for transfers between devices: 27 us -> none  [per_device(): lax.psum_scatter(collected.reshape(bands * count, 2 * width), 'lat', scat...]
    ppermute x12 -> x2, starting transfers between devices: 31.6 us -> 5.86 us  [to_sibling(): return lax.ppermute(value, 'core', [(0, 1), (1, 0)])]
  transfers between devices with their start and end apart: 15 -> 4, of which waited for: 10 -> 3; matrix products, arithmetic and copies ran while one was open for 4% -> 3% of each run, Pallas kernels for 0% -> 0%
where the time goes in v1:
time: 197 us
  blocking collectives  73.4 us (37%)
  local copies, waits for them, and re-layouts  37.3 us (19%)
  waiting for transfers between devices  37.1 us (19%)
  starting transfers between devices  26.8 us (14%)
  Pallas kernels  12.5 us (6%)
  other arithmetic  8.71 us (4%)
    all_to_all x4, blocking collectives, exchange(): return lax.all_to_all(value, axes, 0, 0)  73.4 us
    all_to_all x2, waiting for transfers between devices, exchange(): return lax.all_to_all(value, axes, 0, 0)  33.5 us
    all_to_all x2, starting transfers between devices, exchange(): return lax.all_to_all(value, axes, 0, 0)  21 us
    pallas_call x1, Pallas kernels, block(): pl.pallas_call(block_kernel, out_shape=(jax.ShapeDtypeStruct((CELLS, D),...  12.5 us
    convert_element_type x8, local copies, waits for them, and re-layouts, beside(): jnp.transpose(taken, (1, 0, 2)).reshape(rows, blocks * LANES).astype(f32)  11.8 us
    unnamed x26, local copies, waits for them, and re-layouts  9.45 us
    ppermute x2, starting transfers between devices, to_sibling(): return lax.ppermute(value, 'core', [(0, 1), (1, 0)])  5.86 us
  transfers between devices with their start and end apart: 4, of which 3 were waited for; matrix products, arithmetic and copies ran while one was open for 3% of the time, Pallas kernels for 0%

profile of v1, /device:TPU:1, one launch (start us, length us, event | category | flops | bytes accessed | tf_op | source)
XLA Modules:
  0.0 196.7 jit_solution(9727297611592059609)
XLA Ops:
  0.7 1.1 pad_maximum_fusion
  1.8 1.2 copy.83
  2.9 15.7 %all-to-all-start = ((bf16[256,2,384]{2,1,0:T(2,128)(2,1)}), bf16[256,2,384]{2,1,0:T(2,128)(2,1)S(1)}, u32[]{:S(2)}, u32[]{:S(2)}) async-start(bf16[256,2,384]{2,1,0:T(2,128)(2,1)} %copy.83), calls=%async_computation | async-start | bytes 786432 | tf_op jit(solution)/shard_map/all_to_all | solution.py:209
  20.7 15.7 %all-to-all-done = bf16[256,2,384]{2,1,0:T(2,128)(2,1)S(1)} async-done(((bf16[256,2,384]{2,1,0:T(2,128)(2,1)}), bf16[256,2,384]{2,1,0:T(2,128)(2,1)S(1)}, u32[]{:S(2)}, u32[]{:S(2)}) %all-to-all-start) | async-done | bytes 393248 | tf_op jit(solution)/shard_map/all_to_all | solution.py:209
  37.0 0.8 copy_bitcast_fusion
  37.8 12.5 %shard_map.160 = (bf16[256,384]{1,0:T(8,128)(2,1)}, bf16[256,384]{1,0:T(8,128)(2,1)}, bf16[2,7168,128]{2,1,0:T(8,128)(2,1)}) custom-call(bf16[256,384]{1,0:T(8,128)(2,1)} %get-tuple-element.75.x_ref, bf16[256,384]{1,0:T(8,128)(2,1)} %get-tuple-element.74.cot_ref, f32[1,384]{1,0:T(1,128)} %reshape.87.gain_attn_ref, bf16[384,1152]{1,0:T(8,128)(2,1)} %w_qkv_ref.1, ...), custom_call_target="tpu_custom_call" | custom-call | tf_op jit(solution)/shard_map/pallas_call | solution.py:196
  50.3 2.8 %dynamic-slice_bitcast_fusion = bf16[7168,128]{1,0:T(8,128)(2,1)} fusion(bf16[2,7168,128]{2,1,0:T(8,128)(2,1)} %get-tuple-element.14, s32[]{:T(128)S(6)} %select_n.21), kind=kLoop, calls=%fused_computation.2 | loop fusion | bytes 3670020 | tf_op jit(solution)/shard_map/jit(dynamic_index_in_dim)/squeeze | solution.py:222
  53.1 1.3 collective-permute-start
  54.4 3.6 %collective-permute-done = bf16[7168,128]{1,0:T(8,128)(2,1)S(1)} collective-permute-done((bf16[7168,128]{1,0:T(8,128)(2,1)}, bf16[7168,128]{1,0:T(8,128)(2,1)S(1)}, u32[]{:S(2)}, u32[]{:S(2)}) %collective-permute-start) | collective-permute-done | bytes 1835040 | tf_op jit(solution)/shard_map/ppermute | solution.py:217
  58.0 2.0 %fusion = bf16[7168,128]{1,0:T(8,128)(2,1)S(1)} fusion(bf16[7168,128]{1,0:T(8,128)(2,1)S(1)} %collective-permute-done, bf16[2,7168,128]{2,1,0:T(8,128)(2,1)} %get-tuple-element.14, s32[]{:T(128)S(6)} %select_n.20), kind=kLoop, calls=%fused_computation.1 | loop fusion | flops 3670016 | bytes 5505028 | tf_op jit(solution)/shard_map/convert_element_type | solution.py:224
  60.0 28.1 %all_to_all.30 = bf16[16,448,128]{2,1,0:T(8,128)(2,1)S(1)} all-to-all(bf16[16,448,128]{2,1,0:T(8,128)(2,1)S(1)} %bitcast.53), channel_id=1, replica_groups=mesh['y_lo'=2,'core'=2,'y_hi'=2,'x'=4,'z'=8] {'y_lo','y_hi','x'}, dimensions={0} | all-to-all | bytes 3670016 | tf_op jit(solution)/shard_map/all_to_all | solution.py:209
  88.3 10.1 %all_to_all.31 = bf16[8,56,128]{2,1,0:T(8,128)(2,1)S(1)} all-to-all(bf16[8,56,128]{2,1,0:T(8,128)(2,1)S(1)} %bitcast.61), channel_id=1, replica_groups=mesh['y_lo'=2,'core'=2,'y_hi'=2,'x'=4,'z'=8] {'z'}, dimensions={0} | all-to-all | bytes 229376 | tf_op jit(solution)/shard_map/all_to_all | solution.py:209
  98.5 10.1 %all_to_all.32 = bf16[8,56,128]{2,1,0:T(8,128)(2,1)S(1)} all-to-all(bf16[8,56,128]{2,1,0:T(8,128)(2,1)S(1)} %broadcast_in_dim.10), channel_id=1, replica_groups=mesh['y_lo'=2,'core'=2,'y_hi'=2,'x'=4,'z'=8] {'z'}, dimensions={0} | all-to-all | bytes 229376 | tf_op jit(solution)/shard_map/all_to_all | solution.py:209
  109.0 25.0 %all_to_all.33 = bf16[16,448,128]{2,1,0:T(8,128)(2,1)S(1)} all-to-all(bf16[16,448,128]{2,1,0:T(8,128)(2,1)S(1)} %broadcast_in_dim.11), channel_id=1, replica_groups=mesh['y_lo'=2,'core'=2,'y_hi'=2,'x'=4,'z'=8] {'y_lo','y_hi','x'}, dimensions={0} | all-to-all | bytes 3670016 | tf_op jit(solution)/shard_map/all_to_all | solution.py:209
  134.0 2.9 %copy.91 = bf16[7168,128]{0,1:T(8,128)(2,1)} copy(bf16[7168,128]{1,0:T(8,128)(2,1)S(1)} %bitcast.52) | data formatting | bytes 3670016 | tf_op jit(solution)/shard_map/reshape | solution.py:228
  136.9 4.6 %collective-permute-start.1 = (bf16[7168,128]{0,1:T(8,128)(2,1)}, bf16[7168,128]{0,1:T(8,128)(2,1)}, u32[]{:S(2)}, u32[]{:S(2)}) collective-permute-start(bf16[7168,128]{0,1:T(8,128)(2,1)} %copy.91), channel_id=1, source_target_pairs={{0,64},{64,0},{1,65},{65,1},{2,66},{66,2},{3,67},{67,3},{4,68},{68... | collective-permute-start | bytes 5505032 | tf_op jit(solution)/shard_map/ppermute | solution.py:217
  141.5 1.2 copy.87
  142.7 5.3 %all-to-all-start.1 = ((bf16[256,2,384]{2,1,0:T(2,128)(2,1)}), bf16[256,2,384]{2,1,0:T(2,128)(2,1)S(1)}, u32[]{:S(2)}, u32[]{:S(2)}) async-start(bf16[256,2,384]{2,1,0:T(2,128)(2,1)} %copy.87), calls=%async_computation.1 | async-start | bytes 786432 | tf_op jit(solution)/shard_map/all_to_all | solution.py:209
  148.0 17.8 %all-to-all-done.1 = bf16[256,2,384]{2,1,0:T(2,128)(2,1)S(1)} async-done(((bf16[256,2,384]{2,1,0:T(2,128)(2,1)}), bf16[256,2,384]{2,1,0:T(2,128)(2,1)S(1)}, u32[]{:S(2)}, u32[]{:S(2)}) %all-to-all-start.1) | async-done | bytes 393248 | tf_op jit(solution)/shard_map/all_to_all | solution.py:209
  167.8 1.7 broadcast_select_fusion.1
  169.6 1.6 slice_convert_fusion.1
  171.2 1.0 slice_convert_fusion.2
  174.9 1.1 copy.93
  175.9 3.0 %copy.99 = f32[4608,128]{1,0:T(8,128)} copy(f32[4608,128]{0,1:T(8,128)} %slice_convert_fusion.1) | data formatting | bytes 4718592 | tf_op jit(solution)/shard_map/convert_element_type | solution.py:235
  179.0 3.0 %copy.100 = f32[384,12,128]{0,2,1:T(8,128)} copy(f32[384,12,128]{2,0,1:T(8,128)} %bitcast.48) | data formatting | bytes 4718592 | tf_op jit(solution)/shard_map/convert_element_type | solution.py:235
  182.0 3.1 %copy.107 = f32[384,1536]{1,0:T(8,128)} copy(f32[384,1536]{0,1:T(8,128)} %bitcast.49) | data formatting | bytes 4718592
  185.6 1.1 copy.106
  186.6 1.2 copy.95
  188.0 2.0 copy.101
  190.0 2.0 %copy.102 = f32[1536,3,128]{0,2,1:T(8,128)S(1)} copy(f32[1536,3,128]{2,0,1:T(8,128)} %bitcast.50) | data formatting | bytes 4718592 | tf_op jit(solution)/shard_map/convert_element_type | solution.py:235
  192.1 2.0 copy.108
  194.1 1.9 copy.105
  (53 shorter events, 9.5 us)
Async XLA Ops:
  0.6 17.9 %copy-start.8 = (f32[384]{0:T(512)S(1)}, f32[384]{0:T(512)}, u32[]{:S(2)}) copy-start(f32[384]{0:T(512)} %param.11) | copy-start | bytes 4612
  0.7 18.5 %copy-start.9 = (f32[384]{0:T(512)S(1)}, f32[384]{0:T(512)}, u32[]{:S(2)}) copy-start(f32[384]{0:T(512)} %param.15) | copy-start | bytes 4612
  0.7 19.1 %copy-start.5 = (f32[6,7,7]{2,1,0:T(8,128)S(1)}, f32[6,7,7]{2,1,0:T(8,128)}, u32[]{:S(2)}) copy-start(f32[6,7,7]{2,1,0:T(8,128)} %param.13) | copy-start | bytes 3532
  2.9 33.5 %all-to-all-start = ((bf16[256,2,384]{2,1,0:T(2,128)(2,1)}), bf16[256,2,384]{2,1,0:T(2,128)(2,1)S(1)}, u32[]{:S(2)}, u32[]{:S(2)}) async-start(bf16[256,2,384]{2,1,0:T(2,128)(2,1)} %copy.83), calls=%async_computation | async-start | bytes 786432 | tf_op jit(solution)/shard_map/all_to_all | solution.py:209
  53.1 4.9 %collective-permute-start = (bf16[7168,128]{1,0:T(8,128)(2,1)}, bf16[7168,128]{1,0:T(8,128)(2,1)S(1)}, u32[]{:S(2)}, u32[]{:S(2)}) collective-permute-start(bf16[7168,128]{1,0:T(8,128)(2,1)} %dynamic-slice_bitcast_fusion), channel_id=1, source_target_pairs={{0,64},{64,0},{1,65},{65,1},{2,66},{66,2},{3,67},{67,3},{4,68},{68... | collective-permute-start | bytes 5505032 | tf_op jit(solution)/shard_map/ppermute | solution.py:217
  134.0 7.5 %copy-start.3 = (bf16[256,384]{1,0:T(8,128)(2,1)S(1)}, bf16[256,384]{1,0:T(8,128)(2,1)}, u32[]{:S(2)}) copy-start(bf16[256,384]{1,0:T(8,128)(2,1)} %get-tuple-element.12) | copy-start | bytes 589828
  134.0 7.5 %copy-start.4 = (bf16[256,384]{1,0:T(8,128)(2,1)S(1)}, bf16[256,384]{1,0:T(8,128)(2,1)}, u32[]{:S(2)}) copy-start(bf16[256,384]{1,0:T(8,128)(2,1)} %get-tuple-element.13) | copy-start | bytes 589828
  136.9 30.9 %collective-permute-start.1 = (bf16[7168,128]{0,1:T(8,128)(2,1)}, bf16[7168,128]{0,1:T(8,128)(2,1)}, u32[]{:S(2)}, u32[]{:S(2)}) collective-permute-start(bf16[7168,128]{0,1:T(8,128)(2,1)} %copy.91), channel_id=1, source_target_pairs={{0,64},{64,0},{1,65},{65,1},{2,66},{66,2},{3,67},{67,3},{4,68},{68... | collective-permute-start | bytes 5505032 | tf_op jit(solution)/shard_map/ppermute | solution.py:217
  142.7 25.1 %copy-start = (bf16[7168,128]{0,1:T(8,128)(2,1)S(1)}, bf16[7168,128]{0,1:T(8,128)(2,1)}, u32[]{:S(2)}) copy-start(bf16[7168,128]{0,1:T(8,128)(2,1)} %copy.91) | copy-start | bytes 5505028
  142.7 23.1 %all-to-all-start.1 = ((bf16[256,2,384]{2,1,0:T(2,128)(2,1)}), bf16[256,2,384]{2,1,0:T(2,128)(2,1)S(1)}, u32[]{:S(2)}, u32[]{:S(2)}) async-start(bf16[256,2,384]{2,1,0:T(2,128)(2,1)} %copy.87), calls=%async_computation.1 | async-start | bytes 786432 | tf_op jit(solution)/shard_map/all_to_all | solution.py:209
  182.0 3.1 %copy-start.1 = (f32[1152,128]{0,1:T(8,128)S(1)}, f32[1152,128]{0,1:T(8,128)}, u32[]{:S(2)}) copy-start(f32[1152,128]{0,1:T(8,128)} %get-tuple-element.62) | copy-start | bytes 1769476
  192.0 2.0 copy-start.2
  194.1 1.9 copy-start.6
  194.1 1.9 copy-start.7

commit v2 on v1

--- a/solution.py
+++ b/solution.py
@@ -18,12 +18,16 @@
 PLANE = ("y_lo", "y_hi", "x")
 
 LANES = 128
-HALF = 7168
-PIECE = HALF // 16
-PART = PIECE // 8
+PLACES = 16
+DEPTH = 8
+GRADS = 448
+PART = GRADS // DEPTH
+OWN = 48
+PART_ROOM = 64
+FC1_AT, QKV_AT = 0, 288
+FC2_AT, OUT_AT, QKV_REST_AT = 0, 288, 360
+SMALL_AT = 432
 QKV_FIRST = 6
-FC1_AT, QKV_AT, REL_AT = 0, 4608, 6912
-FC2_AT, OUT_AT, QKV_REST_AT, GAIN_AT = 0, 4608, 5760, 6912
 
 f32, bf16 = jnp.float32, jnp.bfloat16
 
@@ -66,13 +70,16 @@
 
 
 def store_columns(ref, half, at, values):
-    rows, width = values.shape
-    for block in range(width // LANES):
-        ref[half, pl.ds(at + block * rows, rows), :] = values[:, block * LANES : (block + 1) * LANES].astype(bf16)
-
-
-def block_kernel(x_ref, cot_ref, gain_attn_ref, w_qkv_ref, bias_ref, w_out_ref, gain_mlp_ref, w_fc1_ref, w_fc2_ref,
-                 out_ref, d_latent_ref, grads_ref):
+    rows = values.shape[0] // 8
+    for block in range(values.shape[1] // LANES):
+        here = values[:, block * LANES : (block + 1) * LANES].reshape(8, rows, LANES)
+        first = at + block // 2 * rows
+        start = block % 2 * 8
+        ref[half, start : start + 8, first : first + rows, :] = here.astype(bf16)
+
+
+def block_kernel(core_ref, x_ref, cot_ref, gain_attn_ref, w_qkv_ref, bias_ref, w_out_ref, gain_mlp_ref, w_fc1_ref, w_fc2_ref,
+                 kept_ref, sent_ref, halves_ref):
     x = x_ref[...].astype(f32)
     gain_attn = gain_attn_ref[...]
     unit, inverse = norm(x)
@@ -127,17 +134,20 @@
     hidden = dot(normed_two, w_fc1_ref[...])
     active, slope = gelu_and_slope(hidden)
     active = active.astype(bf16)
-    out_ref[...] = (resid + dot(active, w_fc2_ref[...])).astype(bf16)
+    output = resid + dot(active, w_fc2_ref[...])
 
     cot = cot_ref[...]
-    store_columns(grads_ref, 1, FC2_AT, dot_tn(active, cot))
+    d_fc2 = dot_tn(active, cot)
+    for block in range(3):
+        here = d_fc2[:, block * LANES : (block + 1) * LANES].reshape(PLACES, FF // PLACES, LANES)
+        halves_ref[1, :, FC2_AT + block * 96 : FC2_AT + block * 96 + 96, :] = here.astype(bf16)
     d_hidden = (dot_nt(cot, w_fc2_ref[...]) * slope).astype(bf16)
-    store_columns(grads_ref, 0, FC1_AT, dot_tn(normed_two, d_hidden))
+    store_columns(halves_ref, 0, FC1_AT, dot_tn(normed_two, d_hidden))
     d_normed_two = dot_nt(d_hidden, w_fc1_ref[...])
     d_values, d_gain_mlp = norm_back(d_normed_two, gain_mlp, unit_two, inverse_two)
     d_resid = cot.astype(f32) + d_values
     d_resid_b = d_resid.astype(bf16)
-    store_columns(grads_ref, 1, OUT_AT, dot_tn(mixed, d_resid_b))
+    d_out = dot_tn(mixed, d_resid_b)
     d_mixed = dot_nt(d_resid_b, w_out_ref[...]).astype(bf16)
 
     d_queries, d_keys, d_values_ = [], [], []
@@ -152,6 +162,7 @@
             d_mixed_here = one_head(d_mixed_pair, second)
             d_prob = dot_nt(d_mixed_here, value)
             d_score = prob * (d_prob - jnp.sum(prob * d_prob, -1, keepdims=True))
+            sums = []
             for first in range(6):
                 tile = None
                 for band in range(BANDS):
@@ -160,7 +171,19 @@
                             here = d_score[band * SECTORS : (band + 1) * SECTORS, side * LANES : (side + 1) * LANES]
                             tile = here if tile is None else tile + here
                 for step in range(7):
-                    rel_rows.append(jnp.sum(jnp.where(apart == (step - 3) % SECTORS, tile, 0.0), 0, keepdims=True))
+                    sums.append(jnp.sum(jnp.where(apart == (step - 3) % SECTORS, tile, 0.0), 0, keepdims=True))
+            none = jnp.zeros((7, LANES), f32)
+            sums = jnp.concatenate(sums, 0)
+            taps = jnp.concatenate([jnp.where(low, sums, 0.0), none], 0) + jnp.concatenate(
+                [none, jnp.where(low, 0.0, sums)], 0
+            )
+            taps = jnp.concatenate([taps, jnp.zeros((LANES - 49, LANES), f32)], 0)
+            rel_rows.append(
+                lax.dot_general(
+                    jnp.ones((8, LANES), f32), taps, (((1,), (1,)), ((), ())),
+                    precision=lax.Precision.HIGHEST, preferred_element_type=f32,
+                )[:1]
+            )
             d_score_b = (d_score * SCALE).astype(bf16)
             parts = (
                 dot(d_score_b, one_head(key, second)),
@@ -176,84 +199,205 @@
         d_values_.append(d_value.astype(bf16))
     d_proj = jnp.concatenate(d_queries + d_keys + d_values_, 1)
     d_qkv = dot_tn(normed, d_proj)
-    store_columns(grads_ref, 0, QKV_AT, d_qkv[:, : QKV_FIRST * LANES])
-    store_columns(grads_ref, 1, QKV_REST_AT, d_qkv[:, QKV_FIRST * LANES :])
+    store_columns(halves_ref, 0, QKV_AT, d_qkv[:, : QKV_FIRST * LANES])
+    store_columns(halves_ref, 1, OUT_AT, jnp.concatenate([d_out, d_qkv[:, QKV_FIRST * LANES :]], 1))
     d_normed = dot_nt(d_proj, w_qkv_ref[...])
     d_flat, d_gain_attn = norm_back(d_normed, gain_attn, unit, inverse)
-    d_latent_ref[...] = (d_resid + d_flat).astype(bf16)
-
-    rel = jnp.concatenate(rel_rows + [jnp.zeros((4, LANES), f32)], 0)
-    rel_low = jnp.sum(jnp.where(low, rel, 0.0), 1, keepdims=True)
-    rel_high = jnp.sum(jnp.where(low, 0.0, rel), 1, keepdims=True)
-    grads_ref[0, REL_AT:HALF, :] = jnp.where(lane == 0, rel_low, jnp.where(lane == 1, rel_high, 0.0)).astype(bf16)
+    d_latent = d_resid + d_flat
+
     gains = [g[:, k * LANES : (k + 1) * LANES] for g in (d_gain_attn, d_gain_mlp) for k in range(3)]
-    grads_ref[1, GAIN_AT:HALF, :] = jnp.concatenate(gains + [jnp.zeros((HALF - GAIN_AT - 6, LANES), f32)], 0).astype(bf16)
-
-
-def block(x, cot, gain_attn, w_qkv, rel_bias, w_out, gain_mlp, w_fc1, w_fc2, interpret=False):
+    small = jnp.concatenate(rel_rows + [jnp.zeros((2, LANES), f32)] + gains + [jnp.zeros((2, LANES), f32)], 0)
+    halves_ref[0, 0, SMALL_AT:GRADS, :] = small.astype(bf16)
+    halves_ref[0, 1:, SMALL_AT:GRADS, :] = jnp.zeros((PLACES - 1, GRADS - SMALL_AT, LANES), bf16)
+    halves_ref[1, :, SMALL_AT:GRADS, :] = jnp.zeros((PLACES, GRADS - SMALL_AT, LANES), bf16)
+    for band in range(BANDS):
+        y_lo, core = band // 2, band % 2
+        rows = slice(band * SECTORS, (band + 1) * SECTORS)
+        for block in range(3):
+            lanes = slice(block * LANES, (block + 1) * LANES)
+            both = jnp.concatenate([a[rows, lanes].reshape(8, DEPTH, LANES) for a in (output, d_latent)], 1)
+            at = GRADS + block * 16
+            halves_ref[core, y_lo * 8 : y_lo * 8 + 8, at : at + 16, :] = both.astype(bf16)
+    core = core_ref[0]
+    kept_ref[...] = halves_ref[core]
+    sent_ref[...] = halves_ref[1 - core]
+
+
+def params():
+    return pltpu.CompilerParams(vmem_limit_bytes=56 * 1024 * 1024)
+
+
+SCALAR = pl.BlockSpec(memory_space=pltpu.SMEM)
+WHOLE = pl.BlockSpec(memory_space=pltpu.VMEM)
+
+
+def block(core, x, cot, gain_attn, w_qkv, rel_bias, w_out, gain_mlp, w_fc1, w_fc2, interpret=False):
     sides = jnp.stack([rel_bias[:, :6], rel_bias[:, 1:]], -1).reshape(HEADS * 42, 2)
     bias_rows = jnp.repeat(sides, SECTORS, 1)
+    half = jax.ShapeDtypeStruct((PLACES, GRADS + OWN, LANES), bf16)
     return pl.pallas_call(
         block_kernel,
-        out_shape=(
-            jax.ShapeDtypeStruct((CELLS, D), bf16),
-            jax.ShapeDtypeStruct((CELLS, D), bf16),
-            jax.ShapeDtypeStruct((2, HALF, LANES), bf16),
-        ),
-        compiler_params=pltpu.CompilerParams(vmem_limit_bytes=56 * 1024 * 1024),
+        out_shape=(half, half),
+        in_specs=[SCALAR] + [WHOLE] * 9,
+        out_specs=(WHOLE, WHOLE),
+        scratch_shapes=[pltpu.VMEM((2, PLACES, GRADS + OWN, LANES), bf16)],
+        compiler_params=params(),
         interpret=interpret,
-    )(x, cot, gain_attn.reshape(1, D), w_qkv, bias_rows, w_out, gain_mlp.reshape(1, D), w_fc1, w_fc2)
+    )(core, x, cot, gain_attn.reshape(1, D), w_qkv, bias_rows, w_out, gain_mlp.reshape(1, D), w_fc1, w_fc2)
+
+
+def merge_kernel(core_ref, kept_ref, arrived_ref, out_ref):
+    total = kept_ref[:, :GRADS, :].astype(f32) + arrived_ref[:, :GRADS, :].astype(f32)
+    out_ref[:, :GRADS, :] = total.astype(bf16)
+
+    def cells(first, second):
+        out_ref[:, GRADS : GRADS + OWN, :] = first[:, GRADS:, :]
+        out_ref[:, GRADS + OWN :, :] = second[:, GRADS:, :]
+
+    @pl.when(core_ref[0] == 0)
+    def _():
+        cells(kept_ref, arrived_ref)
+
+    @pl.when(core_ref[0] != 0)
+    def _():
+        cells(arrived_ref, kept_ref)
+
+
+def merge(core, kept, arrived, interpret=False):
+    return pl.pallas_call(
+        merge_kernel,
+        out_shape=jax.ShapeDtypeStruct((PLACES, GRADS + 2 * OWN, LANES), bf16),
+        in_specs=[SCALAR, WHOLE, WHOLE],
+        out_specs=WHOLE,
+        compiler_params=params(),
+        interpret=interpret,
+    )(core, kept, arrived)
+
+
+def plane_kernel(arrived_ref, out_ref):
+    total = arrived_ref[0, :GRADS, :].astype(f32)
+    for place in range(1, PLACES):
+        total = total + arrived_ref[place, :GRADS, :].astype(f32)
+    room = jnp.zeros((DEPTH, PART_ROOM - PART, LANES), f32)
+    out_ref[:, :PART_ROOM, :] = jnp.concatenate([total.reshape(DEPTH, PART, LANES), room], 1).astype(bf16)
+    count = 2 * PLACES * 2 * DEPTH
+    blocks = []
+    for block in range(3):
+        at = GRADS + block * 16
+        blocks.append(
+            jnp.concatenate([arrived_ref[:, at + c * OWN : at + c * OWN + 16, :].reshape(256, LANES) for c in range(2)], 0)
+        )
+    rows = jnp.concatenate(blocks, 1)
+    to = lax.broadcasted_iota(jnp.int32, (count, count), 0)
+    source = ((to & 1) << 8) | (((to >> 1) & 15) << 4) | (((to >> 5) & 1) << 3) | (to >> 6)
+    chosen = jnp.where(lax.broadcasted_iota(jnp.int32, (count, count), 1) == source, 1.0, 0.0).astype(bf16)
+    moved = dot(chosen, rows).astype(bf16).reshape(DEPTH, 2, 32, 3 * LANES)
+    for array in range(2):
+        for block in range(3):
+            at = PART_ROOM + (array * 3 + block) * 32
+            out_ref[:, at : at + 32, :] = moved[:, array, :, block * LANES : (block + 1) * LANES]
+
+
+def plane(arrived, interpret=False):
+    return pl.pallas_call(
+        plane_kernel,
+        out_shape=jax.ShapeDtypeStruct((DEPTH, PART_ROOM + 192, LANES), bf16),
+        in_specs=[WHOLE],
+        out_specs=WHOLE,
+        compiler_params=params(),
+        interpret=interpret,
+    )(arrived)
+
+
+def depth_kernel(arrived_ref, part_ref, output_ref, d_latent_ref):
+    total = jnp.sum(arrived_ref[:, :PART_ROOM, :].astype(f32), 0)[:PART]
+    part_ref[...] = jnp.broadcast_to(total[None], (DEPTH, PART, LANES)).astype(bf16)
+    for array, ref in enumerate((output_ref, d_latent_ref)):
+        for block in range(3):
+            at = PART_ROOM + (array * 3 + block) * 32
+            ref[:, block * LANES : (block + 1) * LANES] = arrived_ref[:, at : at + 32, :].reshape(CELLS, LANES)
+
+
+def depth(arrived, interpret=False):
+    cells = jax.ShapeDtypeStruct((CELLS, D), bf16)
+    return pl.pallas_call(
+        depth_kernel,
+        out_shape=(jax.ShapeDtypeStruct((DEPTH, PART, LANES), bf16), cells, cells),
+        in_specs=[WHOLE],
+        out_specs=(WHOLE, WHOLE, WHOLE),
+        compiler_params=params(),
+        interpret=interpret,
+    )(arrived)
+
+
+def assemble_kernel(core_ref, here_ref, other_ref, d_qkv_ref, d_out_ref, d_fc1_ref, d_fc2_ref, small_ref):
+    def columns(half, at, block, rows):
+        first = at + block // 2 * rows
+        start = block % 2 * 8
+        return half[start : start + 8, first : first + rows, :].astype(f32).reshape(8 * rows, LANES)
+
+    def lanes(block):
+        return slice(block * LANES, (block + 1) * LANES)
+
+    def write(first, second):
+        for block in range(12):
+            d_fc1_ref[:, lanes(block)] = columns(first, FC1_AT, block, 48)
+        for block in range(3):
+            at = FC2_AT + block * 96
+            d_fc2_ref[:, lanes(block)] = second[:, at : at + 96, :].astype(f32).reshape(FF, LANES)
+        for block in range(9):
+            if block < QKV_FIRST:
+                d_qkv_ref[:, lanes(block)] = columns(first, QKV_AT, block, 48)
+            else:
+                d_qkv_ref[:, lanes(block)] = columns(second, OUT_AT, block - QKV_FIRST + 3, 48)
+        for block in range(3):
+            d_out_ref[:, lanes(block)] = columns(second, OUT_AT, block, 48)
+        small_ref[...] = first[0, SMALL_AT:GRADS, :].astype(f32)
+
+    @pl.when(core_ref[0] == 0)
+    def _():
+        write(here_ref, other_ref)
+
+    @pl.when(core_ref[0] != 0)
+    def _():
+        write(other_ref, here_ref)
+
+
+def assemble(core, here, other, interpret=False):
+    shapes = ((D, 3 * D), (D, D), (D, FF), (FF, D), (16, LANES))
+    return pl.pallas_call(
+        assemble_kernel,
+        out_shape=tuple(jax.ShapeDtypeStruct(s, f32) for s in shapes),
+        in_specs=[SCALAR, WHOLE, WHOLE],
+        out_specs=(WHOLE,) * 5,
+        compiler_params=params(),
+        interpret=interpret,
+    )(core, here, other)
 
 
 def exchange(value, axes):
     return lax.all_to_all(value, axes, 0, 0)
 
 
-def total(value):
-    return jnp.sum(value.astype(f32), 0).astype(bf16)
-
-
 def to_sibling(value):
     return lax.ppermute(value, "core", [(0, 1), (1, 0)])
 
 
-def reduce_everywhere(grads):
-    core = lax.axis_index("core")
-    arrived = to_sibling(lax.dynamic_index_in_dim(grads, 1 - core, 0, False))
-    kept = lax.dynamic_index_in_dim(grads, core, 0, False)
-    here = (kept.astype(f32) + arrived.astype(f32)).astype(bf16)
-    here = total(exchange(here.reshape(16, PIECE, LANES), PLANE))
-    here = total(exchange(here.reshape(8, PART, LANES), "z"))
-    here = exchange(jnp.broadcast_to(here, (8, PART, LANES)), "z").reshape(PIECE, LANES)
-    here = exchange(jnp.broadcast_to(here, (16, PIECE, LANES)), PLANE).reshape(HALF, LANES)
-    other = to_sibling(here)
-    return jnp.where(core == 0, here, other), jnp.where(core == 0, other, here)
-
-
-def beside(half, at, blocks, rows):
-    taken = half[at : at + blocks * rows].reshape(blocks, rows, LANES)
-    return jnp.transpose(taken, (1, 0, 2)).reshape(rows, blocks * LANES).astype(f32)
-
-
 def per_device(latent, cotangent, gain_attn, w_qkv, rel_bias, w_out, gain_mlp, w_fc1, w_fc2):
     shape = latent.shape
-    sent = jnp.stack([latent.reshape(CELLS, D), cotangent.reshape(CELLS, D)], 1)
+    core = lax.axis_index("core").reshape(1)
+    both = jnp.stack([latent.reshape(CELLS, D), cotangent.reshape(CELLS, D)], 1).reshape(DEPTH, 2, 2, 4, 2, 2, D)
+    sent = jnp.transpose(both, (1, 4, 2, 3, 0, 5, 6)).reshape(CELLS, 2, D)
     arrived = exchange(sent, AXES)
-    out, d_latent, grads = block(
-        arrived[:, 0], arrived[:, 1], gain_attn, w_qkv, rel_bias, w_out, gain_mlp, w_fc1, w_fc2
-    )
-    home = exchange(jnp.stack([out, d_latent], 1), AXES)
-    first, second = reduce_everywhere(grads)
-    d_qkv = jnp.concatenate(
-        [beside(first, QKV_AT, QKV_FIRST, D), beside(second, QKV_REST_AT, 9 - QKV_FIRST, D)], 1
-    )
-    d_out = beside(second, OUT_AT, 3, D)
-    d_fc1 = beside(first, FC1_AT, 12, D)
-    d_fc2 = beside(second, FC2_AT, 3, FF)
-    rel = first[REL_AT : REL_AT + HEADS * 42, :2].astype(f32).reshape(HEADS, 6, 7, 2)
-    d_rel = jnp.pad(rel[..., 0], ((0, 0), (0, 1), (0, 0))) + jnp.pad(rel[..., 1], ((0, 0), (1, 0), (0, 0)))
-    gains = second[GAIN_AT : GAIN_AT + 6].astype(f32).reshape(2, D)
-    return home[:, 0].reshape(shape), home[:, 1].reshape(shape), d_qkv, d_out, d_fc1, d_fc2, d_rel, gains[0], gains[1]
+    kept, sent = block(core, arrived[:, 0], arrived[:, 1], gain_attn, w_qkv, rel_bias, w_out, gain_mlp, w_fc1, w_fc2)
+    merged = merge(core, kept, to_sibling(sent))
+    part, output, d_latent = depth(exchange(plane(exchange(merged, PLANE)), "z"))
+    piece = exchange(part, "z").reshape(GRADS, LANES)
+    here = exchange(jnp.broadcast_to(piece, (PLACES, GRADS, LANES)), PLANE)
+    d_qkv, d_out, d_fc1, d_fc2, small = assemble(core, here, to_sibling(here))
+    d_rel = small[:HEADS, :49].reshape(HEADS, 7, 7)
+    gains = small[8:14].reshape(2, D)
+    return output.reshape(shape), d_latent.reshape(shape), d_qkv, d_out, d_fc1, d_fc2, d_rel, gains[0], gains[1]
 
 
 def solution(mesh):

time: 197 us -> 176 us (0.89)
  local copies, waits for them, and re-layouts: 37.3 us -> 11.7 us
  blocking collectives: 73.4 us -> 89.3 us
  Pallas kernels: 12.5 us -> 27.6 us
  waiting for transfers between devices: 37.1 us -> 23 us
  other arithmetic: 8.71 us -> 1.65 us
  starting transfers between devices: 26.8 us -> 21.9 us
    all_to_all x2 -> x1, waiting for transfers between devices: 33.5 us -> 15.7 us  [exchange(): return lax.all_to_all(value, axes, 0, 0)]
    all_to_all x4, blocking collectives: 73.4 us -> 89.3 us  [exchange(): return lax.all_to_all(value, axes, 0, 0)]
    pallas_call x1 -> x5, Pallas kernels: 12.5 us -> 27.6 us  [the longest x1 13 us: block(): pl.pallas_call(block_kernel, out_shape=(half, half), in_specs=[SCALAR] +...]
    convert_element_type x8 -> x0, local copies, waits for them, and re-layouts: 11.8 us -> none  [beside(): jnp.transpose(taken, (1, 0, 2)).reshape(rows, blocks * LANES).astype(f32)]
    unnamed x26 -> x12, local copies, waits for them, and re-layouts: 9.45 us -> 2.56 us
    all_to_all x2 -> x1, starting transfers between devices: 21 us -> 15.7 us  [exchange(): return lax.all_to_all(value, axes, 0, 0)]
    convert_element_type x5 -> x0, other arithmetic: 4.82 us -> none  [the longest x3 2.83 us: beside(): jnp.transpose(taken, (1, 0, 2)).reshape(rows, blocks * LANES).astype(f32)]
    ppermute x2, waiting for transfers between devices: 3.62 us -> 7.31 us  [to_sibling(): return lax.ppermute(value, 'core', [(0, 1), (1, 0)])]
  transfers between devices with their start and end apart: 4 -> 3, of which waited for: 3 -> 3; matrix products, arithmetic and copies ran while one was open for 3% -> 1% of each run, Pallas kernels for 0% -> 0%
where the time goes in v2:
time: 176 us
  blocking collectives  89.3 us (51%)
  Pallas kernels  27.6 us (16%)
  waiting for transfers between devices  23 us (13%)
  starting transfers between devices  21.9 us (12%)
  local copies, waits for them, and re-layouts  11.7 us (7%)
    all_to_all x4, blocking collectives, exchange(): return lax.all_to_all(value, axes, 0, 0)  89.3 us
    all_to_all x1, starting transfers between devices, exchange(): return lax.all_to_all(value, axes, 0, 0)  15.7 us
    all_to_all x1, waiting for transfers between devices, exchange(): return lax.all_to_all(value, axes, 0, 0)  15.7 us
    pallas_call x1, Pallas kernels, block(): pl.pallas_call(block_kernel, out_shape=(half, half), in_specs=[SCALAR] +...  13 us
    ppermute x2, waiting for transfers between devices, to_sibling(): return lax.ppermute(value, 'core', [(0, 1), (1, 0)])  7.31 us
    ppermute x2, starting transfers between devices, to_sibling(): return lax.ppermute(value, 'core', [(0, 1), (1, 0)])  6.2 us
    pallas_call x1, Pallas kernels, assemble(): pl.pallas_call(assemble_kernel, out_shape=tuple((jax.ShapeDtypeStruct(s,...  5.61 us
    pallas_call x1, Pallas kernels, merge(): pl.pallas_call(merge_kernel, out_shape=jax.ShapeDtypeStruct((PLACES, GRAD...  3.98 us
  transfers between devices with their start and end apart: 3, of which 3 were waited for; matrix products, arithmetic and copies ran while one was open for 1% of the time, Pallas kernels for 0%

profile of v2, /device:TPU:1, one launch (start us, length us, event | category | flops | bytes accessed | tf_op | source)
XLA Modules:
  0.0 175.8 jit_solution(4202707227181030058)
XLA Ops:
  0.7 1.0 stack.16
  1.7 0.3 copy.24
  2.0 1.0 stack.17
  3.0 0.3 copy.25
  3.3 1.6 pad_maximum_fusion
  5.0 15.7 %all-to-all-start = ((bf16[256,2,384]{2,1,0:T(2,128)(2,1)}), bf16[256,2,384]{2,1,0:T(2,128)(2,1)S(1)}, u32[]{:S(2)}, u32[]{:S(2)}) async-start(bf16[256,2,384]{2,1,0:T(2,128)(2,1)} %bitcast.2), calls=%async_computation | async-start | bytes 786432 | tf_op jit(solution)/shard_map/all_to_all | solution.py:379
  20.7 0.6 reshape.62.gain_attn_ref
  21.2 0.6 reshape.64.gain_mlp_ref
  21.9 0.1 stack.20
  22.1 0.8 copy.28.bias_ref
  22.8 15.7 %all-to-all-done = bf16[256,2,384]{2,1,0:T(2,128)(2,1)S(1)} async-done(((bf16[256,2,384]{2,1,0:T(2,128)(2,1)}), bf16[256,2,384]{2,1,0:T(2,128)(2,1)S(1)}, u32[]{:S(2)}, u32[]{:S(2)}) %all-to-all-start) | async-done | bytes 393248 | tf_op jit(solution)/shard_map/all_to_all | solution.py:379
  38.5 0.5 fusion
  39.0 0.8 copy_bitcast_fusion
  39.8 13.0 %shard_map.160 = (bf16[16,496,128]{2,1,0:T(8,128)(2,1)}, bf16[16,496,128]{2,1,0:T(8,128)(2,1)}) custom-call(s32[1]{0:T(128)} %bitcast.core_ref, bf16[256,384]{1,0:T(8,128)(2,1)} %get-tuple-element.36.x_ref, bf16[256,384]{1,0:T(8,128)(2,1)} %get-tuple-element.35.cot_ref, f32[1,384]{1,0:T(1,128)} %reshape.62.gain_attn_ref, bf16[384,1152]{1,0:T(8,128)(2,1)} %w_qkv_ref.1, ...), custom_call_target="tpu_custom_call" | custom-call | tf_op jit(solution)/shard_map/pallas_call | solution.py:238
  52.8 1.3 collective-permute-start
  54.1 3.9 %collective-permute-done.arrived_ref = bf16[16,496,128]{2,1,0:T(8,128)(2,1)S(1)} collective-permute-done((bf16[16,496,128]{2,1,0:T(8,128)(2,1)}, bf16[16,496,128]{2,1,0:T(8,128)(2,1)S(1)}, u32[]{:S(2)}, u32[]{:S(2)}) %collective-permute-start) | collective-permute-done | bytes 2031648 | tf_op jit(solution)/shard_map/ppermute | solution.py:383
  58.0 1.3 copy-done.1
  59.3 4.0 %shard_map.161 = bf16[16,544,128]{2,1,0:T(8,128)(2,1)} custom-call(s32[1]{0:T(128)} %bitcast.core_ref, bf16[16,496,128]{2,1,0:T(8,128)(2,1)} %get-tuple-element.19.kept_ref, bf16[16,496,128]{2,1,0:T(8,128)(2,1)} %copy-done.1), custom_call_target="tpu_custom_call" | custom-call | tf_op jit(solution)/shard_map/pallas_call | solution.py:267
  63.3 34.1 %all_to_all.25.arrived_ref = bf16[16,544,128]{2,1,0:T(8,128)(2,1)} all-to-all(bf16[16,544,128]{2,1,0:T(8,128)(2,1)} %shard_map.161), channel_id=1, replica_groups=mesh['y_lo'=2,'core'=2,'y_hi'=2,'x'=4,'z'=8] {'y_lo','y_hi','x'}, dimensions={0} | all-to-all | bytes 4456448 | tf_op jit(solution)/shard_map/all_to_all | solution.py:379
  97.5 3.1 %shard_map.162 = bf16[8,256,128]{2,1,0:T(8,128)(2,1)} custom-call(bf16[16,544,128]{2,1,0:T(8,128)(2,1)} %all_to_all.25.arrived_ref), custom_call_target="tpu_custom_call" | custom-call | tf_op jit(solution)/shard_map/pallas_call | solution.py:302
  100.6 19.8 %all_to_all.26.arrived_ref = bf16[8,256,128]{2,1,0:T(8,128)(2,1)} all-to-all(bf16[8,256,128]{2,1,0:T(8,128)(2,1)} %shard_map.162), channel_id=1, replica_groups=mesh['y_lo'=2,'core'=2,'y_hi'=2,'x'=4,'z'=8] {'z'}, dimensions={0} | all-to-all | bytes 1048576 | tf_op jit(solution)/shard_map/all_to_all | solution.py:379
  120.4 1.9 %shard_map.163 = (bf16[8,56,128]{2,1,0:T(8,128)(2,1)}, bf16[256,384]{1,0:T(8,128)(2,1)}, bf16[256,384]{1,0:T(8,128)(2,1)}) custom-call(bf16[8,256,128]{2,1,0:T(8,128)(2,1)} %all_to_all.26.arrived_ref), custom_call_target="tpu_custom_call" | custom-call | tf_op jit(solution)/shard_map/pallas_call | solution.py:323
  122.2 11.0 %all_to_all.27 = bf16[8,56,128]{2,1,0:T(8,128)(2,1)S(1)} all-to-all(bf16[8,56,128]{2,1,0:T(8,128)(2,1)} %get-tuple-element.23), channel_id=1, replica_groups=mesh['y_lo'=2,'core'=2,'y_hi'=2,'x'=4,'z'=8] {'z'}, dimensions={0} | all-to-all | bytes 229376 | tf_op jit(solution)/shard_map/all_to_all | solution.py:379
  133.3 0.3 broadcast_in_dim.7
  133.6 24.3 %all_to_all.28.here_ref = bf16[16,448,128]{2,1,0:T(8,128)(2,1)S(1)} all-to-all(bf16[16,448,128]{2,1,0:T(8,128)(2,1)S(1)} %broadcast_in_dim.7), channel_id=1, replica_groups=mesh['y_lo'=2,'core'=2,'y_hi'=2,'x'=4,'z'=8] {'y_lo','y_hi','x'}, dimensions={0} | all-to-all | bytes 3670016 | tf_op jit(solution)/shard_map/all_to_all | solution.py:379
  157.9 4.9 %collective-permute-start.1 = (bf16[16,448,128]{2,1,0:T(8,128)(2,1)S(1)}, bf16[16,448,128]{2,1,0:T(8,128)(2,1)S(1)}, u32[]{:S(2)}, u32[]{:S(2)}) collective-permute-start(bf16[16,448,128]{2,1,0:T(8,128)(2,1)S(1)} %all_to_all.28.here_ref), channel_id=1, source_target_pairs={{0,64},{64,0},{1,65},{65,1},{2,66},{66,2},{3,67},{67,3},{4,68},{68... | collective-permute-start | bytes 5505032 | tf_op jit(solution)/shard_map/ppermute | solution.py:383
  162.8 3.4 %collective-permute-done.1.other_ref = bf16[16,448,128]{2,1,0:T(8,128)(2,1)S(1)} collective-permute-done((bf16[16,448,128]{2,1,0:T(8,128)(2,1)S(1)}, bf16[16,448,128]{2,1,0:T(8,128)(2,1)S(1)}, u32[]{:S(2)}, u32[]{:S(2)}) %collective-permute-start.1) | collective-permute-done | bytes 1835040 | tf_op jit(solution)/shard_map/ppermute | solution.py:383
  166.3 1.2 copy-done.2
  167.5 5.6 %shard_map.164 = (f32[384,1152]{1,0:T(8,128)}, f32[384,384]{1,0:T(8,128)}, f32[384,1536]{1,0:T(8,128)}, f32[1536,384]{1,0:T(8,128)}, f32[16,128]{1,0:T(8,128)}) custom-call(s32[1]{0:T(128)} %bitcast.core_ref, bf16[16,448,128]{2,1,0:T(8,128)(2,1)} %copy-done, bf16[16,448,128]{2,1,0:T(8,128)(2,1)} %copy-done.2), custom_call_target="tpu_custom_call" | custom-call | tf_op jit(solution)/shard_map/pallas_call | solution.py:368
  173.1 0.7 slice.30
  173.8 1.3 slice_bitcast_fusion
  175.1 0.7 reshape.68
  (14 shorter events, 0.1 us)
Async XLA Ops:
  0.6 20.0 %copy-start.4 = (f32[384]{0:T(512)S(1)}, f32[384]{0:T(512)}, u32[]{:S(2)}) copy-start(f32[384]{0:T(512)} %param.11) | copy-start | bytes 4612
  0.7 20.6 %copy-start.5 = (f32[384]{0:T(512)S(1)}, f32[384]{0:T(512)}, u32[]{:S(2)}) copy-start(f32[384]{0:T(512)} %param.15) | copy-start | bytes 4612
  0.7 21.1 %copy-start.3 = (f32[6,7,7]{2,1,0:T(8,128)S(1)}, f32[6,7,7]{2,1,0:T(8,128)}, u32[]{:S(2)}) copy-start(f32[6,7,7]{2,1,0:T(8,128)} %param.13) | copy-start | bytes 3532
  5.0 33.5 %all-to-all-start = ((bf16[256,2,384]{2,1,0:T(2,128)(2,1)}), bf16[256,2,384]{2,1,0:T(2,128)(2,1)S(1)}, u32[]{:S(2)}, u32[]{:S(2)}) async-start(bf16[256,2,384]{2,1,0:T(2,128)(2,1)} %bitcast.2), calls=%async_computation | async-start | bytes 786432 | tf_op jit(solution)/shard_map/all_to_all | solution.py:379
  52.8 5.2 %collective-permute-start = (bf16[16,496,128]{2,1,0:T(8,128)(2,1)}, bf16[16,496,128]{2,1,0:T(8,128)(2,1)S(1)}, u32[]{:S(2)}, u32[]{:S(2)}) collective-permute-start(bf16[16,496,128]{2,1,0:T(8,128)(2,1)} %get-tuple-element.20), channel_id=1, source_target_pairs={{0,64},{64,0},{1,65},{65,1},{2,66},{66,2},{3,67},{67,3},{4,68},{68... | collective-permute-start | bytes 6094856 | tf_op jit(solution)/shard_map/ppermute | solution.py:383
  58.0 1.3 copy-start.1
  157.9 8.3 %copy-start = (bf16[16,448,128]{2,1,0:T(8,128)(2,1)}, bf16[16,448,128]{2,1,0:T(8,128)(2,1)S(1)}, u32[]{:S(2)}) copy-start(bf16[16,448,128]{2,1,0:T(8,128)(2,1)S(1)} %all_to_all.28.here_ref) | copy-start | bytes 5505028
  157.9 8.3 %collective-permute-start.1 = (bf16[16,448,128]{2,1,0:T(8,128)(2,1)S(1)}, bf16[16,448,128]{2,1,0:T(8,128)(2,1)S(1)}, u32[]{:S(2)}, u32[]{:S(2)}) collective-permute-start(bf16[16,448,128]{2,1,0:T(8,128)(2,1)S(1)} %all_to_all.28.here_ref), channel_id=1, source_target_pairs={{0,64},{64,0},{1,65},{65,1},{2,66},{66,2},{3,67},{67,3},{4,68},{68... | collective-permute-start | bytes 5505032 | tf_op jit(solution)/shard_map/ppermute | solution.py:383
  166.3 1.2 copy-start.2

commit v3 on v2

--- a/solution.py
+++ b/solution.py
@@ -118,7 +118,7 @@
             )
             score = dot_nt(one_head(query, second), key) * SCALE + bias
             weight = jnp.exp(score)
-            prob = weight / jnp.sum(weight, -1, keepdims=True)
+            prob = weight * (1.0 / jnp.sum(weight, -1, keepdims=True))
             prob_b = prob.astype(bf16)
             probs.append(prob)
             probs_b.append(prob_b)
@@ -223,27 +223,38 @@
     sent_ref[...] = halves_ref[1 - core]
 
 
-def params():
-    return pltpu.CompilerParams(vmem_limit_bytes=56 * 1024 * 1024)
-
-
 SCALAR = pl.BlockSpec(memory_space=pltpu.SMEM)
 WHOLE = pl.BlockSpec(memory_space=pltpu.VMEM)
+
+
+def call(kernel, outs, operands, interpret, room=16, scalars=0, scratch=()):
+    shapes = tuple((pltpu.VMEM if near and not interpret else jax.ShapeDtypeStruct)(s, t) for s, t, near in outs)
+    if not interpret:
+        operands = operands[:scalars] + tuple(pltpu.with_memory_space_constraint(o, pltpu.VMEM) for o in operands[scalars:])
+    return pl.pallas_call(
+        kernel,
+        out_shape=shapes,
+        in_specs=[SCALAR] * scalars + [WHOLE] * (len(operands) - scalars),
+        out_specs=(WHOLE,) * len(outs),
+        scratch_shapes=scratch,
+        compiler_params=pltpu.CompilerParams(vmem_limit_bytes=room * 1024 * 1024),
+        interpret=interpret,
+    )(*operands)
 
 
 def block(core, x, cot, gain_attn, w_qkv, rel_bias, w_out, gain_mlp, w_fc1, w_fc2, interpret=False):
     sides = jnp.stack([rel_bias[:, :6], rel_bias[:, 1:]], -1).reshape(HEADS * 42, 2)
     bias_rows = jnp.repeat(sides, SECTORS, 1)
-    half = jax.ShapeDtypeStruct((PLACES, GRADS + OWN, LANES), bf16)
-    return pl.pallas_call(
+    half = (PLACES, GRADS + OWN, LANES)
+    return call(
         block_kernel,
-        out_shape=(half, half),
-        in_specs=[SCALAR] + [WHOLE] * 9,
-        out_specs=(WHOLE, WHOLE),
-        scratch_shapes=[pltpu.VMEM((2, PLACES, GRADS + OWN, LANES), bf16)],
-        compiler_params=params(),
-        interpret=interpret,
-    )(core, x, cot, gain_attn.reshape(1, D), w_qkv, bias_rows, w_out, gain_mlp.reshape(1, D), w_fc1, w_fc2)
+        ((half, bf16, True), (half, bf16, True)),
+        (core, x, cot, gain_attn.reshape(1, D), w_qkv, bias_rows, w_out, gain_mlp.reshape(1, D), w_fc1, w_fc2),
+        interpret,
+        room=32,
+        scalars=1,
+        scratch=[pltpu.VMEM((2, *half), bf16)],
+    )
 
 
 def merge_kernel(core_ref, kept_ref, arrived_ref, out_ref):
@@ -264,14 +275,8 @@
 
 
 def merge(core, kept, arrived, interpret=False):
-    return pl.pallas_call(
-        merge_kernel,
-        out_shape=jax.ShapeDtypeStruct((PLACES, GRADS + 2 * OWN, LANES), bf16),
-        in_specs=[SCALAR, WHOLE, WHOLE],
-        out_specs=WHOLE,
-        compiler_params=params(),
-        interpret=interpret,
-    )(core, kept, arrived)
+    out = ((PLACES, GRADS + 2 * OWN, LANES), bf16, True)
+    return call(merge_kernel, (out,), (core, kept, arrived), interpret, scalars=1)[0]
 
 
 def plane_kernel(arrived_ref, out_ref):
@@ -299,38 +304,28 @@
 
 
 def plane(arrived, interpret=False):
-    return pl.pallas_call(
-        plane_kernel,
-        out_shape=jax.ShapeDtypeStruct((DEPTH, PART_ROOM + 192, LANES), bf16),
-        in_specs=[WHOLE],
-        out_specs=WHOLE,
-        compiler_params=params(),
-        interpret=interpret,
-    )(arrived)
+    return call(plane_kernel, (((DEPTH, PART_ROOM + 192, LANES), bf16, True),), (arrived,), interpret)[0]
 
 
 def depth_kernel(arrived_ref, part_ref, output_ref, d_latent_ref):
     total = jnp.sum(arrived_ref[:, :PART_ROOM, :].astype(f32), 0)[:PART]
     part_ref[...] = jnp.broadcast_to(total[None], (DEPTH, PART, LANES)).astype(bf16)
+    to = lax.broadcasted_iota(jnp.int32, (CELLS, CELLS), 0)
+    source = ((to & 7) << 5) | ((to >> 7) << 4) | (((to >> 3) & 7) << 1) | ((to >> 6) & 1)
+    chosen = jnp.where(lax.broadcasted_iota(jnp.int32, (CELLS, CELLS), 1) == source, 1.0, 0.0).astype(bf16)
     for array, ref in enumerate((output_ref, d_latent_ref)):
-        for block in range(3):
-            at = PART_ROOM + (array * 3 + block) * 32
-            ref[:, block * LANES : (block + 1) * LANES] = arrived_ref[:, at : at + 32, :].reshape(CELLS, LANES)
+        starts = [PART_ROOM + (array * 3 + block) * 32 for block in range(3)]
+        rows = jnp.concatenate([arrived_ref[:, at : at + 32, :].reshape(CELLS, LANES) for at in starts], 1)
+        ref[...] = dot(chosen, rows).astype(bf16)
 
 
 def depth(arrived, interpret=False):
-    cells = jax.ShapeDtypeStruct((CELLS, D), bf16)
-    return pl.pallas_call(
-        depth_kernel,
-        out_shape=(jax.ShapeDtypeStruct((DEPTH, PART, LANES), bf16), cells, cells),
-        in_specs=[WHOLE],
-        out_specs=(WHOLE, WHOLE, WHOLE),
-        compiler_params=params(),
-        interpret=interpret,
-    )(arrived)
-
-
-def assemble_kernel(core_ref, here_ref, other_ref, d_qkv_ref, d_out_ref, d_fc1_ref, d_fc2_ref, small_ref):
+    cells = ((CELLS, D), bf16, False)
+    return call(depth_kernel, (((DEPTH, PART, LANES), bf16, True), cells, cells), (arrived,), interpret)
+
+
+def assemble_kernel(core_ref, here_ref, other_ref, d_qkv_ref, d_out_ref, d_fc1_ref, d_fc2_ref,
+                    d_rel_ref, d_gain_attn_ref, d_gain_mlp_ref):
     def columns(half, at, block, rows):
         first = at + block // 2 * rows
         start = block % 2 * 8
@@ -352,7 +347,12 @@
                 d_qkv_ref[:, lanes(block)] = columns(second, OUT_AT, block - QKV_FIRST + 3, 48)
         for block in range(3):
             d_out_ref[:, lanes(block)] = columns(second, OUT_AT, block, 48)
-        small_ref[...] = first[0, SMALL_AT:GRADS, :].astype(f32)
+        small = first[0, SMALL_AT:GRADS, :].astype(f32)
+        for step in range(7):
+            d_rel_ref[:, step, :] = pltpu.roll(small, (LANES - 7 * step) % LANES, 1)[:HEADS, :7]
+        for block in range(3):
+            d_gain_attn_ref[lanes(block)] = small[8 + block]
+            d_gain_mlp_ref[lanes(block)] = small[11 + block]
 
     @pl.when(core_ref[0] == 0)
     def _():
@@ -364,15 +364,8 @@
 
 
 def assemble(core, here, other, interpret=False):
-    shapes = ((D, 3 * D), (D, D), (D, FF), (FF, D), (16, LANES))
-    return pl.pallas_call(
-        assemble_kernel,
-        out_shape=tuple(jax.ShapeDtypeStruct(s, f32) for s in shapes),
-        in_specs=[SCALAR, WHOLE, WHOLE],
-        out_specs=(WHOLE,) * 5,
-        compiler_params=params(),
-        interpret=interpret,
-    )(core, here, other)
+    shapes = ((D, 3 * D), (D, D), (D, FF), (FF, D), (HEADS, 7, 7), (D,), (D,))
+    return call(assemble_kernel, tuple((s, f32, False) for s in shapes), (core, here, other), interpret, scalars=1)
 
 
 def exchange(value, axes):
@@ -386,18 +379,13 @@
 def per_device(latent, cotangent, gain_attn, w_qkv, rel_bias, w_out, gain_mlp, w_fc1, w_fc2):
     shape = latent.shape
     core = lax.axis_index("core").reshape(1)
-    both = jnp.stack([latent.reshape(CELLS, D), cotangent.reshape(CELLS, D)], 1).reshape(DEPTH, 2, 2, 4, 2, 2, D)
-    sent = jnp.transpose(both, (1, 4, 2, 3, 0, 5, 6)).reshape(CELLS, 2, D)
-    arrived = exchange(sent, AXES)
+    arrived = exchange(jnp.stack([latent.reshape(CELLS, D), cotangent.reshape(CELLS, D)], 1), AXES)
     kept, sent = block(core, arrived[:, 0], arrived[:, 1], gain_attn, w_qkv, rel_bias, w_out, gain_mlp, w_fc1, w_fc2)
     merged = merge(core, kept, to_sibling(sent))
     part, output, d_latent = depth(exchange(plane(exchange(merged, PLANE)), "z"))
     piece = exchange(part, "z").reshape(GRADS, LANES)
     here = exchange(jnp.broadcast_to(piece, (PLACES, GRADS, LANES)), PLANE)
-    d_qkv, d_out, d_fc1, d_fc2, small = assemble(core, here, to_sibling(here))
-    d_rel = small[:HEADS, :49].reshape(HEADS, 7, 7)
-    gains = small[8:14].reshape(2, D)
-    return output.reshape(shape), d_latent.reshape(shape), d_qkv, d_out, d_fc1, d_fc2, d_rel, gains[0], gains[1]
+    return (output.reshape(shape), d_latent.reshape(shape)) + assemble(core, here, to_sibling(here))
 
 
 def solution(mesh):

time: 176 us -> 152 us (0.86)
  Pallas kernels: 27.6 us -> 14.7 us
  local copies, waits for them, and re-layouts: 11.7 us -> 3.74 us
  blocking collectives: 89.3 us -> 85.2 us
    pallas_call x5, Pallas kernels: 27.6 us -> 14.7 us  [call(): pl.pallas_call(kernel, out_shape=shapes, in_specs=[SCALAR] * scalars + [W...]
    all_to_all x4, blocking collectives: 89.3 us -> 85.2 us  [exchange(): return lax.all_to_all(value, axes, 0, 0)]
    unnamed x12 -> x14, local copies, waits for them, and re-layouts: 2.56 us -> 0.03 us
  transfers between devices with their start and end apart: 3 -> 3, of which waited for: 3 -> 3; matrix products, arithmetic and copies ran while one was open for 1% -> 0% of each run, Pallas kernels for 0% -> 0%
where the time goes in v3:
time: 152 us
  blocking collectives  85.2 us (56%)
  waiting for transfers between devices  23.7 us (16%)
  starting transfers between devices  22.9 us (15%)
  Pallas kernels  14.7 us (10%)
  local copies, waits for them, and re-layouts  3.74 us (2%)
    all_to_all x4, blocking collectives, exchange(): return lax.all_to_all(value, axes, 0, 0)  85.2 us
    all_to_all x1, waiting for transfers between devices, exchange(): return lax.all_to_all(value, axes, 0, 0)  16.6 us
    all_to_all x1, starting transfers between devices, exchange(): return lax.all_to_all(value, axes, 0, 0)  16.5 us
    pallas_call x5, Pallas kernels, call(): pl.pallas_call(kernel, out_shape=shapes, in_specs=[SCALAR] * scalars + [W...  14.7 us
    ppermute x2, waiting for transfers between devices, to_sibling(): return lax.ppermute(value, 'core', [(0, 1), (1, 0)])  7.1 us
    ppermute x2, starting transfers between devices, to_sibling(): return lax.ppermute(value, 'core', [(0, 1), (1, 0)])  6.38 us
  transfers between devices with their start and end apart: 3, of which 3 were waited for; matrix products, arithmetic and copies ran while one was open for 0% of the time, Pallas kernels for 0%

profile of v3, /device:TPU:1, one launch (start us, length us, event | category | flops | bytes accessed | tf_op | source)
XLA Modules:
  0.0 152.2 jit_solution(17147135388282011825)
XLA Ops:
  0.6 0.0 copy-start.5
  0.7 0.0 copy-start.6
  0.7 0.0 copy-start.4
  0.7 1.1 pad_maximum_fusion
  1.8 1.2 copy.23
  2.9 16.5 %all-to-all-start = ((bf16[256,2,384]{2,1,0:T(2,128)(2,1)}), bf16[256,2,384]{2,1,0:T(2,128)(2,1)}, u32[]{:S(2)}, u32[]{:S(2)}) async-start(bf16[256,2,384]{2,1,0:T(2,128)(2,1)} %copy.23), calls=%async_computation | async-start | bytes 786432 | tf_op jit(solution)/shard_map/all_to_all | solution.py:372
  19.5 0.0 copy-done.5
  19.5 0.0 copy-done.6
  19.5 0.0 copy-done.4
  19.5 0.1 stack.13
  19.6 0.1 stack.14
  19.8 0.1 copy.26.bias_ref
  19.9 16.6 %all-to-all-done = bf16[256,2,384]{2,1,0:T(2,128)(2,1)} async-done(((bf16[256,2,384]{2,1,0:T(2,128)(2,1)}), bf16[256,2,384]{2,1,0:T(2,128)(2,1)}, u32[]{:S(2)}, u32[]{:S(2)}) %all-to-all-start) | async-done | bytes 393248 | tf_op jit(solution)/shard_map/all_to_all | solution.py:372
  36.5 1.8 %fusion = (bf16[256,1,384]{2,1,0:T(2,128)(2,1)S(1)}, bf16[256,1,384]{2,1,0:T(2,128)(2,1)S(1)}) fusion(bf16[256,2,384]{2,1,0:T(2,128)(2,1)} %all-to-all-done), kind=kLoop, calls=%fused_computation.4 | loop fusion | bytes 786432 | tf_op jit(solution)/shard_map/slice | solution.py:383
  38.3 0.1 copy_bitcast_fusion
  38.4 0.0 copy-done
  38.4 0.0 copy-done.1
  38.4 0.0 copy-done.2
  38.4 9.0 %shard_map.160 = (bf16[16,496,128]{2,1,0:T(8,128)(2,1)S(1)}, bf16[16,496,128]{2,1,0:T(8,128)(2,1)S(1)}) custom-call(s32[1]{0:T(128)} %bitcast.core_ref, bf16[256,384]{1,0:T(8,128)(2,1)S(1)} %get-tuple-element.38.x_ref, bf16[256,384]{1,0:T(8,128)(2,1)S(1)} %get-tuple-element.37.cot_ref, f32[1,384]{1,0:T(1,128)S(1)} %reshape.45.gain_attn_ref, ...), custom_call_target="tpu_custom_call" | custom-call | tf_op jit(solution)/shard_map/pallas_call | solution.py:234
  47.4 1.6 %collective-permute-start = (bf16[16,496,128]{2,1,0:T(8,128)(2,1)S(1)}, bf16[16,496,128]{2,1,0:T(8,128)(2,1)S(1)}, u32[]{:S(2)}, u32[]{:S(2)}) collective-permute-start(bf16[16,496,128]{2,1,0:T(8,128)(2,1)S(1)} %get-tuple-element.22), channel_id=1, source_target_pairs={{0,64},{64,0},{1,65},{65,1},{2,66},{66,2},{3,67},{67,3},{4,68},{68... | collective-permute-start | bytes 6094856 | tf_op jit(solution)/shard_map/ppermute | solution.py:376
  49.0 3.7 %collective-permute-done.arrived_ref = bf16[16,496,128]{2,1,0:T(8,128)(2,1)S(1)} collective-permute-done((bf16[16,496,128]{2,1,0:T(8,128)(2,1)S(1)}, bf16[16,496,128]{2,1,0:T(8,128)(2,1)S(1)}, u32[]{:S(2)}, u32[]{:S(2)}) %collective-permute-start) | collective-permute-done | bytes 2031648 | tf_op jit(solution)/shard_map/ppermute | solution.py:376
  52.7 0.4 shard_map.161
  53.2 32.0 %all_to_all.25.arrived_ref = bf16[16,544,128]{2,1,0:T(8,128)(2,1)S(1)} all-to-all(bf16[16,544,128]{2,1,0:T(8,128)(2,1)S(1)} %shard_map.161), channel_id=1, replica_groups=mesh['y_lo'=2,'core'=2,'y_hi'=2,'x'=4,'z'=8] {'y_lo','y_hi','x'}, dimensions={0} | all-to-all | bytes 4456448 | tf_op jit(solution)/shard_map/all_to_all | solution.py:372
  85.2 0.7 shard_map.162
  85.9 17.2 %all_to_all.26.arrived_ref = bf16[8,256,128]{2,1,0:T(8,128)(2,1)S(1)} all-to-all(bf16[8,256,128]{2,1,0:T(8,128)(2,1)S(1)} %shard_map.162), channel_id=1, replica_groups=mesh['y_lo'=2,'core'=2,'y_hi'=2,'x'=4,'z'=8] {'z'}, dimensions={0} | all-to-all | bytes 1048576 | tf_op jit(solution)/shard_map/all_to_all | solution.py:372
  103.1 1.0 shard_map.163
  104.1 11.0 %all_to_all.27 = bf16[8,56,128]{2,1,0:T(8,128)(2,1)S(1)} all-to-all(bf16[8,56,128]{2,1,0:T(8,128)(2,1)S(1)} %get-tuple-element.25), channel_id=1, replica_groups=mesh['y_lo'=2,'core'=2,'y_hi'=2,'x'=4,'z'=8] {'z'}, dimensions={0} | all-to-all | bytes 229376 | tf_op jit(solution)/shard_map/all_to_all | solution.py:372
  115.1 0.3 broadcast_in_dim.7
  115.5 24.9 %all_to_all.28.here_ref = bf16[16,448,128]{2,1,0:T(8,128)(2,1)S(1)} all-to-all(bf16[16,448,128]{2,1,0:T(8,128)(2,1)S(1)} %broadcast_in_dim.7), channel_id=1, replica_groups=mesh['y_lo'=2,'core'=2,'y_hi'=2,'x'=4,'z'=8] {'y_lo','y_hi','x'}, dimensions={0} | all-to-all | bytes 3670016 | tf_op jit(solution)/shard_map/all_to_all | solution.py:372
  140.4 4.8 %collective-permute-start.1 = (bf16[16,448,128]{2,1,0:T(8,128)(2,1)S(1)}, bf16[16,448,128]{2,1,0:T(8,128)(2,1)S(1)}, u32[]{:S(2)}, u32[]{:S(2)}) collective-permute-start(bf16[16,448,128]{2,1,0:T(8,128)(2,1)S(1)} %all_to_all.28.here_ref), channel_id=1, source_target_pairs={{0,64},{64,0},{1,65},{65,1},{2,66},{66,2},{3,67},{67,3},{4,68},{68... | collective-permute-start | bytes 5505032 | tf_op jit(solution)/shard_map/ppermute | solution.py:376
  145.2 3.4 %collective-permute-done.1.other_ref = bf16[16,448,128]{2,1,0:T(8,128)(2,1)S(1)} collective-permute-done((bf16[16,448,128]{2,1,0:T(8,128)(2,1)S(1)}, bf16[16,448,128]{2,1,0:T(8,128)(2,1)S(1)}, u32[]{:S(2)}, u32[]{:S(2)}) %collective-permute-start.1) | collective-permute-done | bytes 1835040 | tf_op jit(solution)/shard_map/ppermute | solution.py:376
  148.6 3.6 %shard_map.164 = (f32[384,1152]{1,0:T(8,128)}, f32[384,384]{1,0:T(8,128)}, f32[384,1536]{1,0:T(8,128)}, f32[1536,384]{1,0:T(8,128)}, f32[6,7,7]{2,1,0:T(8,128)}, /*index=5*/f32[384]{0:T(512)}, f32[384]{0:T(512)}) custom-call(s32[1]{0:T(128)} %bitcast.core_ref, bf16[16,448,128]{2,1,0:T(8,128)(2,1)S(1)} %all_to_all.28.here_ref, ...), custom_call_target="tpu_custom_call" | custom-call | tf_op jit(solution)/shard_map/pallas_call | solution.py:234
  (10 shorter events, 0.0 us)
Async XLA Ops:
  0.6 18.8 %copy-start.5 = (f32[384]{0:T(512)S(1)}, f32[384]{0:T(512)}, u32[]{:S(2)}) copy-start(f32[384]{0:T(512)} %param.11) | copy-start | bytes 4612
  0.7 18.8 %copy-start.6 = (f32[384]{0:T(512)S(1)}, f32[384]{0:T(512)}, u32[]{:S(2)}) copy-start(f32[384]{0:T(512)} %param.15) | copy-start | bytes 4612
  0.7 18.8 %copy-start.4 = (f32[6,7,7]{2,1,0:T(8,128)S(1)}, f32[6,7,7]{2,1,0:T(8,128)}, u32[]{:S(2)}) copy-start(f32[6,7,7]{2,1,0:T(8,128)} %param.13) | copy-start | bytes 3532
  2.9 35.5 %copy-start = (bf16[384,1536]{1,0:T(8,128)(2,1)S(1)}, bf16[384,1536]{1,0:T(8,128)(2,1)}, u32[]{:S(2)}) copy-start(bf16[384,1536]{1,0:T(8,128)(2,1)} %w_fc1_ref.1) | copy-start | bytes 3538948
  2.9 35.5 %copy-start.1 = (bf16[1536,384]{1,0:T(8,128)(2,1)S(1)}, bf16[1536,384]{1,0:T(8,128)(2,1)}, u32[]{:S(2)}) copy-start(bf16[1536,384]{1,0:T(8,128)(2,1)} %w_fc2_ref.1) | copy-start | bytes 3538948
  2.9 35.5 %copy-start.2 = (bf16[384,1152]{1,0:T(8,128)(2,1)S(1)}, bf16[384,1152]{1,0:T(8,128)(2,1)}, u32[]{:S(2)}) copy-start(bf16[384,1152]{1,0:T(8,128)(2,1)} %w_qkv_ref.1) | copy-start | bytes 2654212
  2.9 33.6 %all-to-all-start = ((bf16[256,2,384]{2,1,0:T(2,128)(2,1)}), bf16[256,2,384]{2,1,0:T(2,128)(2,1)}, u32[]{:S(2)}, u32[]{:S(2)}) async-start(bf16[256,2,384]{2,1,0:T(2,128)(2,1)} %copy.23), calls=%async_computation | async-start | bytes 786432 | tf_op jit(solution)/shard_map/all_to_all | solution.py:372
  36.5 1.9 %copy-start.3 = (bf16[384,384]{1,0:T(8,128)(2,1)S(1)}, bf16[384,384]{1,0:T(8,128)(2,1)}, u32[]{:S(2)}) copy-start(bf16[384,384]{1,0:T(8,128)(2,1)} %w_out_ref.1) | copy-start | bytes 884740
  47.4 5.3 %collective-permute-start = (bf16[16,496,128]{2,1,0:T(8,128)(2,1)S(1)}, bf16[16,496,128]{2,1,0:T(8,128)(2,1)S(1)}, u32[]{:S(2)}, u32[]{:S(2)}) collective-permute-start(bf16[16,496,128]{2,1,0:T(8,128)(2,1)S(1)} %get-tuple-element.22), channel_id=1, source_target_pairs={{0,64},{64,0},{1,65},{65,1},{2,66},{66,2},{3,67},{67,3},{4,68},{68... | collective-permute-start | bytes 6094856 | tf_op jit(solution)/shard_map/ppermute | solution.py:376
  140.4 8.2 %collective-permute-start.1 = (bf16[16,448,128]{2,1,0:T(8,128)(2,1)S(1)}, bf16[16,448,128]{2,1,0:T(8,128)(2,1)S(1)}, u32[]{:S(2)}, u32[]{:S(2)}) collective-permute-start(bf16[16,448,128]{2,1,0:T(8,128)(2,1)S(1)} %all_to_all.28.here_ref), channel_id=1, source_target_pairs={{0,64},{64,0},{1,65},{65,1},{2,66},{66,2},{3,67},{67,3},{4,68},{68... | collective-permute-start | bytes 5505032 | tf_op jit(solution)/shard_map/ppermute | solution.py:376

commit v4 on v3

--- a/solution.py
+++ b/solution.py
@@ -78,10 +78,61 @@
         ref[half, start : start + 8, first : first + rows, :] = here.astype(bf16)
 
 
-def block_kernel(core_ref, x_ref, cot_ref, gain_attn_ref, w_qkv_ref, bias_ref, w_out_ref, gain_mlp_ref, w_fc1_ref, w_fc2_ref,
-                 kept_ref, sent_ref, halves_ref):
-    x = x_ref[...].astype(f32)
-    gain_attn = gain_attn_ref[...]
+def bits(number, low, count):
+    return (number >> low) & ((1 << count) - 1)
+
+
+def reorder(rows, source):
+    count = rows.shape[0]
+    to = lax.broadcasted_iota(jnp.int32, (count, count), 0)
+    chosen = jnp.where(lax.broadcasted_iota(jnp.int32, (count, count), 1) == source(to), 1.0, 0.0).astype(bf16)
+    return dot(chosen, rows)
+
+
+def pack_kernel(latent_ref, cot_ref, out_ref):
+    for start in range(0, CELLS, 128):
+        parts = [ref[start // 16 : start // 16 + 8].reshape(128, D) for ref in (latent_ref, cot_ref)]
+        rows = reorder(jnp.concatenate(parts, 0), lambda to: bits(to, 0, 1) << 7 | to >> 1)
+        out_ref[start : start + 128] = rows.astype(bf16).reshape(128, 2, D)
+
+
+def pack(latent, cot, interpret=False):
+    return call(pack_kernel, (((CELLS, 2, D), bf16, True),), (latent, cot), interpret, near=False)[0]
+
+
+def fetch_kernel(*refs):
+    count = len(refs) // 2
+    sems = refs[-1]
+    copies = [pltpu.make_async_copy(refs[i], refs[count + i], sems.at[i]) for i in range(count)]
+    for copy in copies:
+        copy.start()
+    for copy in copies:
+        copy.wait()
+
+
+def fetch(*arrays):
+    return pl.pallas_call(
+        fetch_kernel,
+        out_shape=tuple(pltpu.VMEM(a.shape, a.dtype) for a in arrays),
+        in_specs=[pl.BlockSpec(memory_space=pltpu.HBM)] * len(arrays),
+        out_specs=(WHOLE,) * len(arrays),
+        scratch_shapes=[pltpu.SemaphoreType.DMA((len(arrays),))],
+        compiler_params=pltpu.CompilerParams(vmem_limit_bytes=1024 * 1024),
+    )(*(pltpu.with_memory_space_constraint(a, pltpu.HBM) for a in arrays))
+
+
+def gain_row(ref):
+    return jnp.concatenate([ref[lanes(block)].reshape(1, LANES) for block in range(3)], 1)
+
+
+def block_kernel(core_ref, both_ref, gain_attn_ref, w_qkv_ref, bias_ref, w_out_ref, gain_mlp_ref, w_fc1_ref, w_fc2_far_ref,
+                 kept_ref, sent_ref, halves_ref, w_fc2_ref, sem):
+    w_fc2_copy = pltpu.make_async_copy(w_fc2_far_ref, w_fc2_ref, sem)
+    w_fc2_copy.start()
+    groups = [both_ref[start : start + 128].reshape(256, D) for start in range(0, CELLS, 128)]
+    groups = [reorder(group, lambda to: bits(to, 0, 7) << 1 | to >> 7) for group in groups]
+    x = jnp.concatenate([group[:128] for group in groups], 0)
+    gain_attn = gain_row(gain_attn_ref)
     unit, inverse = norm(x)
     normed = (unit * gain_attn).astype(bf16)
     projected = dot(normed, w_qkv_ref[...]).astype(bf16)
@@ -93,6 +144,13 @@
         - lax.broadcasted_iota(jnp.int32, (SECTORS, LANES), 0)
     ) & (SECTORS - 1)
 
+    same = lax.broadcasted_iota(jnp.int32, (7, 7), 0) == lax.broadcasted_iota(jnp.int32, (7, 7), 1)
+    bias_rows = []
+    for head in range(HEADS):
+        table = bias_ref[head]
+        columns = [jnp.sum(jnp.where(same, table[band : band + 1], 0.0), 1, keepdims=True) for band in range(7)]
+        bias_rows.append([jnp.where(low, columns[first], columns[first + 1]) for first in range(6)])
+
     def one_head(pair, second):
         return jnp.where(low, jnp.bfloat16(0), pair) if second else jnp.where(low, pair, jnp.bfloat16(0))
 
@@ -103,6 +161,7 @@
     probs, probs_b, mixed = [], [], []
     for pair in range(HEADS // 2):
         query, key, value = (pair_of(projected, part, pair) for part in range(3))
+        query = query * jnp.bfloat16(SCALE)
         total = None
         for second in range(2):
             head = 2 * pair + second
@@ -110,13 +169,13 @@
             for first in range(6):
                 tile = jnp.full((SECTORS, LANES), ABSENT, f32)
                 for step in range(7):
-                    row = bias_ref[(head * 6 + first) * 7 + step : (head * 6 + first) * 7 + step + 1, :]
+                    row = bias_rows[head][first][step : step + 1]
                     tile = jnp.where(apart == (step - 3) % SECTORS, row, tile)
                 tiles.append(tile)
             bias = jnp.concatenate(
                 [jnp.concatenate([tiles[2 * side - band + 3] for band in range(BANDS)], 0) for side in range(2)], 1
             )
-            score = dot_nt(one_head(query, second), key) * SCALE + bias
+            score = dot_nt(one_head(query, second), key) + bias
             weight = jnp.exp(score)
             prob = weight * (1.0 / jnp.sum(weight, -1, keepdims=True))
             prob_b = prob.astype(bf16)
@@ -128,15 +187,16 @@
     mixed = jnp.concatenate(mixed, 1)
 
     resid = x + dot(mixed, w_out_ref[...])
-    gain_mlp = gain_mlp_ref[...]
+    gain_mlp = gain_row(gain_mlp_ref)
     unit_two, inverse_two = norm(resid)
     normed_two = (unit_two * gain_mlp).astype(bf16)
     hidden = dot(normed_two, w_fc1_ref[...])
     active, slope = gelu_and_slope(hidden)
     active = active.astype(bf16)
+    w_fc2_copy.wait()
     output = resid + dot(active, w_fc2_ref[...])
 
-    cot = cot_ref[...]
+    cot = jnp.concatenate([group[128:] for group in groups], 0).astype(bf16)
     d_fc2 = dot_tn(active, cot)
     for block in range(3):
         here = d_fc2[:, block * LANES : (block + 1) * LANES].reshape(PLACES, FF // PLACES, LANES)
@@ -154,6 +214,7 @@
     rel_rows = []
     for pair in range(HEADS // 2):
         query, key, value = (pair_of(projected, part, pair) for part in range(3))
+        query = query * jnp.bfloat16(SCALE)
         d_mixed_pair = pair_of(d_mixed, 0, pair)
         d_query = d_key = d_value = None
         for second in range(2):
@@ -177,14 +238,8 @@
             taps = jnp.concatenate([jnp.where(low, sums, 0.0), none], 0) + jnp.concatenate(
                 [none, jnp.where(low, 0.0, sums)], 0
             )
-            taps = jnp.concatenate([taps, jnp.zeros((LANES - 49, LANES), f32)], 0)
-            rel_rows.append(
-                lax.dot_general(
-                    jnp.ones((8, LANES), f32), taps, (((1,), (1,)), ((), ())),
-                    precision=lax.Precision.HIGHEST, preferred_element_type=f32,
-                )[:1]
-            )
-            d_score_b = (d_score * SCALE).astype(bf16)
+            rel_rows.append(jnp.concatenate([taps, jnp.zeros((LANES - 49, LANES), f32)], 0))
+            d_score_b = d_score.astype(bf16)
             parts = (
                 dot(d_score_b, one_head(key, second)),
                 dot_tn(d_score_b, one_head(query, second)),
@@ -194,7 +249,7 @@
                 d_query, d_key, d_value = parts
             else:
                 d_query, d_key, d_value = d_query + parts[0], d_key + parts[1], d_value + parts[2]
-        d_queries.append(d_query.astype(bf16))
+        d_queries.append((d_query * SCALE).astype(bf16))
         d_keys.append(d_key.astype(bf16))
         d_values_.append(d_value.astype(bf16))
     d_proj = jnp.concatenate(d_queries + d_keys + d_values_, 1)
@@ -206,6 +261,11 @@
     d_latent = d_resid + d_flat
 
     gains = [g[:, k * LANES : (k + 1) * LANES] for g in (d_gain_attn, d_gain_mlp) for k in range(3)]
+    rel = lax.dot_general(
+        jnp.ones((8, LANES), f32), jnp.concatenate(rel_rows, 0), (((1,), (1,)), ((), ())),
+        precision=lax.Precision.HIGHEST, preferred_element_type=f32,
+    )
+    rel_rows = [rel[:1, head * LANES : (head + 1) * LANES] for head in range(HEADS)]
     small = jnp.concatenate(rel_rows + [jnp.zeros((2, LANES), f32)] + gains + [jnp.zeros((2, LANES), f32)], 0)
     halves_ref[0, 0, SMALL_AT:GRADS, :] = small.astype(bf16)
     halves_ref[0, 1:, SMALL_AT:GRADS, :] = jnp.zeros((PLACES - 1, GRADS - SMALL_AT, LANES), bf16)
@@ -227,14 +287,16 @@
 WHOLE = pl.BlockSpec(memory_space=pltpu.VMEM)
 
 
-def call(kernel, outs, operands, interpret, room=16, scalars=0, scratch=()):
+def call(kernel, outs, operands, interpret, room=16, scalars=0, scratch=(), near=True, loose=0):
+    tight = len(operands) - loose
     shapes = tuple((pltpu.VMEM if near and not interpret else jax.ShapeDtypeStruct)(s, t) for s, t, near in outs)
     if not interpret:
-        operands = operands[:scalars] + tuple(pltpu.with_memory_space_constraint(o, pltpu.VMEM) for o in operands[scalars:])
+        places = [pltpu.VMEM if near else pltpu.HBM] * (tight - scalars) + [pltpu.HBM] * loose
+        operands = operands[:scalars] + tuple(map(pltpu.with_memory_space_constraint, operands[scalars:], places))
     return pl.pallas_call(
         kernel,
         out_shape=shapes,
-        in_specs=[SCALAR] * scalars + [WHOLE] * (len(operands) - scalars),
+        in_specs=[SCALAR] * scalars + [WHOLE] * (tight - scalars) + [pl.BlockSpec(memory_space=pltpu.HBM)] * loose,
         out_specs=(WHOLE,) * len(outs),
         scratch_shapes=scratch,
         compiler_params=pltpu.CompilerParams(vmem_limit_bytes=room * 1024 * 1024),
@@ -242,18 +304,17 @@
     )(*operands)
 
 
-def block(core, x, cot, gain_attn, w_qkv, rel_bias, w_out, gain_mlp, w_fc1, w_fc2, interpret=False):
-    sides = jnp.stack([rel_bias[:, :6], rel_bias[:, 1:]], -1).reshape(HEADS * 42, 2)
-    bias_rows = jnp.repeat(sides, SECTORS, 1)
+def block(core, both, gain_attn, w_qkv, rel_bias, w_out, gain_mlp, w_fc1, w_fc2, interpret=False):
     half = (PLACES, GRADS + OWN, LANES)
     return call(
         block_kernel,
         ((half, bf16, True), (half, bf16, True)),
-        (core, x, cot, gain_attn.reshape(1, D), w_qkv, bias_rows, w_out, gain_mlp.reshape(1, D), w_fc1, w_fc2),
+        (core, both, gain_attn, w_qkv, rel_bias, w_out, gain_mlp, w_fc1, w_fc2),
         interpret,
         room=32,
         scalars=1,
-        scratch=[pltpu.VMEM((2, *half), bf16)],
+        scratch=[pltpu.VMEM((2, *half), bf16), pltpu.VMEM(w_fc2.shape, bf16), pltpu.SemaphoreType.DMA],
+        loose=1,
     )
 
 
@@ -285,7 +346,6 @@
         total = total + arrived_ref[place, :GRADS, :].astype(f32)
     room = jnp.zeros((DEPTH, PART_ROOM - PART, LANES), f32)
     out_ref[:, :PART_ROOM, :] = jnp.concatenate([total.reshape(DEPTH, PART, LANES), room], 1).astype(bf16)
-    count = 2 * PLACES * 2 * DEPTH
     blocks = []
     for block in range(3):
         at = GRADS + block * 16
@@ -293,10 +353,8 @@
             jnp.concatenate([arrived_ref[:, at + c * OWN : at + c * OWN + 16, :].reshape(256, LANES) for c in range(2)], 0)
         )
     rows = jnp.concatenate(blocks, 1)
-    to = lax.broadcasted_iota(jnp.int32, (count, count), 0)
-    source = ((to & 1) << 8) | (((to >> 1) & 15) << 4) | (((to >> 5) & 1) << 3) | (to >> 6)
-    chosen = jnp.where(lax.broadcasted_iota(jnp.int32, (count, count), 1) == source, 1.0, 0.0).astype(bf16)
-    moved = dot(chosen, rows).astype(bf16).reshape(DEPTH, 2, 32, 3 * LANES)
+    moved = reorder(rows, lambda to: bits(to, 0, 1) << 8 | bits(to, 1, 4) << 4 | bits(to, 5, 1) << 3 | to >> 6)
+    moved = moved.astype(bf16).reshape(DEPTH, 2, 32, 3 * LANES)
     for array in range(2):
         for block in range(3):
             at = PART_ROOM + (array * 3 + block) * 32
@@ -310,13 +368,11 @@
 def depth_kernel(arrived_ref, part_ref, output_ref, d_latent_ref):
     total = jnp.sum(arrived_ref[:, :PART_ROOM, :].astype(f32), 0)[:PART]
     part_ref[...] = jnp.broadcast_to(total[None], (DEPTH, PART, LANES)).astype(bf16)
-    to = lax.broadcasted_iota(jnp.int32, (CELLS, CELLS), 0)
-    source = ((to & 7) << 5) | ((to >> 7) << 4) | (((to >> 3) & 7) << 1) | ((to >> 6) & 1)
-    chosen = jnp.where(lax.broadcasted_iota(jnp.int32, (CELLS, CELLS), 1) == source, 1.0, 0.0).astype(bf16)
     for array, ref in enumerate((output_ref, d_latent_ref)):
         starts = [PART_ROOM + (array * 3 + block) * 32 for block in range(3)]
         rows = jnp.concatenate([arrived_ref[:, at : at + 32, :].reshape(CELLS, LANES) for at in starts], 1)
-        ref[...] = dot(chosen, rows).astype(bf16)
+        moved = reorder(rows, lambda to: bits(to, 0, 3) << 5 | bits(to, 7, 1) << 4 | bits(to, 3, 3) << 1 | bits(to, 6, 1))
+        ref[...] = moved.astype(bf16)
 
 
 def depth(arrived, interpret=False):
@@ -324,48 +380,101 @@
     return call(depth_kernel, (((DEPTH, PART, LANES), bf16, True), cells, cells), (arrived,), interpret)
 
 
-def assemble_kernel(core_ref, here_ref, other_ref, d_qkv_ref, d_out_ref, d_fc1_ref, d_fc2_ref,
-                    d_rel_ref, d_gain_attn_ref, d_gain_mlp_ref):
-    def columns(half, at, block, rows):
-        first = at + block // 2 * rows
-        start = block % 2 * 8
-        return half[start : start + 8, first : first + rows, :].astype(f32).reshape(8 * rows, LANES)
-
-    def lanes(block):
-        return slice(block * LANES, (block + 1) * LANES)
-
-    def write(first, second):
-        for block in range(12):
-            d_fc1_ref[:, lanes(block)] = columns(first, FC1_AT, block, 48)
+def half_columns(half, at, block, rows):
+    first = at + block // 2 * rows
+    start = block % 2 * 8
+    return half[start : start + 8, first : first + rows, :].astype(f32).reshape(8 * rows, LANES)
+
+
+def lanes(block):
+    return slice(block * LANES, (block + 1) * LANES)
+
+
+def write_half(which, half_ref, outs, rooms, sems):
+    d_qkv_ref, d_out_ref, d_fc1_ref, d_fc2_ref = outs
+    fc1_room, fc2_room, qkv_room, out_room = rooms
+    split = QKV_FIRST * LANES
+
+    @pl.when(which == 0)
+    def _():
+        copies = []
+        for part in range(3):
+            for block in range(4 * part, 4 * part + 4):
+                fc1_room[:, lanes(block)] = half_columns(half_ref, FC1_AT, block, 48)
+            columns = pl.ds(part * 4 * LANES, 4 * LANES)
+            copies.append(pltpu.make_async_copy(fc1_room.at[:, columns], d_fc1_ref.at[:, columns], sems.at[part]))
+            copies[-1].start()
+        for block in range(QKV_FIRST):
+            qkv_room[:, lanes(block)] = half_columns(half_ref, QKV_AT, block, 48)
+        columns = pl.ds(0, split)
+        copies.append(pltpu.make_async_copy(qkv_room.at[:, columns], d_qkv_ref.at[:, columns], sems.at[3]))
+        copies[-1].start()
+        for copy in copies:
+            copy.wait()
+
+    @pl.when(which != 0)
+    def _():
+        copies = []
         for block in range(3):
             at = FC2_AT + block * 96
-            d_fc2_ref[:, lanes(block)] = second[:, at : at + 96, :].astype(f32).reshape(FF, LANES)
-        for block in range(9):
-            if block < QKV_FIRST:
-                d_qkv_ref[:, lanes(block)] = columns(first, QKV_AT, block, 48)
-            else:
-                d_qkv_ref[:, lanes(block)] = columns(second, OUT_AT, block - QKV_FIRST + 3, 48)
+            fc2_room[:, lanes(block)] = half_ref[:, at : at + 96, :].astype(f32).reshape(FF, LANES)
+            columns = pl.ds(block * LANES, LANES)
+            copies.append(pltpu.make_async_copy(fc2_room.at[:, columns], d_fc2_ref.at[:, columns], sems.at[block]))
+            copies[-1].start()
+        for block in range(QKV_FIRST, 9):
+            qkv_room[:, lanes(block)] = half_columns(half_ref, OUT_AT, block - QKV_FIRST + 3, 48)
+        columns = pl.ds(split, 3 * D - split)
+        copies.append(pltpu.make_async_copy(qkv_room.at[:, columns], d_qkv_ref.at[:, columns], sems.at[3]))
+        copies[-1].start()
         for block in range(3):
-            d_out_ref[:, lanes(block)] = columns(second, OUT_AT, block, 48)
-        small = first[0, SMALL_AT:GRADS, :].astype(f32)
-        for step in range(7):
-            d_rel_ref[:, step, :] = pltpu.roll(small, (LANES - 7 * step) % LANES, 1)[:HEADS, :7]
-        for block in range(3):
-            d_gain_attn_ref[lanes(block)] = small[8 + block]
-            d_gain_mlp_ref[lanes(block)] = small[11 + block]
-
-    @pl.when(core_ref[0] == 0)
-    def _():
-        write(here_ref, other_ref)
-
-    @pl.when(core_ref[0] != 0)
-    def _():
-        write(other_ref, here_ref)
-
-
-def assemble(core, here, other, interpret=False):
-    shapes = ((D, 3 * D), (D, D), (D, FF), (FF, D), (HEADS, 7, 7), (D,), (D,))
-    return call(assemble_kernel, tuple((s, f32, False) for s in shapes), (core, here, other), interpret, scalars=1)
+            out_room[:, lanes(block)] = half_columns(half_ref, OUT_AT, block, 48)
+        copies.append(pltpu.make_async_copy(out_room, d_out_ref, sems.at[4]))
+        copies[-1].start()
+        for copy in copies:
+            copy.wait()
+
+
+def near_kernel(core_ref, here_ref, *refs):
+    write_half(core_ref[0], here_ref, refs[:4], refs[4:8], refs[8])
+
+
+def far_kernel(core_ref, here_ref, other_ref, *refs):
+    outs, (d_rel_ref, d_gain_attn_ref, d_gain_mlp_ref), rooms, sems = refs[4:8], refs[8:11], refs[11:15], refs[15]
+    first = jnp.where(core_ref[0] == 0, here_ref[0, SMALL_AT:GRADS, :], other_ref[0, SMALL_AT:GRADS, :])
+    small = first.astype(f32)
+    for step in range(7):
+        d_rel_ref[:, step, :] = pltpu.roll(small, (LANES - 7 * step) % LANES, 1)[:HEADS, :7]
+    for block in range(3):
+        d_gain_attn_ref[lanes(block)] = small[8 + block]
+        d_gain_mlp_ref[lanes(block)] = small[11 + block]
+    write_half(1 - core_ref[0], other_ref, outs, rooms, sems)
+
+
+def assemble(core, here, other):
+    shapes = ((D, 3 * D), (D, D), (D, FF), (FF, D))
+    large = tuple(jax.ShapeDtypeStruct(s, f32) for s in shapes)
+    small = tuple(jax.ShapeDtypeStruct(s, f32) for s in ((HEADS, 7, 7), (D,), (D,)))
+    rooms = [pltpu.VMEM(s, f32) for s in ((D, FF), (FF, D), (D, 3 * D), (D, D))] + [pltpu.SemaphoreType.DMA((5,))]
+    far_away = pl.BlockSpec(memory_space=pl.ANY)
+    options = pltpu.CompilerParams(vmem_limit_bytes=16 * 1024 * 1024)
+    here = pltpu.with_memory_space_constraint(here, pltpu.VMEM)
+    begun = pl.pallas_call(
+        near_kernel,
+        out_shape=large,
+        in_specs=[SCALAR, WHOLE],
+        out_specs=(far_away,) * 4,
+        scratch_shapes=rooms,
+        compiler_params=options,
+    )(core, here)
+    return pl.pallas_call(
+        far_kernel,
+        out_shape=large + small,
+        in_specs=[SCALAR, WHOLE, WHOLE] + [far_away] * 4,
+        out_specs=(far_away,) * 4 + (WHOLE,) * 3,
+        scratch_shapes=rooms,
+        input_output_aliases={3: 0, 4: 1, 5: 2, 6: 3},
+        compiler_params=options,
+    )(core, here, pltpu.with_memory_space_constraint(other, pltpu.VMEM), *begun)
 
 
 def exchange(value, axes):
@@ -379,8 +488,9 @@
 def per_device(latent, cotangent, gain_attn, w_qkv, rel_bias, w_out, gain_mlp, w_fc1, w_fc2):
     shape = latent.shape
     core = lax.axis_index("core").reshape(1)
-    arrived = exchange(jnp.stack([latent.reshape(CELLS, D), cotangent.reshape(CELLS, D)], 1), AXES)
-    kept, sent = block(core, arrived[:, 0], arrived[:, 1], gain_attn, w_qkv, rel_bias, w_out, gain_mlp, w_fc1, w_fc2)
+    gain_attn, w_qkv, rel_bias, w_out, gain_mlp, w_fc1 = fetch(gain_attn, w_qkv, rel_bias, w_out, gain_mlp, w_fc1)
+    arrived = exchange(pack(latent, cotangent), AXES)
+    kept, sent = block(core, arrived, gain_attn, w_qkv, rel_bias, w_out, gain_mlp, w_fc1, w_fc2)
     merged = merge(core, kept, to_sibling(sent))
     part, output, d_latent = depth(exchange(plane(exchange(merged, PLANE)), "z"))
     piece = exchange(part, "z").reshape(GRADS, LANES)

time: 152 us -> 150 us (0.987)
  Pallas kernels: 14.7 us -> 20 us
  local copies, waits for them, and re-layouts: 3.74 us -> 0.35 us
  waiting for transfers between devices: 23.7 us -> 21.3 us
    pallas_call x0 -> x3, Pallas kernels: none -> 6.24 us  [the longest x1 2.63 us: assemble(): pl.pallas_call(far_kernel, out_shape=large + small, in_specs=[SCALAR, WHO...]
    ppermute x2, waiting for transfers between devices: 7.1 us -> 5.22 us  [to_sibling(): return lax.ppermute(value, 'core', [(0, 1), (1, 0)])]
    slice x2 -> x0, local copies, waits for them, and re-layouts: 1.84 us -> none  [the longest x1 1.84 us: per_device(): arrived[:, 1]]
  transfers between devices with their start and end apart: 3 -> 3, of which waited for: 3 -> 3; matrix products, arithmetic and copies ran while one was open for 0% -> 0% of each run, Pallas kernels for 0% -> 2%
where the time goes in v4:
time: 150 us
  blocking collectives  85.2 us (57%)
  starting transfers between devices  21.8 us (15%)
  waiting for transfers between devices  21.3 us (14%)
  Pallas kernels  20 us (13%)
    all_to_all x4, blocking collectives, exchange(): return lax.all_to_all(value, axes, 0, 0)  85.2 us
    all_to_all x1, waiting for transfers between devices, exchange(): return lax.all_to_all(value, axes, 0, 0)  16.1 us
    all_to_all x1, starting transfers between devices, exchange(): return lax.all_to_all(value, axes, 0, 0)  15.7 us
    pallas_call x5, Pallas kernels, call(): pl.pallas_call(kernel, out_shape=shapes, in_specs=[SCALAR] * scalars + [W...  13.8 us
    ppermute x2, starting transfers between devices, to_sibling(): return lax.ppermute(value, 'core', [(0, 1), (1, 0)])  6.12 us
    ppermute x2, waiting for transfers between devices, to_sibling(): return lax.ppermute(value, 'core', [(0, 1), (1, 0)])  5.22 us
  transfers between devices with their start and end apart: 3, of which 3 were waited for; matrix products, arithmetic and copies ran while one was open for 0% of the time, Pallas kernels for 2%

profile of v4, /device:TPU:1, one launch (start us, length us, event | category | flops | bytes accessed | tf_op | source)
XLA Modules:
  0.0 149.5 jit_solution(2906334830407802628)
XLA Ops:
  0.6 2.1 %shard_map.160 = bf16[256,2,384]{2,1,0:T(2,128)(2,1)} custom-call(bf16[16,16,384]{2,1,0:T(8,128)(2,1)} %latent_ref.1, bf16[16,16,384]{2,1,0:T(8,128)(2,1)} %cot_ref.1), custom_call_target="tpu_custom_call" | custom-call | tf_op jit(solution)/shard_map/pallas_call | solution.py:296
  2.7 15.7 %all-to-all-start = ((bf16[256,2,384]{2,1,0:T(2,128)(2,1)}), bf16[256,2,384]{2,1,0:T(2,128)(2,1)S(1)}, u32[]{:S(2)}, u32[]{:S(2)}) async-start(bf16[256,2,384]{2,1,0:T(2,128)(2,1)} %shard_map.160), calls=%async_computation | async-start | bytes 786432 | tf_op jit(solution)/shard_map/all_to_all | solution.py:481
  18.4 1.7 %shard_map.161 = (f32[384]{0:T(512)S(1)}, bf16[384,1152]{1,0:T(8,128)(2,1)S(1)}, f32[6,7,7]{2,1,0:T(8,128)S(1)}, bf16[384,384]{1,0:T(8,128)(2,1)S(1)}, f32[384]{0:T(512)S(1)}, /*index=5*/bf16[384,1536]{1,0:T(8,128)(2,1)S(1)}) custom-call(f32[384]{0:T(512)} %refs_0_.1, bf16[384,1152]{1,0:T(8,128)(2,1)} %refs_1_.1, f32[6,7,7]{2,1,0:T(8,128)} %refs_2_.1, ...), custom_call_target="tpu_custom_call" | custom-call | tf_op jit(solution)/shard_map/pallas_call | solution.py:114
  20.1 16.1 %all-to-all-done.both_ref = bf16[256,2,384]{2,1,0:T(2,128)(2,1)S(1)} async-done(((bf16[256,2,384]{2,1,0:T(2,128)(2,1)}), bf16[256,2,384]{2,1,0:T(2,128)(2,1)S(1)}, u32[]{:S(2)}, u32[]{:S(2)}) %all-to-all-start) | async-done | bytes 393248 | tf_op jit(solution)/shard_map/all_to_all | solution.py:481
  36.2 9.6 %shard_map.162 = (bf16[16,496,128]{2,1,0:T(8,128)(2,1)S(1)}, bf16[16,496,128]{2,1,0:T(8,128)(2,1)S(1)}) custom-call(s32[1]{0:T(128)} %bitcast.core_ref, bf16[256,2,384]{2,1,0:T(2,128)(2,1)S(1)} %all-to-all-done.both_ref, f32[384]{0:T(512)S(1)} %get-tuple-element.31.gain_attn_ref, bf16[384,1152]{1,0:T(8,128)(2,1)S(1)} %get-tuple-element.32.w_qkv_ref, ...), custom_call_target="tpu_custom_call" | custom-call | tf_op jit(solution)/shard_map/pallas_call | solution.py:296
  45.8 1.4 collective-permute-start
  47.1 3.7 %collective-permute-done.arrived_ref = bf16[16,496,128]{2,1,0:T(8,128)(2,1)S(1)} collective-permute-done((bf16[16,496,128]{2,1,0:T(8,128)(2,1)S(1)}, bf16[16,496,128]{2,1,0:T(8,128)(2,1)S(1)}, u32[]{:S(2)}, u32[]{:S(2)}) %collective-permute-start) | collective-permute-done | bytes 2031648 | tf_op jit(solution)/shard_map/ppermute | solution.py:485
  50.8 0.4 shard_map.163
  51.3 32.0 %all_to_all.25.arrived_ref = bf16[16,544,128]{2,1,0:T(8,128)(2,1)S(1)} all-to-all(bf16[16,544,128]{2,1,0:T(8,128)(2,1)S(1)} %shard_map.163), channel_id=1, replica_groups=mesh['y_lo'=2,'core'=2,'y_hi'=2,'x'=4,'z'=8] {'y_lo','y_hi','x'}, dimensions={0} | all-to-all | bytes 4456448 | tf_op jit(solution)/shard_map/all_to_all | solution.py:481
  83.3 0.7 shard_map.164
  84.0 17.2 %all_to_all.26.arrived_ref = bf16[8,256,128]{2,1,0:T(8,128)(2,1)S(1)} all-to-all(bf16[8,256,128]{2,1,0:T(8,128)(2,1)S(1)} %shard_map.164), channel_id=1, replica_groups=mesh['y_lo'=2,'core'=2,'y_hi'=2,'x'=4,'z'=8] {'z'}, dimensions={0} | all-to-all | bytes 1048576 | tf_op jit(solution)/shard_map/all_to_all | solution.py:481
  101.3 1.0 shard_map.165
  102.3 11.0 %all_to_all.27 = bf16[8,56,128]{2,1,0:T(8,128)(2,1)S(1)} all-to-all(bf16[8,56,128]{2,1,0:T(8,128)(2,1)S(1)} %get-tuple-element.41), channel_id=1, replica_groups=mesh['y_lo'=2,'core'=2,'y_hi'=2,'x'=4,'z'=8] {'z'}, dimensions={0} | all-to-all | bytes 229376 | tf_op jit(solution)/shard_map/all_to_all | solution.py:481
  113.2 0.3 broadcast_in_dim.3
  113.6 25.0 %all_to_all.28.here_ref = bf16[16,448,128]{2,1,0:T(8,128)(2,1)S(1)} all-to-all(bf16[16,448,128]{2,1,0:T(8,128)(2,1)S(1)} %broadcast_in_dim.3), channel_id=1, replica_groups=mesh['y_lo'=2,'core'=2,'y_hi'=2,'x'=4,'z'=8] {'y_lo','y_hi','x'}, dimensions={0} | all-to-all | bytes 3670016 | tf_op jit(solution)/shard_map/all_to_all | solution.py:481
  138.6 4.7 %collective-permute-start.1 = (bf16[16,448,128]{2,1,0:T(8,128)(2,1)S(1)}, bf16[16,448,128]{2,1,0:T(8,128)(2,1)S(1)}, u32[]{:S(2)}, u32[]{:S(2)}) collective-permute-start(bf16[16,448,128]{2,1,0:T(8,128)(2,1)S(1)} %all_to_all.28.here_ref), channel_id=1, source_target_pairs={{0,64},{64,0},{1,65},{65,1},{2,66},{66,2},{3,67},{67,3},{4,68},{68... | collective-permute-start | bytes 5505032 | tf_op jit(solution)/shard_map/ppermute | solution.py:485
  143.3 1.9 %shard_map.166 = (f32[384,1152]{1,0:T(8,128)}, f32[384,384]{1,0:T(8,128)}, f32[384,1536]{1,0:T(8,128)}, f32[1536,384]{1,0:T(8,128)}) custom-call(s32[1]{0:T(128)} %bitcast.core_ref, bf16[16,448,128]{2,1,0:T(8,128)(2,1)S(1)} %all_to_all.28.here_ref), custom_call_target="tpu_custom_call" | custom-call | tf_op jit(solution)/shard_map/pallas_call | solution.py:461
  145.2 1.5 %collective-permute-done.1.other_ref = bf16[16,448,128]{2,1,0:T(8,128)(2,1)S(1)} collective-permute-done((bf16[16,448,128]{2,1,0:T(8,128)(2,1)S(1)}, bf16[16,448,128]{2,1,0:T(8,128)(2,1)S(1)}, u32[]{:S(2)}, u32[]{:S(2)}) %collective-permute-start.1) | collective-permute-done | bytes 1835040 | tf_op jit(solution)/shard_map/ppermute | solution.py:485
  146.8 2.6 %shard_map.167 = (f32[384,1152]{1,0:T(8,128)}, f32[384,384]{1,0:T(8,128)}, f32[384,1536]{1,0:T(8,128)}, f32[1536,384]{1,0:T(8,128)}, f32[6,7,7]{2,1,0:T(8,128)}, /*index=5*/f32[384]{0:T(512)}, f32[384]{0:T(512)}) custom-call(s32[1]{0:T(128)} %bitcast.core_ref, ...), custom_call_target="tpu_custom_call", output_to_operand_aliasing={{0}: (3, {}), {1}: (4, {}), {2}: (5, {}), {3}: (6, {})} | custom-call | tf_op jit(solution)/shard_map/pallas_call | solution.py:469
Async XLA Ops:
  2.7 33.5 %all-to-all-start = ((bf16[256,2,384]{2,1,0:T(2,128)(2,1)}), bf16[256,2,384]{2,1,0:T(2,128)(2,1)S(1)}, u32[]{:S(2)}, u32[]{:S(2)}) async-start(bf16[256,2,384]{2,1,0:T(2,128)(2,1)} %shard_map.160), calls=%async_computation | async-start | bytes 786432 | tf_op jit(solution)/shard_map/all_to_all | solution.py:481
  45.8 5.1 %collective-permute-start = (bf16[16,496,128]{2,1,0:T(8,128)(2,1)S(1)}, bf16[16,496,128]{2,1,0:T(8,128)(2,1)S(1)}, u32[]{:S(2)}, u32[]{:S(2)}) collective-permute-start(bf16[16,496,128]{2,1,0:T(8,128)(2,1)S(1)} %get-tuple-element.38), channel_id=1, source_target_pairs={{0,64},{64,0},{1,65},{65,1},{2,66},{66,2},{3,67},{67,3},{4,68},{68... | collective-permute-start | bytes 6094856 | tf_op jit(solution)/shard_map/ppermute | solution.py:485
  138.6 8.2 %collective-permute-start.1 = (bf16[16,448,128]{2,1,0:T(8,128)(2,1)S(1)}, bf16[16,448,128]{2,1,0:T(8,128)(2,1)S(1)}, u32[]{:S(2)}, u32[]{:S(2)}) collective-permute-start(bf16[16,448,128]{2,1,0:T(8,128)(2,1)S(1)} %all_to_all.28.here_ref), channel_id=1, source_target_pairs={{0,64},{64,0},{1,65},{65,1},{2,66},{66,2},{3,67},{67,3},{4,68},{68... | collective-permute-start | bytes 5505032 | tf_op jit(solution)/shard_map/ppermute | solution.py:485

commit v5 on v4

--- a/solution.py
+++ b/solution.py
@@ -24,6 +24,7 @@
 PART = GRADS // DEPTH
 OWN = 48
 PART_ROOM = 64
+ROOM = PART_ROOM + 96
 FC1_AT, QKV_AT = 0, 288
 FC2_AT, OUT_AT, QKV_REST_AT = 0, 288, 360
 SMALL_AT = 432
@@ -340,7 +341,7 @@
     return call(merge_kernel, (out,), (core, kept, arrived), interpret, scalars=1)[0]
 
 
-def plane_kernel(arrived_ref, out_ref):
+def plane_kernel(arrived_ref, out_ref, later_ref):
     total = arrived_ref[0, :GRADS, :].astype(f32)
     for place in range(1, PLACES):
         total = total + arrived_ref[place, :GRADS, :].astype(f32)
@@ -355,29 +356,36 @@
     rows = jnp.concatenate(blocks, 1)
     moved = reorder(rows, lambda to: bits(to, 0, 1) << 8 | bits(to, 1, 4) << 4 | bits(to, 5, 1) << 3 | to >> 6)
     moved = moved.astype(bf16).reshape(DEPTH, 2, 32, 3 * LANES)
-    for array in range(2):
+    for array, (ref, start) in enumerate(((out_ref, PART_ROOM), (later_ref, 0))):
         for block in range(3):
-            at = PART_ROOM + (array * 3 + block) * 32
-            out_ref[:, at : at + 32, :] = moved[:, array, :, block * LANES : (block + 1) * LANES]
+            at = start + block * 32
+            ref[:, at : at + 32, :] = moved[:, array, :, block * LANES : (block + 1) * LANES]
 
 
 def plane(arrived, interpret=False):
-    return call(plane_kernel, (((DEPTH, PART_ROOM + 192, LANES), bf16, True),), (arrived,), interpret)[0]
-
-
-def depth_kernel(arrived_ref, part_ref, output_ref, d_latent_ref):
-    total = jnp.sum(arrived_ref[:, :PART_ROOM, :].astype(f32), 0)[:PART]
-    part_ref[...] = jnp.broadcast_to(total[None], (DEPTH, PART, LANES)).astype(bf16)
-    for array, ref in enumerate((output_ref, d_latent_ref)):
-        starts = [PART_ROOM + (array * 3 + block) * 32 for block in range(3)]
-        rows = jnp.concatenate([arrived_ref[:, at : at + 32, :].reshape(CELLS, LANES) for at in starts], 1)
-        moved = reorder(rows, lambda to: bits(to, 0, 3) << 5 | bits(to, 7, 1) << 4 | bits(to, 3, 3) << 1 | bits(to, 6, 1))
-        ref[...] = moved.astype(bf16)
-
-
-def depth(arrived, interpret=False):
-    cells = ((CELLS, D), bf16, False)
-    return call(depth_kernel, (((DEPTH, PART, LANES), bf16, True), cells, cells), (arrived,), interpret)
+    outs = (((DEPTH, ROOM, LANES), bf16, True), ((DEPTH, ROOM - PART_ROOM, LANES), bf16, True))
+    return call(plane_kernel, outs, (arrived,), interpret)
+
+
+def depth_kernel(arrived_ref, later_ref, out_ref):
+    total = jnp.sum(arrived_ref[:, :PART_ROOM, :].astype(f32), 0)
+    out_ref[:, :PART_ROOM, :] = jnp.broadcast_to(total[None], (DEPTH, PART_ROOM, LANES)).astype(bf16)
+    out_ref[:, PART_ROOM:, :] = later_ref[...]
+
+
+def depth(arrived, later, interpret=False):
+    return call(depth_kernel, (((DEPTH, ROOM, LANES), bf16, True),), (arrived, later), interpret)[0]
+
+
+def spread_kernel(arrived_ref, out_ref):
+    parts = arrived_ref[:, :PART_ROOM, :].astype(f32)[:, :PART]
+    piece = parts.reshape(GRADS, LANES).astype(bf16)
+    for place in range(PLACES):
+        out_ref[place] = piece
+
+
+def spread(arrived, interpret=False):
+    return call(spread_kernel, (((PLACES, GRADS, LANES), bf16, True),), (arrived,), interpret)[0]
 
 
 def half_columns(half, at, block, rows):
@@ -434,8 +442,13 @@
             copy.wait()
 
 
-def near_kernel(core_ref, here_ref, *refs):
-    write_half(core_ref[0], here_ref, refs[:4], refs[4:8], refs[8])
+def near_kernel(core_ref, here_ref, output_ref, d_latent_ref, *refs):
+    for cells_ref, ref in zip((output_ref, d_latent_ref), refs[4:6]):
+        starts = [PART_ROOM + block * 32 for block in range(3)]
+        rows = jnp.concatenate([cells_ref[:, at : at + 32, :].reshape(CELLS, LANES) for at in starts], 1)
+        moved = reorder(rows, lambda to: bits(to, 0, 3) << 5 | bits(to, 7, 1) << 4 | bits(to, 3, 3) << 1 | bits(to, 6, 1))
+        ref[...] = moved.astype(bf16)
+    write_half(core_ref[0], here_ref, refs[:4], refs[6:10], refs[10])
 
 
 def far_kernel(core_ref, here_ref, other_ref, *refs):
@@ -450,7 +463,7 @@
     write_half(1 - core_ref[0], other_ref, outs, rooms, sems)
 
 
-def assemble(core, here, other):
+def assemble(core, here, other, *cells):
     shapes = ((D, 3 * D), (D, D), (D, FF), (FF, D))
     large = tuple(jax.ShapeDtypeStruct(s, f32) for s in shapes)
     small = tuple(jax.ShapeDtypeStruct(s, f32) for s in ((HEADS, 7, 7), (D,), (D,)))
@@ -460,13 +473,13 @@
     here = pltpu.with_memory_space_constraint(here, pltpu.VMEM)
     begun = pl.pallas_call(
         near_kernel,
-        out_shape=large,
-        in_specs=[SCALAR, WHOLE],
-        out_specs=(far_away,) * 4,
+        out_shape=large + (jax.ShapeDtypeStruct((CELLS, D), bf16),) * 2,
+        in_specs=[SCALAR] + [WHOLE] * 3,
+        out_specs=(far_away,) * 4 + (WHOLE,) * 2,
         scratch_shapes=rooms,
         compiler_params=options,
-    )(core, here)
-    return pl.pallas_call(
+    )(core, here, *(pltpu.with_memory_space_constraint(c, pltpu.VMEM) for c in cells))
+    return begun[4:], pl.pallas_call(
         far_kernel,
         out_shape=large + small,
         in_specs=[SCALAR, WHOLE, WHOLE] + [far_away] * 4,
@@ -474,7 +487,7 @@
         scratch_shapes=rooms,
         input_output_aliases={3: 0, 4: 1, 5: 2, 6: 3},
         compiler_params=options,
-    )(core, here, pltpu.with_memory_space_constraint(other, pltpu.VMEM), *begun)
+    )(core, here, pltpu.with_memory_space_constraint(other, pltpu.VMEM), *begun[:4])
 
 
 def exchange(value, axes):
@@ -492,10 +505,12 @@
     arrived = exchange(pack(latent, cotangent), AXES)
     kept, sent = block(core, arrived, gain_attn, w_qkv, rel_bias, w_out, gain_mlp, w_fc1, w_fc2)
     merged = merge(core, kept, to_sibling(sent))
-    part, output, d_latent = depth(exchange(plane(exchange(merged, PLANE)), "z"))
-    piece = exchange(part, "z").reshape(GRADS, LANES)
-    here = exchange(jnp.broadcast_to(piece, (PLACES, GRADS, LANES)), PLANE)
-    return (output.reshape(shape), d_latent.reshape(shape)) + assemble(core, here, to_sibling(here))
+    parts, later = plane(exchange(merged, PLANE))
+    first = exchange(parts, "z")
+    second = exchange(depth(first, later), "z")
+    here = exchange(spread(second), PLANE)
+    (output, d_latent), grads = assemble(core, here, to_sibling(here), first, second)
+    return (output.reshape(shape), d_latent.reshape(shape)) + grads
 
 
 def solution(mesh):

time: 150 us -> 147 us (0.980)
  blocking collectives: 85.2 us -> 82.5 us
    all_to_all x4, blocking collectives: 85.2 us -> 82.5 us  [exchange(): return lax.all_to_all(value, axes, 0, 0)]
    pallas_call x5 -> x6, Pallas kernels: 13.8 us -> 13.2 us  [call(): pl.pallas_call(kernel, out_shape=shapes, in_specs=[SCALAR] * scalars + [W...]
  transfers between devices with their start and end apart: 3 -> 3, of which waited for: 3 -> 3; matrix products, arithmetic and copies ran while one was open for 0% -> 0% of each run, Pallas kernels for 2% -> 3%
where the time goes in v5:
time: 147 us
  blocking collectives  82.5 us (56%)
  starting transfers between devices  22.7 us (15%)
  Pallas kernels  20.4 us (14%)
  waiting for transfers between devices  20.3 us (14%)
    all_to_all x4, blocking collectives, exchange(): return lax.all_to_all(value, axes, 0, 0)  82.5 us
    all_to_all x1, waiting for transfers between devices, exchange(): return lax.all_to_all(value, axes, 0, 0)  16.1 us
    all_to_all x1, starting transfers between devices, exchange(): return lax.all_to_all(value, axes, 0, 0)  15.7 us
    pallas_call x6, Pallas kernels, call(): pl.pallas_call(kernel, out_shape=shapes, in_specs=[SCALAR] * scalars + [W...  13.2 us
    ppermute x2, starting transfers between devices, to_sibling(): return lax.ppermute(value, 'core', [(0, 1), (1, 0)])  7.02 us
    ppermute x2, waiting for transfers between devices, to_sibling(): return lax.ppermute(value, 'core', [(0, 1), (1, 0)])  4.19 us
  transfers between devices with their start and end apart: 3, of which 3 were waited for; matrix products, arithmetic and copies ran while one was open for 0% of the time, Pallas kernels for 3%

profile of v5, /device:TPU:1, one launch (start us, length us, event | category | flops | bytes accessed | tf_op | source)
XLA Modules:
  0.0 146.7 jit_solution(17393630629515090299)
XLA Ops:
  0.6 2.1 %shard_map.160 = bf16[256,2,384]{2,1,0:T(2,128)(2,1)} custom-call(bf16[16,16,384]{2,1,0:T(8,128)(2,1)} %latent_ref.1, bf16[16,16,384]{2,1,0:T(8,128)(2,1)} %cot_ref.1), custom_call_target="tpu_custom_call" | custom-call | tf_op jit(solution)/shard_map/pallas_call | solution.py:297
  2.7 15.7 %all-to-all-start = ((bf16[256,2,384]{2,1,0:T(2,128)(2,1)}), bf16[256,2,384]{2,1,0:T(2,128)(2,1)S(1)}, u32[]{:S(2)}, u32[]{:S(2)}) async-start(bf16[256,2,384]{2,1,0:T(2,128)(2,1)} %shard_map.160), calls=%async_computation | async-start | bytes 786432 | tf_op jit(solution)/shard_map/all_to_all | solution.py:494
  18.4 1.7 %shard_map.161 = (f32[384]{0:T(512)S(1)}, bf16[384,1152]{1,0:T(8,128)(2,1)S(1)}, f32[6,7,7]{2,1,0:T(8,128)S(1)}, bf16[384,384]{1,0:T(8,128)(2,1)S(1)}, f32[384]{0:T(512)S(1)}, /*index=5*/bf16[384,1536]{1,0:T(8,128)(2,1)S(1)}) custom-call(f32[384]{0:T(512)} %refs_0_.1, bf16[384,1152]{1,0:T(8,128)(2,1)} %refs_1_.1, f32[6,7,7]{2,1,0:T(8,128)} %refs_2_.1, ...), custom_call_target="tpu_custom_call" | custom-call | tf_op jit(solution)/shard_map/pallas_call | solution.py:115
  20.1 16.1 %all-to-all-done.both_ref = bf16[256,2,384]{2,1,0:T(2,128)(2,1)S(1)} async-done(((bf16[256,2,384]{2,1,0:T(2,128)(2,1)}), bf16[256,2,384]{2,1,0:T(2,128)(2,1)S(1)}, u32[]{:S(2)}, u32[]{:S(2)}) %all-to-all-start) | async-done | bytes 393248 | tf_op jit(solution)/shard_map/all_to_all | solution.py:494
  36.2 9.5 %shard_map.162 = (bf16[16,496,128]{2,1,0:T(8,128)(2,1)S(1)}, bf16[16,496,128]{2,1,0:T(8,128)(2,1)S(1)}) custom-call(s32[1]{0:T(128)} %bitcast.core_ref, bf16[256,2,384]{2,1,0:T(2,128)(2,1)S(1)} %all-to-all-done.both_ref, f32[384]{0:T(512)S(1)} %get-tuple-element.32.gain_attn_ref, bf16[384,1152]{1,0:T(8,128)(2,1)S(1)} %get-tuple-element.33.w_qkv_ref, ...), custom_call_target="tpu_custom_call" | custom-call | tf_op jit(solution)/shard_map/pallas_call | solution.py:297
  45.8 1.4 collective-permute-start
  47.1 3.7 %collective-permute-done.arrived_ref = bf16[16,496,128]{2,1,0:T(8,128)(2,1)S(1)} collective-permute-done((bf16[16,496,128]{2,1,0:T(8,128)(2,1)S(1)}, bf16[16,496,128]{2,1,0:T(8,128)(2,1)S(1)}, u32[]{:S(2)}, u32[]{:S(2)}) %collective-permute-start) | collective-permute-done | bytes 2031648 | tf_op jit(solution)/shard_map/ppermute | solution.py:498
  50.8 0.4 shard_map.163
  51.3 32.0 %all_to_all.25.arrived_ref = bf16[16,544,128]{2,1,0:T(8,128)(2,1)S(1)} all-to-all(bf16[16,544,128]{2,1,0:T(8,128)(2,1)S(1)} %shard_map.163), channel_id=1, replica_groups=mesh['y_lo'=2,'core'=2,'y_hi'=2,'x'=4,'z'=8] {'y_lo','y_hi','x'}, dimensions={0} | all-to-all | bytes 4456448 | tf_op jit(solution)/shard_map/all_to_all | solution.py:494
  83.3 0.7 shard_map.164
  84.0 13.1 %all_to_all.26.arrived_ref.output_ref = bf16[8,160,128]{2,1,0:T(8,128)(2,1)S(1)} all-to-all(bf16[8,160,128]{2,1,0:T(8,128)(2,1)S(1)} %get-tuple-element.40), channel_id=1, replica_groups=mesh['y_lo'=2,'core'=2,'y_hi'=2,'x'=4,'z'=8] {'z'}, dimensions={0} | all-to-all | bytes 655360 | tf_op jit(solution)/shard_map/all_to_all | solution.py:494
  97.2 13.4 %all_to_all.27.arrived_ref.d_latent_ref = bf16[8,160,128]{2,1,0:T(8,128)(2,1)S(1)} all-to-all(bf16[8,160,128]{2,1,0:T(8,128)(2,1)S(1)} %shard_map.165), channel_id=1, replica_groups=mesh['y_lo'=2,'core'=2,'y_hi'=2,'x'=4,'z'=8] {'z'}, dimensions={0} | all-to-all | bytes 655360 | tf_op jit(solution)/shard_map/all_to_all | solution.py:494
  110.6 0.3 shard_map.166
  110.9 24.0 %all_to_all.28.here_ref = bf16[16,448,128]{2,1,0:T(8,128)(2,1)S(1)} all-to-all(bf16[16,448,128]{2,1,0:T(8,128)(2,1)S(1)} %shard_map.166), channel_id=1, replica_groups=mesh['y_lo'=2,'core'=2,'y_hi'=2,'x'=4,'z'=8] {'y_lo','y_hi','x'}, dimensions={0} | all-to-all | bytes 3670016 | tf_op jit(solution)/shard_map/all_to_all | solution.py:494
  134.9 5.6 %collective-permute-start.1 = (bf16[16,448,128]{2,1,0:T(8,128)(2,1)S(1)}, bf16[16,448,128]{2,1,0:T(8,128)(2,1)S(1)}, u32[]{:S(2)}, u32[]{:S(2)}) collective-permute-start(bf16[16,448,128]{2,1,0:T(8,128)(2,1)S(1)} %all_to_all.28.here_ref), channel_id=1, source_target_pairs={{0,64},{64,0},{1,65},{65,1},{2,66},{66,2},{3,67},{67,3},{4,68},{68... | collective-permute-start | bytes 5505032 | tf_op jit(solution)/shard_map/ppermute | solution.py:498
  140.5 2.9 %shard_map.167 = (f32[384,1152]{1,0:T(8,128)}, f32[384,384]{1,0:T(8,128)}, f32[384,1536]{1,0:T(8,128)}, f32[1536,384]{1,0:T(8,128)}, bf16[256,384]{1,0:T(8,128)(2,1)}, /*index=5*/bf16[256,384]{1,0:T(8,128)(2,1)}) custom-call(s32[1]{0:T(128)} %bitcast.core_ref, bf16[16,448,128]{2,1,0:T(8,128)(2,1)S(1)} %all_to_all.28.here_ref, ...), custom_call_target="tpu_custom_call" | custom-call | tf_op jit(solution)/shard_map/pallas_call | solution.py:474
  143.5 0.5 collective-permute-done.1.other_ref
  144.0 2.6 %shard_map.168 = (f32[384,1152]{1,0:T(8,128)}, f32[384,384]{1,0:T(8,128)}, f32[384,1536]{1,0:T(8,128)}, f32[1536,384]{1,0:T(8,128)}, f32[6,7,7]{2,1,0:T(8,128)}, /*index=5*/f32[384]{0:T(512)}, f32[384]{0:T(512)}) custom-call(s32[1]{0:T(128)} %bitcast.core_ref, ...), custom_call_target="tpu_custom_call", output_to_operand_aliasing={{0}: (3, {}), {1}: (4, {}), {2}: (5, {}), {3}: (6, {})} | custom-call | tf_op jit(solution)/shard_map/pallas_call | solution.py:482
  (1 shorter events, 0.0 us)
Async XLA Ops:
  2.7 33.5 %all-to-all-start = ((bf16[256,2,384]{2,1,0:T(2,128)(2,1)}), bf16[256,2,384]{2,1,0:T(2,128)(2,1)S(1)}, u32[]{:S(2)}, u32[]{:S(2)}) async-start(bf16[256,2,384]{2,1,0:T(2,128)(2,1)} %shard_map.160), calls=%async_computation | async-start | bytes 786432 | tf_op jit(solution)/shard_map/all_to_all | solution.py:494
  45.8 5.1 %collective-permute-start = (bf16[16,496,128]{2,1,0:T(8,128)(2,1)S(1)}, bf16[16,496,128]{2,1,0:T(8,128)(2,1)S(1)}, u32[]{:S(2)}, u32[]{:S(2)}) collective-permute-start(bf16[16,496,128]{2,1,0:T(8,128)(2,1)S(1)} %get-tuple-element.39), channel_id=1, source_target_pairs={{0,64},{64,0},{1,65},{65,1},{2,66},{66,2},{3,67},{67,3},{4,68},{68... | collective-permute-start | bytes 6094856 | tf_op jit(solution)/shard_map/ppermute | solution.py:498
  134.9 9.0 %collective-permute-start.1 = (bf16[16,448,128]{2,1,0:T(8,128)(2,1)S(1)}, bf16[16,448,128]{2,1,0:T(8,128)(2,1)S(1)}, u32[]{:S(2)}, u32[]{:S(2)}) collective-permute-start(bf16[16,448,128]{2,1,0:T(8,128)(2,1)S(1)} %all_to_all.28.here_ref), channel_id=1, source_target_pairs={{0,64},{64,0},{1,65},{65,1},{2,66},{66,2},{3,67},{67,3},{4,68},{68... | collective-permute-start | bytes 5505032 | tf_op jit(solution)/shard_map/ppermute | solution.py:498

commit v6 on v5

--- a/solution.py
+++ b/solution.py
@@ -452,15 +452,22 @@
 
 
 def far_kernel(core_ref, here_ref, other_ref, *refs):
-    outs, (d_rel_ref, d_gain_attn_ref, d_gain_mlp_ref), rooms, sems = refs[4:8], refs[8:11], refs[11:15], refs[15]
+    outs, small_outs, rooms, sems = refs[4:8], refs[8:11], refs[11:15], refs[15]
+    small_rooms, small_sems = refs[16:19], refs[19]
+    d_rel_room, d_gain_attn_room, d_gain_mlp_room = small_rooms
     first = jnp.where(core_ref[0] == 0, here_ref[0, SMALL_AT:GRADS, :], other_ref[0, SMALL_AT:GRADS, :])
     small = first.astype(f32)
     for step in range(7):
-        d_rel_ref[:, step, :] = pltpu.roll(small, (LANES - 7 * step) % LANES, 1)[:HEADS, :7]
+        d_rel_room[:, step, :] = pltpu.roll(small, (LANES - 7 * step) % LANES, 1)[:HEADS, :7]
     for block in range(3):
-        d_gain_attn_ref[lanes(block)] = small[8 + block]
-        d_gain_mlp_ref[lanes(block)] = small[11 + block]
+        d_gain_attn_room[lanes(block)] = small[8 + block]
+        d_gain_mlp_room[lanes(block)] = small[11 + block]
+    copies = [pltpu.make_async_copy(small_rooms[i], small_outs[i], small_sems.at[i]) for i in range(3)]
+    for copy in copies:
+        copy.start()
     write_half(1 - core_ref[0], other_ref, outs, rooms, sems)
+    for copy in copies:
+        copy.wait()
 
 
 def assemble(core, here, other, *cells):
@@ -483,8 +490,10 @@
         far_kernel,
         out_shape=large + small,
         in_specs=[SCALAR, WHOLE, WHOLE] + [far_away] * 4,
-        out_specs=(far_away,) * 4 + (WHOLE,) * 3,
-        scratch_shapes=rooms,
+        out_specs=(far_away,) * 7,
+        scratch_shapes=rooms
+        + [pltpu.VMEM(o.shape, f32) for o in small]
+        + [pltpu.SemaphoreType.DMA((3,))],
         input_output_aliases={3: 0, 4: 1, 5: 2, 6: 3},
         compiler_params=options,
     )(core, here, pltpu.with_memory_space_constraint(other, pltpu.VMEM), *begun[:4])

time: 147 us -> 146 us (level)
  no operation moved by 1% of the time
where the time goes in v6:
time: 146 us
  blocking collectives  82.5 us (57%)
  starting transfers between devices  22.7 us (16%)
  waiting for transfers between devices  20.3 us (14%)
  Pallas kernels  19.9 us (14%)
    all_to_all x4, blocking collectives, exchange(): return lax.all_to_all(value, axes, 0, 0)  82.5 us
    all_to_all x1, waiting for transfers between devices, exchange(): return lax.all_to_all(value, axes, 0, 0)  16.1 us
    all_to_all x1, starting transfers between devices, exchange(): return lax.all_to_all(value, axes, 0, 0)  15.7 us
    pallas_call x6, Pallas kernels, call(): pl.pallas_call(kernel, out_shape=shapes, in_specs=[SCALAR] * scalars + [W...  13.2 us
    ppermute x2, starting transfers between devices, to_sibling(): return lax.ppermute(value, 'core', [(0, 1), (1, 0)])  7.02 us
    ppermute x2, waiting for transfers between devices, to_sibling(): return lax.ppermute(value, 'core', [(0, 1), (1, 0)])  4.19 us
  transfers between devices with their start and end apart: 3, of which 3 were waited for; matrix products, arithmetic and copies ran while one was open for 0% of the time, Pallas kernels for 3%

profile of v6, /device:TPU:1, one launch (start us, length us, event | category | flops | bytes accessed | tf_op | source)
XLA Modules:
  0.0 146.2 jit_solution(11210980098296007015)
XLA Ops:
  0.6 2.1 %shard_map.160 = bf16[256,2,384]{2,1,0:T(2,128)(2,1)} custom-call(bf16[16,16,384]{2,1,0:T(8,128)(2,1)} %latent_ref.1, bf16[16,16,384]{2,1,0:T(8,128)(2,1)} %cot_ref.1), custom_call_target="tpu_custom_call" | custom-call | tf_op jit(solution)/shard_map/pallas_call | solution.py:297
  2.7 15.7 %all-to-all-start = ((bf16[256,2,384]{2,1,0:T(2,128)(2,1)}), bf16[256,2,384]{2,1,0:T(2,128)(2,1)S(1)}, u32[]{:S(2)}, u32[]{:S(2)}) async-start(bf16[256,2,384]{2,1,0:T(2,128)(2,1)} %shard_map.160), calls=%async_computation | async-start | bytes 786432 | tf_op jit(solution)/shard_map/all_to_all | solution.py:503
  18.4 1.7 %shard_map.161 = (f32[384]{0:T(512)S(1)}, bf16[384,1152]{1,0:T(8,128)(2,1)S(1)}, f32[6,7,7]{2,1,0:T(8,128)S(1)}, bf16[384,384]{1,0:T(8,128)(2,1)S(1)}, f32[384]{0:T(512)S(1)}, /*index=5*/bf16[384,1536]{1,0:T(8,128)(2,1)S(1)}) custom-call(f32[384]{0:T(512)} %refs_0_.1, bf16[384,1152]{1,0:T(8,128)(2,1)} %refs_1_.1, f32[6,7,7]{2,1,0:T(8,128)} %refs_2_.1, ...), custom_call_target="tpu_custom_call" | custom-call | tf_op jit(solution)/shard_map/pallas_call | solution.py:115
  20.1 16.1 %all-to-all-done.both_ref = bf16[256,2,384]{2,1,0:T(2,128)(2,1)S(1)} async-done(((bf16[256,2,384]{2,1,0:T(2,128)(2,1)}), bf16[256,2,384]{2,1,0:T(2,128)(2,1)S(1)}, u32[]{:S(2)}, u32[]{:S(2)}) %all-to-all-start) | async-done | bytes 393248 | tf_op jit(solution)/shard_map/all_to_all | solution.py:503
  36.2 9.5 %shard_map.162 = (bf16[16,496,128]{2,1,0:T(8,128)(2,1)S(1)}, bf16[16,496,128]{2,1,0:T(8,128)(2,1)S(1)}) custom-call(s32[1]{0:T(128)} %bitcast.core_ref, bf16[256,2,384]{2,1,0:T(2,128)(2,1)S(1)} %all-to-all-done.both_ref, f32[384]{0:T(512)S(1)} %get-tuple-element.32.gain_attn_ref, bf16[384,1152]{1,0:T(8,128)(2,1)S(1)} %get-tuple-element.33.w_qkv_ref, ...), custom_call_target="tpu_custom_call" | custom-call | tf_op jit(solution)/shard_map/pallas_call | solution.py:297
  45.8 1.4 collective-permute-start
  47.1 3.7 %collective-permute-done.arrived_ref = bf16[16,496,128]{2,1,0:T(8,128)(2,1)S(1)} collective-permute-done((bf16[16,496,128]{2,1,0:T(8,128)(2,1)S(1)}, bf16[16,496,128]{2,1,0:T(8,128)(2,1)S(1)}, u32[]{:S(2)}, u32[]{:S(2)}) %collective-permute-start) | collective-permute-done | bytes 2031648 | tf_op jit(solution)/shard_map/ppermute | solution.py:507
  50.8 0.4 shard_map.163
  51.3 32.0 %all_to_all.25.arrived_ref = bf16[16,544,128]{2,1,0:T(8,128)(2,1)S(1)} all-to-all(bf16[16,544,128]{2,1,0:T(8,128)(2,1)S(1)} %shard_map.163), channel_id=1, replica_groups=mesh['y_lo'=2,'core'=2,'y_hi'=2,'x'=4,'z'=8] {'y_lo','y_hi','x'}, dimensions={0} | all-to-all | bytes 4456448 | tf_op jit(solution)/shard_map/all_to_all | solution.py:503
  83.3 0.7 shard_map.164
  84.0 13.1 %all_to_all.26.arrived_ref.output_ref = bf16[8,160,128]{2,1,0:T(8,128)(2,1)S(1)} all-to-all(bf16[8,160,128]{2,1,0:T(8,128)(2,1)S(1)} %get-tuple-element.40), channel_id=1, replica_groups=mesh['y_lo'=2,'core'=2,'y_hi'=2,'x'=4,'z'=8] {'z'}, dimensions={0} | all-to-all | bytes 655360 | tf_op jit(solution)/shard_map/all_to_all | solution.py:503
  97.2 13.4 %all_to_all.27.arrived_ref.d_latent_ref = bf16[8,160,128]{2,1,0:T(8,128)(2,1)S(1)} all-to-all(bf16[8,160,128]{2,1,0:T(8,128)(2,1)S(1)} %shard_map.165), channel_id=1, replica_groups=mesh['y_lo'=2,'core'=2,'y_hi'=2,'x'=4,'z'=8] {'z'}, dimensions={0} | all-to-all | bytes 655360 | tf_op jit(solution)/shard_map/all_to_all | solution.py:503
  110.6 0.3 shard_map.166
  110.9 24.0 %all_to_all.28.here_ref = bf16[16,448,128]{2,1,0:T(8,128)(2,1)S(1)} all-to-all(bf16[16,448,128]{2,1,0:T(8,128)(2,1)S(1)} %shard_map.166), channel_id=1, replica_groups=mesh['y_lo'=2,'core'=2,'y_hi'=2,'x'=4,'z'=8] {'y_lo','y_hi','x'}, dimensions={0} | all-to-all | bytes 3670016 | tf_op jit(solution)/shard_map/all_to_all | solution.py:503
  134.9 5.6 %collective-permute-start.1 = (bf16[16,448,128]{2,1,0:T(8,128)(2,1)S(1)}, bf16[16,448,128]{2,1,0:T(8,128)(2,1)S(1)}, u32[]{:S(2)}, u32[]{:S(2)}) collective-permute-start(bf16[16,448,128]{2,1,0:T(8,128)(2,1)S(1)} %all_to_all.28.here_ref), channel_id=1, source_target_pairs={{0,64},{64,0},{1,65},{65,1},{2,66},{66,2},{3,67},{67,3},{4,68},{68... | collective-permute-start | bytes 5505032 | tf_op jit(solution)/shard_map/ppermute | solution.py:507
  140.5 2.9 %shard_map.167 = (f32[384,1152]{1,0:T(8,128)}, f32[384,384]{1,0:T(8,128)}, f32[384,1536]{1,0:T(8,128)}, f32[1536,384]{1,0:T(8,128)}, bf16[256,384]{1,0:T(8,128)(2,1)}, /*index=5*/bf16[256,384]{1,0:T(8,128)(2,1)}) custom-call(s32[1]{0:T(128)} %bitcast.core_ref, bf16[16,448,128]{2,1,0:T(8,128)(2,1)S(1)} %all_to_all.28.here_ref, ...), custom_call_target="tpu_custom_call" | custom-call | tf_op jit(solution)/shard_map/pallas_call | solution.py:481
  143.5 0.5 collective-permute-done.1.other_ref
  144.0 2.0 %shard_map.168 = (f32[384,1152]{1,0:T(8,128)}, f32[384,384]{1,0:T(8,128)}, f32[384,1536]{1,0:T(8,128)}, f32[1536,384]{1,0:T(8,128)}, f32[6,7,7]{2,1,0:T(8,128)}, /*index=5*/f32[384]{0:T(512)}, f32[384]{0:T(512)}) custom-call(s32[1]{0:T(128)} %bitcast.core_ref, ...), custom_call_target="tpu_custom_call", output_to_operand_aliasing={{0}: (3, {}), {1}: (4, {}), {2}: (5, {}), {3}: (6, {})} | custom-call | tf_op jit(solution)/shard_map/pallas_call | solution.py:489
  (1 shorter events, 0.0 us)
Async XLA Ops:
  2.7 33.5 %all-to-all-start = ((bf16[256,2,384]{2,1,0:T(2,128)(2,1)}), bf16[256,2,384]{2,1,0:T(2,128)(2,1)S(1)}, u32[]{:S(2)}, u32[]{:S(2)}) async-start(bf16[256,2,384]{2,1,0:T(2,128)(2,1)} %shard_map.160), calls=%async_computation | async-start | bytes 786432 | tf_op jit(solution)/shard_map/all_to_all | solution.py:503
  45.8 5.1 %collective-permute-start = (bf16[16,496,128]{2,1,0:T(8,128)(2,1)S(1)}, bf16[16,496,128]{2,1,0:T(8,128)(2,1)S(1)}, u32[]{:S(2)}, u32[]{:S(2)}) collective-permute-start(bf16[16,496,128]{2,1,0:T(8,128)(2,1)S(1)} %get-tuple-element.39), channel_id=1, source_target_pairs={{0,64},{64,0},{1,65},{65,1},{2,66},{66,2},{3,67},{67,3},{4,68},{68... | collective-permute-start | bytes 6094856 | tf_op jit(solution)/shard_map/ppermute | solution.py:507
  134.9 9.0 %collective-permute-start.1 = (bf16[16,448,128]{2,1,0:T(8,128)(2,1)S(1)}, bf16[16,448,128]{2,1,0:T(8,128)(2,1)S(1)}, u32[]{:S(2)}, u32[]{:S(2)}) collective-permute-start(bf16[16,448,128]{2,1,0:T(8,128)(2,1)S(1)} %all_to_all.28.here_ref), channel_id=1, source_target_pairs={{0,64},{64,0},{1,65},{65,1},{2,66},{66,2},{3,67},{67,3},{4,68},{68... | collective-permute-start | bytes 5505032 | tf_op jit(solution)/shard_map/ppermute | solution.py:507

commit v7 on v6

--- a/solution.py
+++ b/solution.py
@@ -127,7 +127,7 @@
 
 
 def block_kernel(core_ref, both_ref, gain_attn_ref, w_qkv_ref, bias_ref, w_out_ref, gain_mlp_ref, w_fc1_ref, w_fc2_far_ref,
-                 kept_ref, sent_ref, halves_ref, w_fc2_ref, sem):
+                 kept_ref, sent_ref, halves_ref, w_fc2_ref, sem, move_sems):
     w_fc2_copy = pltpu.make_async_copy(w_fc2_far_ref, w_fc2_ref, sem)
     w_fc2_copy.start()
     groups = [both_ref[start : start + 128].reshape(256, D) for start in range(0, CELLS, 128)]
@@ -210,6 +210,15 @@
     d_resid_b = d_resid.astype(bf16)
     d_out = dot_tn(mixed, d_resid_b)
     d_mixed = dot_nt(d_resid_b, w_out_ref[...]).astype(bf16)
+
+    core = core_ref[0]
+    done = pl.ds(0, QKV_AT)
+    moves = [
+        pltpu.make_async_copy(halves_ref.at[core, :, done, :], kept_ref.at[:, done, :], move_sems.at[0]),
+        pltpu.make_async_copy(halves_ref.at[1 - core, :, done, :], sent_ref.at[:, done, :], move_sems.at[1]),
+    ]
+    for move in moves:
+        move.start()
 
     d_queries, d_keys, d_values_ = [], [], []
     rel_rows = []
@@ -272,16 +281,18 @@
     halves_ref[0, 1:, SMALL_AT:GRADS, :] = jnp.zeros((PLACES - 1, GRADS - SMALL_AT, LANES), bf16)
     halves_ref[1, :, SMALL_AT:GRADS, :] = jnp.zeros((PLACES, GRADS - SMALL_AT, LANES), bf16)
     for band in range(BANDS):
-        y_lo, core = band // 2, band % 2
+        y_lo, home = band // 2, band % 2
         rows = slice(band * SECTORS, (band + 1) * SECTORS)
         for block in range(3):
             lanes = slice(block * LANES, (block + 1) * LANES)
             both = jnp.concatenate([a[rows, lanes].reshape(8, DEPTH, LANES) for a in (output, d_latent)], 1)
             at = GRADS + block * 16
-            halves_ref[core, y_lo * 8 : y_lo * 8 + 8, at : at + 16, :] = both.astype(bf16)
+            halves_ref[home, y_lo * 8 : y_lo * 8 + 8, at : at + 16, :] = both.astype(bf16)
     core = core_ref[0]
-    kept_ref[...] = halves_ref[core]
-    sent_ref[...] = halves_ref[1 - core]
+    kept_ref[:, QKV_AT:, :] = halves_ref[core, :, QKV_AT:, :]
+    sent_ref[:, QKV_AT:, :] = halves_ref[1 - core, :, QKV_AT:, :]
+    for move in moves:
+        move.wait()
 
 
 SCALAR = pl.BlockSpec(memory_space=pltpu.SMEM)
@@ -314,7 +325,8 @@
         interpret,
         room=32,
         scalars=1,
-        scratch=[pltpu.VMEM((2, *half), bf16), pltpu.VMEM(w_fc2.shape, bf16), pltpu.SemaphoreType.DMA],
+        scratch=[pltpu.VMEM((2, *half), bf16), pltpu.VMEM(w_fc2.shape, bf16), pltpu.SemaphoreType.DMA]
+        + [pltpu.SemaphoreType.DMA((2,))],
         loose=1,
     )
 

time: 146 us -> 147 us (level)
  no operation moved by 1% of the time
where the time goes in v7:
time: 147 us; the launch traced here: 146 us
  blocking collectives  82.5 us (56%)
  starting transfers between devices  22.6 us (15%)
  waiting for transfers between devices  20.3 us (14%)
  Pallas kernels  20 us (14%)
    all_to_all x4, blocking collectives, exchange(): return lax.all_to_all(value, axes, 0, 0)  82.5 us
    all_to_all x1, waiting for transfers between devices, exchange(): return lax.all_to_all(value, axes, 0, 0)  16.1 us
    all_to_all x1, starting transfers between devices, exchange(): return lax.all_to_all(value, axes, 0, 0)  15.7 us
    pallas_call x6, Pallas kernels, call(): pl.pallas_call(kernel, out_shape=shapes, in_specs=[SCALAR] * scalars + [W...  13.3 us
    ppermute x2, starting transfers between devices, to_sibling(): return lax.ppermute(value, 'core', [(0, 1), (1, 0)])  6.98 us
    ppermute x2, waiting for transfers between devices, to_sibling(): return lax.ppermute(value, 'core', [(0, 1), (1, 0)])  4.19 us
  transfers between devices with their start and end apart: 3, of which 3 were waited for; matrix products, arithmetic and copies ran while one was open for 0% of the time, Pallas kernels for 3%

profile of v7, /device:TPU:1, one launch (start us, length us, event | category | flops | bytes accessed | tf_op | source)
XLA Modules:
  0.0 146.3 jit_solution(8157088892252533742)
XLA Ops:
  0.6 2.1 %shard_map.160 = bf16[256,2,384]{2,1,0:T(2,128)(2,1)} custom-call(bf16[16,16,384]{2,1,0:T(8,128)(2,1)} %latent_ref.1, bf16[16,16,384]{2,1,0:T(8,128)(2,1)} %cot_ref.1), custom_call_target="tpu_custom_call" | custom-call | tf_op jit(solution)/shard_map/pallas_call | solution.py:308
  2.7 15.7 %all-to-all-start = ((bf16[256,2,384]{2,1,0:T(2,128)(2,1)}), bf16[256,2,384]{2,1,0:T(2,128)(2,1)S(1)}, u32[]{:S(2)}, u32[]{:S(2)}) async-start(bf16[256,2,384]{2,1,0:T(2,128)(2,1)} %shard_map.160), calls=%async_computation | async-start | bytes 786432 | tf_op jit(solution)/shard_map/all_to_all | solution.py:515
  18.4 1.7 %shard_map.161 = (f32[384]{0:T(512)S(1)}, bf16[384,1152]{1,0:T(8,128)(2,1)S(1)}, f32[6,7,7]{2,1,0:T(8,128)S(1)}, bf16[384,384]{1,0:T(8,128)(2,1)S(1)}, f32[384]{0:T(512)S(1)}, /*index=5*/bf16[384,1536]{1,0:T(8,128)(2,1)S(1)}) custom-call(f32[384]{0:T(512)} %refs_0_.1, bf16[384,1152]{1,0:T(8,128)(2,1)} %refs_1_.1, f32[6,7,7]{2,1,0:T(8,128)} %refs_2_.1, ...), custom_call_target="tpu_custom_call" | custom-call | tf_op jit(solution)/shard_map/pallas_call | solution.py:115
  20.1 16.1 %all-to-all-done.both_ref = bf16[256,2,384]{2,1,0:T(2,128)(2,1)S(1)} async-done(((bf16[256,2,384]{2,1,0:T(2,128)(2,1)}), bf16[256,2,384]{2,1,0:T(2,128)(2,1)S(1)}, u32[]{:S(2)}, u32[]{:S(2)}) %all-to-all-start) | async-done | bytes 393248 | tf_op jit(solution)/shard_map/all_to_all | solution.py:515
  36.2 9.7 %shard_map.162 = (bf16[16,496,128]{2,1,0:T(8,128)(2,1)S(1)}, bf16[16,496,128]{2,1,0:T(8,128)(2,1)S(1)}) custom-call(s32[1]{0:T(128)} %bitcast.core_ref, bf16[256,2,384]{2,1,0:T(2,128)(2,1)S(1)} %all-to-all-done.both_ref, f32[384]{0:T(512)S(1)} %get-tuple-element.32.gain_attn_ref, bf16[384,1152]{1,0:T(8,128)(2,1)S(1)} %get-tuple-element.33.w_qkv_ref, ...), custom_call_target="tpu_custom_call" | custom-call | tf_op jit(solution)/shard_map/pallas_call | solution.py:308
  45.9 1.4 collective-permute-start
  47.3 3.7 %collective-permute-done.arrived_ref = bf16[16,496,128]{2,1,0:T(8,128)(2,1)S(1)} collective-permute-done((bf16[16,496,128]{2,1,0:T(8,128)(2,1)S(1)}, bf16[16,496,128]{2,1,0:T(8,128)(2,1)S(1)}, u32[]{:S(2)}, u32[]{:S(2)}) %collective-permute-start) | collective-permute-done | bytes 2031648 | tf_op jit(solution)/shard_map/ppermute | solution.py:519
  51.0 0.4 shard_map.163
  51.4 32.0 %all_to_all.25.arrived_ref = bf16[16,544,128]{2,1,0:T(8,128)(2,1)S(1)} all-to-all(bf16[16,544,128]{2,1,0:T(8,128)(2,1)S(1)} %shard_map.163), channel_id=1, replica_groups=mesh['y_lo'=2,'core'=2,'y_hi'=2,'x'=4,'z'=8] {'y_lo','y_hi','x'}, dimensions={0} | all-to-all | bytes 4456448 | tf_op jit(solution)/shard_map/all_to_all | solution.py:515
  83.4 0.7 shard_map.164
  84.2 13.1 %all_to_all.26.arrived_ref.output_ref = bf16[8,160,128]{2,1,0:T(8,128)(2,1)S(1)} all-to-all(bf16[8,160,128]{2,1,0:T(8,128)(2,1)S(1)} %get-tuple-element.40), channel_id=1, replica_groups=mesh['y_lo'=2,'core'=2,'y_hi'=2,'x'=4,'z'=8] {'z'}, dimensions={0} | all-to-all | bytes 655360 | tf_op jit(solution)/shard_map/all_to_all | solution.py:515
  97.3 13.4 %all_to_all.27.arrived_ref.d_latent_ref = bf16[8,160,128]{2,1,0:T(8,128)(2,1)S(1)} all-to-all(bf16[8,160,128]{2,1,0:T(8,128)(2,1)S(1)} %shard_map.165), channel_id=1, replica_groups=mesh['y_lo'=2,'core'=2,'y_hi'=2,'x'=4,'z'=8] {'z'}, dimensions={0} | all-to-all | bytes 655360 | tf_op jit(solution)/shard_map/all_to_all | solution.py:515
  110.7 0.3 shard_map.166
  111.1 24.0 %all_to_all.28.here_ref = bf16[16,448,128]{2,1,0:T(8,128)(2,1)S(1)} all-to-all(bf16[16,448,128]{2,1,0:T(8,128)(2,1)S(1)} %shard_map.166), channel_id=1, replica_groups=mesh['y_lo'=2,'core'=2,'y_hi'=2,'x'=4,'z'=8] {'y_lo','y_hi','x'}, dimensions={0} | all-to-all | bytes 3670016 | tf_op jit(solution)/shard_map/all_to_all | solution.py:515
  135.1 5.6 %collective-permute-start.1 = (bf16[16,448,128]{2,1,0:T(8,128)(2,1)S(1)}, bf16[16,448,128]{2,1,0:T(8,128)(2,1)S(1)}, u32[]{:S(2)}, u32[]{:S(2)}) collective-permute-start(bf16[16,448,128]{2,1,0:T(8,128)(2,1)S(1)} %all_to_all.28.here_ref), channel_id=1, source_target_pairs={{0,64},{64,0},{1,65},{65,1},{2,66},{66,2},{3,67},{67,3},{4,68},{68... | collective-permute-start | bytes 5505032 | tf_op jit(solution)/shard_map/ppermute | solution.py:519
  140.7 2.9 %shard_map.167 = (f32[384,1152]{1,0:T(8,128)}, f32[384,384]{1,0:T(8,128)}, f32[384,1536]{1,0:T(8,128)}, f32[1536,384]{1,0:T(8,128)}, bf16[256,384]{1,0:T(8,128)(2,1)}, /*index=5*/bf16[256,384]{1,0:T(8,128)(2,1)}) custom-call(s32[1]{0:T(128)} %bitcast.core_ref, bf16[16,448,128]{2,1,0:T(8,128)(2,1)S(1)} %all_to_all.28.here_ref, ...), custom_call_target="tpu_custom_call" | custom-call | tf_op jit(solution)/shard_map/pallas_call | solution.py:493
  143.6 0.5 collective-permute-done.1.other_ref
  144.1 2.0 %shard_map.168 = (f32[384,1152]{1,0:T(8,128)}, f32[384,384]{1,0:T(8,128)}, f32[384,1536]{1,0:T(8,128)}, f32[1536,384]{1,0:T(8,128)}, f32[6,7,7]{2,1,0:T(8,128)}, /*index=5*/f32[384]{0:T(512)}, f32[384]{0:T(512)}) custom-call(s32[1]{0:T(128)} %bitcast.core_ref, ...), custom_call_target="tpu_custom_call", output_to_operand_aliasing={{0}: (3, {}), {1}: (4, {}), {2}: (5, {}), {3}: (6, {})} | custom-call | tf_op jit(solution)/shard_map/pallas_call | solution.py:501
  (1 shorter events, 0.0 us)
Async XLA Ops:
  2.7 33.5 %all-to-all-start = ((bf16[256,2,384]{2,1,0:T(2,128)(2,1)}), bf16[256,2,384]{2,1,0:T(2,128)(2,1)S(1)}, u32[]{:S(2)}, u32[]{:S(2)}) async-start(bf16[256,2,384]{2,1,0:T(2,128)(2,1)} %shard_map.160), calls=%async_computation | async-start | bytes 786432 | tf_op jit(solution)/shard_map/all_to_all | solution.py:515
  45.9 5.1 %collective-permute-start = (bf16[16,496,128]{2,1,0:T(8,128)(2,1)S(1)}, bf16[16,496,128]{2,1,0:T(8,128)(2,1)S(1)}, u32[]{:S(2)}, u32[]{:S(2)}) collective-permute-start(bf16[16,496,128]{2,1,0:T(8,128)(2,1)S(1)} %get-tuple-element.39), channel_id=1, source_target_pairs={{0,64},{64,0},{1,65},{65,1},{2,66},{66,2},{3,67},{67,3},{4,68},{68... | collective-permute-start | bytes 6094856 | tf_op jit(solution)/shard_map/ppermute | solution.py:519
  135.1 9.0 %collective-permute-start.1 = (bf16[16,448,128]{2,1,0:T(8,128)(2,1)S(1)}, bf16[16,448,128]{2,1,0:T(8,128)(2,1)S(1)}, u32[]{:S(2)}, u32[]{:S(2)}) collective-permute-start(bf16[16,448,128]{2,1,0:T(8,128)(2,1)S(1)} %all_to_all.28.here_ref), channel_id=1, source_target_pairs={{0,64},{64,0},{1,65},{65,1},{2,66},{66,2},{3,67},{67,3},{4,68},{68... | collective-permute-start | bytes 5505032 | tf_op jit(solution)/shard_map/ppermute | solution.py:519
